TPU v7x, 32 devices: a whole 2x2x4 slice. The times are simulated.
32 devices in a mesh: dp: 8 (over z, x), ctx: 4 (over y, core).
Axes of the slice: x: 2, y: 2, z: 4, core: 2. Of those that a mesh axis runs over, the one named last changes fastest.
Arguments:
- scan_input: bfloat16 [8, 512, 4096], P('dp', 'ctx'), may hold values from -6 to 6
- step_raw: bfloat16 [8, 512, 4096], P('dp', 'ctx'), may hold values from -3 to 11
- input_proj: float32 [8, 16, 512], P('dp', None, 'ctx'), may hold values from -6 to 6
- output_proj: float32 [8, 16, 512], P('dp', None, 'ctx'), may hold values from -6 to 6
- out_cotangent: bfloat16 [8, 512, 4096], P('dp', 'ctx'), may hold values from -6 to 6
- conv_weight: float32 [4, 4096], replicated, may hold values from -3 to 3
- conv_bias: float32 [4096], replicated, may hold values from -0.5 to 0.5
- step_bias: float32 [4096], replicated, may hold values from -9 to -1
- decay_log: float32 [16, 4096], replicated, may hold values from -2.5 to 2.8
- skip_weight: float32 [4096], replicated, may hold values from 0.5 to 1.5
Outputs:
- grad_input: bfloat16 [8, 512, 4096], P('dp', 'ctx')
- grad_input_proj: float32 [8, 16, 512], P('dp', None, 'ctx')
- grad_output_proj: float32 [8, 16, 512], P('dp', None, 'ctx')
- convolution_weight_gradient: float32 [4, 4096], replicated
- grad_conv_bias: float32 [4096], replicated
- step_bias_gradient: float32 [4096], replicated
- grad_decay_log: float32 [16, 4096], replicated
- grad_skip_weight: float32 [4096], replicated
All inputs are finite; a program needn't handle non-finite values.
Results may differ from a plain program's by a relative error of at most 0.009.
Values may be sent and summed in bfloat16 or wider, within the bound.
No kernel may reach another device: no remote copies, remote signals or barrier semaphores. Data moves between devices by JAX's collectives and lax.ppermute only.
A program may use at most 128 MiB of HBM per device.

v0:
```python
from functools import partial

import jax
import jax.numpy as jnp
from jax import lax
from jax.sharding import PartitionSpec as P


def from_behind(value, axis, steps):
    count = lax.axis_size(axis)
    leading, last = (max(0, -steps), min(count, count - steps))
    return lax.ppermute(value, axis, [(source, source + steps) for source in range(leading, last)])


def prefix(value, axis, join, neutral):
    place = lax.axis_index(axis)
    gathered = jax.tree.map(
        lambda a, kind: lax.all_gather(a.astype(kind), axis), value, (jnp.bfloat16, jnp.bfloat16)
    )
    state = jax.tree.map(lambda a, e: jnp.zeros_like(a) + jnp.asarray(e, a.dtype), value, neutral)

    def one(hop, state):
        return join(
            state,
            jax.tree.map(
                lambda a, own: lax.dynamic_index_in_dim(a, hop, 0, False).astype(own.dtype),
                gathered,
                value,
            ),
        )

    return lax.fori_loop(0, place, one, state)


def prefix_2(value, axis, join, neutral):
    count, mine = (lax.axis_size(axis), lax.axis_index(axis))
    pieces = jax.tree.map(lambda part: lax.all_gather(part, axis), value)
    pieces = jax.tree.map(lambda part: part[::-1], pieces)
    mine = count - 1 - mine
    running = jax.tree.map(
        lambda part, zero: jnp.full_like(part, 0) + jnp.asarray(zero, part.dtype), value, neutral
    )

    def hop(position, running):
        longer = join(running, jax.tree.map(lambda part: part[position], pieces))
        return jax.tree.map(lambda new, old: jnp.where(position < mine, new, old), longer, running)

    return lax.fori_loop(0, count - 1, hop, running)


def advance(carry_state, inputs, decay_rate):
    step_now, activation, b_col, c_col = inputs
    carry_state = (
        jnp.exp(step_now[None, :] * decay_rate) * carry_state
        + b_col[:, None] * (step_now * activation)[None, :]
    )
    return (carry_state, jnp.sum(c_col[:, None] * carry_state, axis=0))


def convolve(extended, conv_weight, conv_bias, length):
    running = conv_bias + conv_weight[0] * extended[0:length]
    for offset in range(1, conv_weight.shape[0]):
        running = running + conv_weight[offset] * extended[offset : offset + length]
    return jax.nn.silu(running)


def blocked_decay_sum(exponent, weights, columns, decay_rate):
    length = exponent.shape[0]
    blocks = length // 16
    parts = (
        exponent.reshape(blocks, 16, -1),
        weights.reshape(blocks, 16, -1),
        columns.reshape(blocks, 16, -1),
    )
    start_total = jnp.zeros((columns.shape[1], exponent.shape[1]), jnp.float32)

    def add_block(total, block_items):
        expo_rows, weight_rows, column_rows = block_items
        terms = (
            jnp.exp(decay_rate[None] * expo_rows[:, None, :])
            * column_rows[:, :, None]
            * weight_rows[:, None, :]
        )
        return (total + jnp.sum(terms, axis=0), None)

    total, _ = lax.scan(add_block, start_total, parts)
    return total


def local_end(step_size, activation, b_matrix, decay_rate):
    inclusive = jnp.cumsum(step_size[::-1], axis=0)[::-1]
    after = jnp.concatenate(
        [inclusive[1:], jnp.zeros((1, step_size.shape[1]), jnp.float32)], axis=0
    )
    return blocked_decay_sum(after, step_size * activation, b_matrix.T, decay_rate)


def local_adjoint(step_size, c_matrix, grad_out, decay_rate):
    upto = jnp.cumsum(step_size, axis=0)
    return blocked_decay_sum(upto, grad_out, c_matrix.T, decay_rate)


def run_document(
    extended,
    b_matrix,
    c_matrix,
    conv_weight,
    conv_bias,
    step_bias,
    decay_log,
    skip_weight,
    step_float,
    start_state,
):
    length = step_float.shape[0]
    blocks = length // 16
    activation = convolve(extended, conv_weight, conv_bias, length)
    step_size = jax.nn.softplus(step_float + step_bias)
    decay_rate = -jnp.exp(decay_log)
    inputs = (
        step_size.reshape(blocks, 16, -1),
        activation.reshape(blocks, 16, -1),
        b_matrix.T.reshape(blocks, 16, -1),
        c_matrix.T.reshape(blocks, 16, -1),
    )

    def block_scan(carry_state, block_inputs):
        steps_in, acts_in, b_rows, c_rows = block_inputs
        outputs = []
        for position in range(16):
            carry_state, output_row = advance(
                carry_state,
                (steps_in[position], acts_in[position], b_rows[position], c_rows[position]),
                decay_rate,
            )
            outputs.append(output_row)
        return (carry_state, jnp.stack(outputs))

    final_state, scanned = lax.scan(jax.checkpoint(block_scan), start_state, inputs)
    return (scanned.reshape(length, -1) + skip_weight * activation, final_state)


def combine_product(earlier, later):
    return (earlier[0] * later[0], later[0] * earlier[1] + later[1])


def per_device(
    scan_input,
    step_raw,
    input_proj,
    output_proj,
    out_cotangent,
    conv_weight,
    conv_bias,
    step_bias,
    decay_log,
    skip_weight,
):
    rim_width = conv_weight.shape[0] - 1
    length = scan_input.shape[1]
    rim_rows = from_behind(scan_input[:, length - rim_width :, :], "ctx", 1)
    extended = jnp.concatenate([rim_rows, scan_input], axis=1).astype(jnp.float32)
    step_float = step_raw.astype(jnp.float32)
    grad_out = out_cotangent.astype(jnp.float32)
    decay_rate = -jnp.exp(decay_log)
    step_size = jax.nn.softplus(step_float + step_bias)
    activation = jax.vmap(lambda ext_rows: convolve(ext_rows, conv_weight, conv_bias, length))(
        extended
    )
    end_states = jax.vmap(partial(local_end, decay_rate=decay_rate))(
        step_size, activation, input_proj
    )
    start_adjoints = jax.vmap(partial(local_adjoint, decay_rate=decay_rate))(
        step_size, output_proj, grad_out
    )
    step_totals = jnp.sum(step_size, axis=1)
    group_decay = jnp.exp(decay_rate[None] * step_totals[:, None, :])
    identity_pair = (jnp.ones_like(group_decay), jnp.zeros_like(end_states))
    _, state_in = prefix((group_decay, end_states), "ctx", combine_product, identity_pair)
    _, adjoint_in = prefix_2((group_decay, start_adjoints), "ctx", combine_product, identity_pair)

    def forward_all(
        ext_rows, b_matrix, c_matrix, weight_taps, bias_taps, bias_steps, log_rates, direct_weight
    ):
        mapped = jax.vmap(run_document, in_axes=(0, 0, 0, None, None, None, None, None, 0, 0))
        return mapped(
            ext_rows,
            b_matrix,
            c_matrix,
            weight_taps,
            bias_taps,
            bias_steps,
            log_rates,
            direct_weight,
            step_float,
            state_in,
        )

    _, pullback = jax.vjp(
        forward_all,
        extended,
        input_proj,
        output_proj,
        conv_weight,
        conv_bias,
        step_bias,
        decay_log,
        skip_weight,
    )
    gradients = pullback((grad_out, adjoint_in))
    grad_ext = gradients[0]
    from_next = from_behind(grad_ext[:, :rim_width, :].astype(jnp.bfloat16), "ctx", -1).astype(
        jnp.float32
    )
    grad_input = jnp.concatenate(
        [grad_ext[:, rim_width:length, :], grad_ext[:, length:, :] + from_next], axis=1
    ).astype(jnp.bfloat16)
    summed = lax.psum(
        (gradients[3], gradients[4], gradients[5], gradients[6], gradients[7]), ("dp", "ctx")
    )
    return (
        grad_input,
        gradients[1],
        gradients[2],
        summed[0],
        summed[1],
        summed[2],
        summed[3],
        summed[4],
    )


def solution(mesh):
    in_specs = (
        P("dp", "ctx", None),
        P("dp", "ctx", None),
        P("dp", None, "ctx"),
        P("dp", None, "ctx"),
        P("dp", "ctx", None),
        P(),
        P(),
        P(),
        P(),
        P(),
    )
    out_specs = (
        P("dp", "ctx", None),
        P("dp", None, "ctx"),
        P("dp", None, "ctx"),
        P(),
        P(),
        P(),
        P(),
        P(),
    )
    return jax.shard_map(
        per_device, mesh=mesh, in_specs=in_specs, out_specs=out_specs, check_vma=False
    )
```

profile of v0, /device:TPU:0, one launch (start us, length us, event | category | flops | bytes accessed | tf_op | source)
XLA Modules:
  0.0 543.6 jit_solution(10698882053574720558)
XLA Ops:
  8.1 2.4 collective-permute-start
  13.0 2.7 convert.19
  18.1 4.8 multiply_reduce_fusion.49
  22.9 3.4 fusion.59
  27.3 16.7 %rev.12 = f32[1,128,4096]{2,1,0:T(8,128)} reverse(f32[1,128,4096]{2,1,0:T(8,128)} %get-tuple-element.1199), dimensions={1} | reverse | bytes 4194304 | tf_op jit(solution)/shard_map/vmap()/rev | solution.py:91
  43.9 4.7 reduce_window_sum.17
  48.6 21.9 %while.88 = (s32[]{:T(128)}, f32[1,16,4096]{2,1,0:T(8,128)S(1)}, f32[16,4096]{1,0:T(8,128)S(1)}, f32[8,1,16,4096]{3,2,1,0:T(8,128)}, f32[8,1,16,16]{3,2,1,0:T(8,...) while((s32[]{:T(128)}, f32[1,16,4096]{2,1,0:T(8,128)S(1)}, f32[16,4096]{1,0:T(8,128)S(1)}, ...), condition=%wide.region_4.5_spmd.clone, body=%wide.region_2.4_spmd.clone.sunk | while | flops 4259843 | bytes 2886767 | solution.py:86
  70.5 10.2 %all-gather.2 = bf16[64,4096]{1,0:T(8,128)(2,1)} all-gather(bf16[16,4096]{1,0:T(8,128)(2,1)} %get-tuple-element.1019), channel_id=4, replica_groups=mesh['dp'=8,'ctx'=4] {'ctx'}, dimensions={0}, use_global_device_ids=true | all-gather | bytes 655360 | tf_op jit(solution)/shard_map/all_gather | solution.py:18
  80.7 4.7 reduce_window_sum.18
  85.4 16.8 %slice.934 = f32[1,127,4096]{2,1,0:T(8,128)} reverse(f32[1,127,4096]{2,1,0:T(8,128)} %bitcast.1401), dimensions={1} | reverse | bytes 4161536 | tf_op jit(solution)/shard_map/vmap()/slice | solution.py:93
  102.2 3.1 concatenate.26
  105.3 21.9 %while.90 = (s32[]{:T(128)}, f32[1,16,4096]{2,1,0:T(8,128)S(1)}, f32[16,4096]{1,0:T(8,128)S(1)}, f32[8,1,16,4096]{3,2,1,0:T(8,128)}, f32[8,1,16,16]{3,2,1,0:T(8,...) while((s32[]{:T(128)}, f32[1,16,4096]{2,1,0:T(8,128)S(1)}, ...), condition=%wide.region_10.11_spmd.clone, body=%wide.region_8.10_spmd.clone.sunk | while | flops 4259843 | bytes 2886767 | solution.py:86
  127.2 7.3 %all-gather.3 = bf16[4,16,4096]{2,1,0:T(8,128)(2,1)S(1)} all-gather(bf16[1,16,4096]{2,1,0:T(8,128)(2,1)S(1)} %convert_element_type.71), channel_id=5, replica_groups=mesh['dp'=8,'ctx'=4] {'ctx'}, dimensions={0}, use_global_device_ids=true | all-gather | bytes 655360 | tf_op jit(solution)/shard_map/all_gather | solution.py:18
  136.3 32.8 %while.87 = (s32[]{:T(128)}, f32[1,16,4096]{2,1,0:T(8,128)S(1)}, f32[8,1,16,4096]{3,2,1,0:T(8,128)}, f32[8,1,16,4096]{3,2,1,0:T(8,128)}, f32[1,16,4096]{2,1,0:T(...) while((s32[]{:T(128)}, f32[1,16,4096]{2,1,0:T(8,128)S(1)}, ...), condition=%wide.region_14.15_spmd, body=%wide.region_13.14_spmd.sunk | while | flops 4259842 | bytes 4183145 | solution.py:139
  171.4 2.4 reverse_bitcast_fusion
  173.8 3.8 while.89
  182.0 208.5 %while.91 = (s32[]{:T(128)}, f32[16,4096]{1,0:T(8,128)}, f32[1,16,4096]{2,1,0:T(8,128)S(1)}, f32[8,1,16,4096]{3,2,1,0:T(8,128)}, f32[8,1,16,4096]{3,2,1,0:T(8,12...) while((s32[]{:T(128)}, f32[16,4096]{1,0:T(8,128)}, ...), condition=%wide.region_80.81_spmd.clone, body=%wide.region_15.80_spmd.clone.sunk | while | flops 35462148 | bytes 28035160 | solution.py:139
  189.6 2.3 fusion.92
  193.0 2.8 fusion.93
  215.7 2.3 fusion.92
  219.1 2.8 fusion.93
  241.8 2.3 fusion.92
  245.2 2.8 fusion.93
  267.8 2.3 fusion.92
  271.2 2.8 fusion.93
  297.3 2.8 fusion.93
  323.3 2.8 fusion.93
  349.4 2.8 fusion.93
  375.5 2.8 fusion.93
  390.5 4.1 multiply_reduce_fusion.53
  404.3 43.7 %all-reduce.73 = (f32[4096]{0:T(1024)}, f32[4096]{0:T(1024)}, f32[4096]{0:T(1024)}) all-reduce(f32[4096]{0:T(1024)S(1)} %get-tuple-element.910, f32[4096]{0:T(1024)S(1)} %fusion.55, f32[4096]{0:T(1024)S(1)} %copy-done.53), channel_id=1, replica_groups=mesh['dp'=8,'ctx'=4] {'dp','ctx'}, use_global_device_ids=true, to_apply=%region_87.88 | all-reduce | flops 12288 | bytes 98304 | tf_op jit(solution)/shard_map/psum | solution.py:218
  450.0 83.9 %all-reduce.77.cloned.1.call-done = (f32[4,4096]{1,0:T(4,128)}, f32[16,4096]{1,0:T(8,128)}) async-done(((f32[4,4096]{1,0:T(4,128)}, f32[16,4096]{1,0:T(8,128)}), (f32[4,4096]{1,0:T(4,128)}, f32[16,4096]{1,0:T(8,128)})) %all-reduce.77.cloned.1.call-update) | async-done | bytes 327696 | tf_op jit(solution)/shard_map/psum | solution.py:218
  (946 shorter events, 282.0 us)
Async XLA Ops:
  7.2 8.6 %copy-start.55 = (f32[1,16,128]{2,1,0:T(8,128)S(1)}, f32[1,16,128]{2,1,0:T(8,128)}, u32[]{:S(2)}) copy-start(f32[1,16,128]{2,1,0:T(8,128)} %param.24) | copy-start | bytes 24580
  7.2 162.0 %all-gather.7.cloned.1.call-start = ((), (), s32[]{:S(2)}) async-start(), calls=%async_computation | async-start | bytes 1310720 | tf_op jit(solution)/shard_map/all_gather | solution.py:37
  8.1 8.4 %collective-permute-start = (bf16[1,3,4096]{2,1,0:T(4,128)(2,1)S(1)}, bf16[1,3,4096]{2,1,0:T(4,128)(2,1)S(1)}, u32[]{:S(2)}, u32[]{:S(2)}) collective-permute-start(bf16[1,3,4096]{2,1,0:T(4,128)(2,1)S(1)} %slice.936), channel_id=1, source_target_pairs={{0,1},{1,2},{2,3},{4,5},{5,6},{6,7},{8,9},{9,10},{10,11},{12,13},{... | collective-permute-start | bytes 73736 | tf_op jit(solution)/shard_map/ppermute | solution.py:12
  27.2 144.2 %all-gather.9.cloned.1.call-start = ((), (), s32[]{:S(2)}) async-start(), calls=%async_computation.1 | async-start | bytes 1310720 | tf_op jit(solution)/shard_map/all_gather | solution.py:37
  70.5 14.9 %copy-start.28 = (f32[1,16,4096]{2,1,0:T(8,128)}, f32[1,16,4096]{2,1,0:T(8,128)S(1)}, u32[]{:S(2)}) copy-start(f32[1,16,4096]{2,1,0:T(8,128)S(1)} %get-tuple-element.595) | copy-start | bytes 786436
  134.5 399.4 %all-reduce.77.cloned.1.call-start = ((), (), s32[]{:S(2)}) async-start(), calls=%async_computation.2 | async-start | bytes 655360 | tf_op jit(solution)/shard_map/psum | solution.py:218
  188.6 7.3 %copy-start.19 = (f32[1,1,4096]{2,1,0:T(1,128)S(1)}, f32[1,1,4096]{2,1,0:T(1,128)}, u32[]{:S(2)}) copy-start(f32[1,1,4096]{2,1,0:T(1,128)} %get-tuple-element.1802) | copy-start | bytes 49156 | tf_op jit(solution)/shard_map/transpose(jvp(vmap()))/while
  188.6 7.3 %copy-start.30 = (f32[1,1,4096]{2,1,0:T(1,128)S(1)}, f32[1,1,4096]{2,1,0:T(1,128)}, u32[]{:S(2)}) copy-start(f32[1,1,4096]{2,1,0:T(1,128)} %get-tuple-element.1814) | copy-start | bytes 49156 | tf_op jit(solution)/shard_map/transpose(jvp(vmap()))/while
  188.6 7.3 %copy-start.31 = (f32[1,1,4096]{2,1,0:T(1,128)S(1)}, f32[1,1,4096]{2,1,0:T(1,128)}, u32[]{:S(2)}) copy-start(f32[1,1,4096]{2,1,0:T(1,128)} %get-tuple-element.1805) | copy-start | bytes 49156 | tf_op jit(solution)/shard_map/transpose(jvp(vmap()))/while
  188.6 7.3 %copy-start.32 = (f32[1,1,4096]{2,1,0:T(1,128)S(1)}, f32[1,1,4096]{2,1,0:T(1,128)}, u32[]{:S(2)}) copy-start(f32[1,1,4096]{2,1,0:T(1,128)} %get-tuple-element.1808) | copy-start | bytes 49156 | tf_op jit(solution)/shard_map/transpose(jvp(vmap()))/while
  214.6 7.3 %copy-start.19 = (f32[1,1,4096]{2,1,0:T(1,128)S(1)}, f32[1,1,4096]{2,1,0:T(1,128)}, u32[]{:S(2)}) copy-start(f32[1,1,4096]{2,1,0:T(1,128)} %get-tuple-element.1802) | copy-start | bytes 49156 | tf_op jit(solution)/shard_map/transpose(jvp(vmap()))/while
  214.7 7.3 %copy-start.30 = (f32[1,1,4096]{2,1,0:T(1,128)S(1)}, f32[1,1,4096]{2,1,0:T(1,128)}, u32[]{:S(2)}) copy-start(f32[1,1,4096]{2,1,0:T(1,128)} %get-tuple-element.1814) | copy-start | bytes 49156 | tf_op jit(solution)/shard_map/transpose(jvp(vmap()))/while
  214.7 7.3 %copy-start.31 = (f32[1,1,4096]{2,1,0:T(1,128)S(1)}, f32[1,1,4096]{2,1,0:T(1,128)}, u32[]{:S(2)}) copy-start(f32[1,1,4096]{2,1,0:T(1,128)} %get-tuple-element.1805) | copy-start | bytes 49156 | tf_op jit(solution)/shard_map/transpose(jvp(vmap()))/while
  214.7 7.3 %copy-start.32 = (f32[1,1,4096]{2,1,0:T(1,128)S(1)}, f32[1,1,4096]{2,1,0:T(1,128)}, u32[]{:S(2)}) copy-start(f32[1,1,4096]{2,1,0:T(1,128)} %get-tuple-element.1808) | copy-start | bytes 49156 | tf_op jit(solution)/shard_map/transpose(jvp(vmap()))/while
  240.7 7.3 %copy-start.19 = (f32[1,1,4096]{2,1,0:T(1,128)S(1)}, f32[1,1,4096]{2,1,0:T(1,128)}, u32[]{:S(2)}) copy-start(f32[1,1,4096]{2,1,0:T(1,128)} %get-tuple-element.1802) | copy-start | bytes 49156 | tf_op jit(solution)/shard_map/transpose(jvp(vmap()))/while
  240.7 7.3 %copy-start.30 = (f32[1,1,4096]{2,1,0:T(1,128)S(1)}, f32[1,1,4096]{2,1,0:T(1,128)}, u32[]{:S(2)}) copy-start(f32[1,1,4096]{2,1,0:T(1,128)} %get-tuple-element.1814) | copy-start | bytes 49156 | tf_op jit(solution)/shard_map/transpose(jvp(vmap()))/while
  240.7 7.3 %copy-start.31 = (f32[1,1,4096]{2,1,0:T(1,128)S(1)}, f32[1,1,4096]{2,1,0:T(1,128)}, u32[]{:S(2)}) copy-start(f32[1,1,4096]{2,1,0:T(1,128)} %get-tuple-element.1805) | copy-start | bytes 49156 | tf_op jit(solution)/shard_map/transpose(jvp(vmap()))/while
  240.7 7.3 %copy-start.32 = (f32[1,1,4096]{2,1,0:T(1,128)S(1)}, f32[1,1,4096]{2,1,0:T(1,128)}, u32[]{:S(2)}) copy-start(f32[1,1,4096]{2,1,0:T(1,128)} %get-tuple-element.1808) | copy-start | bytes 49156 | tf_op jit(solution)/shard_map/transpose(jvp(vmap()))/while
  266.8 7.3 %copy-start.19 = (f32[1,1,4096]{2,1,0:T(1,128)S(1)}, f32[1,1,4096]{2,1,0:T(1,128)}, u32[]{:S(2)}) copy-start(f32[1,1,4096]{2,1,0:T(1,128)} %get-tuple-element.1802) | copy-start | bytes 49156 | tf_op jit(solution)/shard_map/transpose(jvp(vmap()))/while
  266.8 7.3 %copy-start.30 = (f32[1,1,4096]{2,1,0:T(1,128)S(1)}, f32[1,1,4096]{2,1,0:T(1,128)}, u32[]{:S(2)}) copy-start(f32[1,1,4096]{2,1,0:T(1,128)} %get-tuple-element.1814) | copy-start | bytes 49156 | tf_op jit(solution)/shard_map/transpose(jvp(vmap()))/while
  266.8 7.3 %copy-start.31 = (f32[1,1,4096]{2,1,0:T(1,128)S(1)}, f32[1,1,4096]{2,1,0:T(1,128)}, u32[]{:S(2)}) copy-start(f32[1,1,4096]{2,1,0:T(1,128)} %get-tuple-element.1805) | copy-start | bytes 49156 | tf_op jit(solution)/shard_map/transpose(jvp(vmap()))/while
  266.8 7.3 %copy-start.32 = (f32[1,1,4096]{2,1,0:T(1,128)S(1)}, f32[1,1,4096]{2,1,0:T(1,128)}, u32[]{:S(2)}) copy-start(f32[1,1,4096]{2,1,0:T(1,128)} %get-tuple-element.1808) | copy-start | bytes 49156 | tf_op jit(solution)/shard_map/transpose(jvp(vmap()))/while
  292.8 7.3 %copy-start.19 = (f32[1,1,4096]{2,1,0:T(1,128)S(1)}, f32[1,1,4096]{2,1,0:T(1,128)}, u32[]{:S(2)}) copy-start(f32[1,1,4096]{2,1,0:T(1,128)} %get-tuple-element.1802) | copy-start | bytes 49156 | tf_op jit(solution)/shard_map/transpose(jvp(vmap()))/while
  292.8 7.3 %copy-start.30 = (f32[1,1,4096]{2,1,0:T(1,128)S(1)}, f32[1,1,4096]{2,1,0:T(1,128)}, u32[]{:S(2)}) copy-start(f32[1,1,4096]{2,1,0:T(1,128)} %get-tuple-element.1814) | copy-start | bytes 49156 | tf_op jit(solution)/shard_map/transpose(jvp(vmap()))/while
  292.8 7.3 %copy-start.31 = (f32[1,1,4096]{2,1,0:T(1,128)S(1)}, f32[1,1,4096]{2,1,0:T(1,128)}, u32[]{:S(2)}) copy-start(f32[1,1,4096]{2,1,0:T(1,128)} %get-tuple-element.1805) | copy-start | bytes 49156 | tf_op jit(solution)/shard_map/transpose(jvp(vmap()))/while
  292.8 7.3 %copy-start.32 = (f32[1,1,4096]{2,1,0:T(1,128)S(1)}, f32[1,1,4096]{2,1,0:T(1,128)}, u32[]{:S(2)}) copy-start(f32[1,1,4096]{2,1,0:T(1,128)} %get-tuple-element.1808) | copy-start | bytes 49156 | tf_op jit(solution)/shard_map/transpose(jvp(vmap()))/while
  318.9 7.3 %copy-start.19 = (f32[1,1,4096]{2,1,0:T(1,128)S(1)}, f32[1,1,4096]{2,1,0:T(1,128)}, u32[]{:S(2)}) copy-start(f32[1,1,4096]{2,1,0:T(1,128)} %get-tuple-element.1802) | copy-start | bytes 49156 | tf_op jit(solution)/shard_map/transpose(jvp(vmap()))/while
  318.9 7.3 %copy-start.30 = (f32[1,1,4096]{2,1,0:T(1,128)S(1)}, f32[1,1,4096]{2,1,0:T(1,128)}, u32[]{:S(2)}) copy-start(f32[1,1,4096]{2,1,0:T(1,128)} %get-tuple-element.1814) | copy-start | bytes 49156 | tf_op jit(solution)/shard_map/transpose(jvp(vmap()))/while
  318.9 7.3 %copy-start.31 = (f32[1,1,4096]{2,1,0:T(1,128)S(1)}, f32[1,1,4096]{2,1,0:T(1,128)}, u32[]{:S(2)}) copy-start(f32[1,1,4096]{2,1,0:T(1,128)} %get-tuple-element.1805) | copy-start | bytes 49156 | tf_op jit(solution)/shard_map/transpose(jvp(vmap()))/while
  318.9 7.3 %copy-start.32 = (f32[1,1,4096]{2,1,0:T(1,128)S(1)}, f32[1,1,4096]{2,1,0:T(1,128)}, u32[]{:S(2)}) copy-start(f32[1,1,4096]{2,1,0:T(1,128)} %get-tuple-element.1808) | copy-start | bytes 49156 | tf_op jit(solution)/shard_map/transpose(jvp(vmap()))/while
  345.0 7.3 %copy-start.19 = (f32[1,1,4096]{2,1,0:T(1,128)S(1)}, f32[1,1,4096]{2,1,0:T(1,128)}, u32[]{:S(2)}) copy-start(f32[1,1,4096]{2,1,0:T(1,128)} %get-tuple-element.1802) | copy-start | bytes 49156 | tf_op jit(solution)/shard_map/transpose(jvp(vmap()))/while
  398.0 50.0 %collective-permute-start.1 = (bf16[1,3,4096]{2,1,0:T(4,128)(2,1)S(1)}, bf16[1,3,4096]{2,1,0:T(4,128)(2,1)S(1)}, u32[]{:S(2)}, u32[]{:S(2)}) collective-permute-start(bf16[1,3,4096]{2,1,0:T(4,128)(2,1)S(1)} %slice.1065), channel_id=1, source_target_pairs={{1,0},{2,1},{3,2},{5,4},{6,5},{7,6},{9,8},{10,9},{11,10},{13,12},{... | collective-permute-start | bytes 73736 | tf_op jit(solution)/shard_map/ppermute | solution.py:12
  (253 other events, 940.9 us)
Sparse Core Ops, SparseCore 0:
  27.3 19.2 all-gather.6
  134.7 19.9 all-gather.8
  404.4 129.4 all-reduce.76
where the time goes:
time: 551 us; the launch traced here: 544 us
  other arithmetic  195 us (35%)
  local copies, waits for them, and re-layouts  180 us (33%)
  waiting for transfers between devices  84 us (15%)
  blocking collectives  61.2 us (11%)
  between operations  14.2 us (3%)
    psum x1, waiting for transfers between devices, per_device(): lax.psum((gradients[3], gradients[4], gradients[5], gradients[6], gradien...  83.9 us
    squeeze x40, local copies, waits for them, and re-layouts, blocked_decay_sum(): total, _ = lax.scan(add_block, start_total, parts)  47.4 us
    psum x1, blocking collectives, per_device(): lax.psum((gradients[3], gradients[4], gradients[5], gradients[6], gradien...  43.7 us
    reduce_sum x32, other arithmetic, advance(): return (carry_state, jnp.sum(c_col[:, None] * carry_state, axis=0))  35.6 us
    reduce_sum x32, other arithmetic, advance(): step_now[None, :] * decay_rate  32 us
    mul x32, local copies, waits for them, and re-layouts, add_block(): jnp.exp(decay_rate[None] * expo_rows[:, None, :]) * column_rows[:, :, None]  28.4 us
    dynamic_update_slice x32, other arithmetic, run_document(): lax.scan(jax.checkpoint(block_scan), start_state, inputs)  26.9 us
    mul x48, other arithmetic, advance(): step_now * activation  18.9 us
  transfers between devices with their start and end apart: 5, of which 1 were waited for; matrix products, arithmetic and copies ran while one was open for 25% of the time, Pallas kernels for 0%

commit v1 on v0

v1 whole, which is shorter than its diff:
```python
import math

import jax
import jax.numpy as jnp
from jax import lax
from jax.experimental import pallas as pl
from jax.experimental.pallas import tpu as pltpu
from jax.sharding import PartitionSpec as P

F32 = jnp.float32
BF16 = jnp.bfloat16
LOG2E = 1.0 / math.log(2.0)
BLOCK = 16
LANES = 128
WIDTH = 512
VMEM = 60 * 1024 * 1024


def lane_slices(width):
    return [slice(j, j + LANES) for j in range(0, width, LANES)]


def row_of(ref, t, j):
    row = ref[j, pl.ds(t, 8, stride=0), :]
    return jnp.concatenate([row, row], axis=0)


def put(ref, rows, value):
    for j in range(ref.shape[0]):
        ref[j, rows, :] = value[:, j * LANES : (j + 1) * LANES]


def take(ref, rows):
    return jnp.concatenate([ref[j, rows, :] for j in range(ref.shape[0])], axis=1)


def joined_tiles(ref):
    return jnp.concatenate([ref[j] for j in range(ref.shape[0])], axis=1)


def row_sum(value):
    total = value[0:8]
    for r in range(8, value.shape[0], 8):
        total = total + value[r : r + 8]
    return total


def set_rates(dl_ref, rates):
    for j, s in enumerate(lane_slices(dl_ref.shape[1])):
        rates[j] = -jnp.exp(dl_ref[:, s]) * LOG2E


def ends_kernel(x_ref, rim_ref, step_ref, dy_ref, bb_ref, cm_ref, cw_ref, cb_ref, sb_ref, dl_ref,
                out_ref, dls, dus, dyf, u_ref, sig_ref, slope_ref, dub_ref, xe, xs, rates):
    length, width = x_ref.shape
    states = dl_ref.shape[0]
    taps = cw_ref.shape[0]
    blocks = length // BLOCK
    weights = [cw_ref[k : k + 1, :] for k in range(taps)]
    bias, shift = cb_ref[...], sb_ref[...]
    slices = lane_slices(width)
    set_rates(dl_ref, rates)
    xe[0:8, :] = jnp.zeros((8, width), F32)
    xe[8 - (taps - 1) : 8, :] = rim_ref[...].astype(F32)
    total = jnp.zeros((8, width), F32)
    for b in range(blocks):
        rows = slice(b * BLOCK, (b + 1) * BLOCK)
        xe[8 + b * BLOCK : 8 + (b + 1) * BLOCK, :] = x_ref[rows, :].astype(F32)
        put(dyf, rows, dy_ref[rows, :].astype(F32))
        z = jnp.exp(step_ref[rows, :].astype(F32) + shift)
        series = z * (1.0 - z * (0.5 - z * (1.0 / 3.0 - 0.25 * z)))
        delta = jnp.where(z < 0.015625, series, jnp.log(1.0 + z))
        p = bias
        for k in range(taps):
            first = b * BLOCK + 9 - taps + k
            p = p + weights[k] * xe[first : first + BLOCK, :]
        gate = 1.0 / (1.0 + jnp.exp(-p))
        u = p * gate
        du = delta * u
        put(dls, rows, delta)
        put(dus, rows, du)
        u_ref[rows, :] = u
        sig_ref[rows, :] = z / (1.0 + z)
        slope_ref[rows, :] = gate + u * (1.0 - gate)
        dub_ref[rows, :] = du.astype(BF16)
        total = total + row_sum(delta)
    total = jnp.sum(total, axis=0, keepdims=True)

    def block(b, carry):
        state, decay, adjoint = carry
        state, decay = list(state), list(decay)
        base = pl.multiple_of(b * BLOCK, BLOCK)
        for i in range(BLOCK):
            t = base + i
            column = bb_ref[pl.ds(pl.multiple_of(t * states, states), states), :]
            for j in range(len(slices)):
                a = jnp.exp2(row_of(dls, t, j) * rates[j])
                state[j] = a * state[j] + column * row_of(dus, t, j)
                decay[j] = decay[j] * a
                xs[j, i * states : (i + 1) * states, :] = (decay[j] * row_of(dyf, t, j)).astype(BF16)
        adjoint = adjoint + jnp.dot(
            cm_ref[pl.ds(pl.multiple_of(b * states, states), states), :], joined_tiles(xs),
            preferred_element_type=F32)
        return tuple(state), tuple(decay), adjoint

    zero = tuple(jnp.zeros((states, LANES), F32) for _ in slices)
    one = tuple(jnp.ones((states, LANES), F32) for _ in slices)
    state, _, adjoint = lax.fori_loop(0, blocks, block, (zero, one, jnp.zeros((states, width), F32)))
    for j, s in enumerate(slices):
        out_ref[0:states, s] = state[j].astype(BF16)
    out_ref[states : 2 * states, :] = adjoint.astype(BF16)
    high = total.astype(BF16)
    rest = total - high.astype(F32)
    middle = rest.astype(BF16)
    low = (rest - middle.astype(F32)).astype(BF16)
    row = lax.broadcasted_iota(jnp.int32, (16, width), 0)
    packed = jnp.where(row == 0, high.astype(F32), jnp.where(row == 1, middle.astype(F32), low.astype(F32)))
    out_ref[2 * states : 2 * states + 16, :] = packed.astype(BF16)


def main_kernel(si_ref, ai_ref, x_ref, rim_ref, dy_ref, dls, dus, dyf, u_ref, sig_ref, slope_ref, dub_ref,
                bb_ref, cb2_ref, bd_ref, cw_ref, dl_ref, sk_ref,
                gin_ref, borrow_ref, tail_ref, gb_ref, gc_ref, pg_ref,
                xe, ahs, hb, dpe, acc, rates, naturals):
    length, width = x_ref.shape
    states = dl_ref.shape[0]
    taps = cw_ref.shape[0]
    blocks = length // BLOCK
    slices = lane_slices(width)
    pairs = [slices[j : j + 2] for j in range(0, len(slices), 2)]

    @pl.when(pl.program_id(0) == 0)
    def _():
        gb_ref[...] = jnp.zeros_like(gb_ref)
        gc_ref[...] = jnp.zeros_like(gc_ref)

    set_rates(dl_ref, rates)
    for j, s in enumerate(slices):
        naturals[j] = (-jnp.exp(dl_ref[:, s])).astype(BF16)
    lane = lax.broadcasted_iota(jnp.int32, (states, length), 1)

    def forward(b, carry):
        state, gc = carry
        state = list(state)
        base = pl.multiple_of(b * BLOCK, BLOCK)
        for i in range(BLOCK):
            t = base + i
            rows = pl.ds(pl.multiple_of(t * states, states), states)
            column = bb_ref[rows, :]
            for j in range(len(slices)):
                a = jnp.exp2(row_of(dls, t, j) * rates[j])
                kept = a * state[j]
                ahs[j, rows, :] = kept.astype(BF16)
                state[j] = kept + column * row_of(dus, t, j)
                hb[j, i * states : (i + 1) * states, :] = state[j].astype(BF16)
        product = lax.dot_general(joined_tiles(hb), dy_ref[...], (((1,), (1,)), ((), ())),
                                  preferred_element_type=F32)
        for i in range(BLOCK):
            gc = jnp.where(lane == base + i, product[i * states : (i + 1) * states], gc)
        return tuple(state), gc

    nothing = jnp.zeros((states, length), F32)
    _, gc = lax.fori_loop(0, blocks, forward, (tuple(si_ref[:, s] for s in slices), nothing))
    gc_ref[...] += gc

    acc[...] = jnp.zeros_like(acc)
    dpe[0:8, :] = jnp.zeros((8, width), F32)
    dpe[length + 8 : length + 16, :] = jnp.zeros((8, width), F32)
    rows_of = lax.broadcasted_iota(jnp.int32, (BLOCK, BLOCK * states), 0)
    cols_of = lax.broadcasted_iota(jnp.int32, (BLOCK, BLOCK * states), 1)
    over_states = jnp.where(rows_of == cols_of // states, 1.0, 0.0).astype(BF16)
    rows_of = lax.broadcasted_iota(jnp.int32, (states, BLOCK * states), 0)
    cols_of = lax.broadcasted_iota(jnp.int32, (states, BLOCK * states), 1)
    over_steps = jnp.where(rows_of == cols_of % states, 1.0, 0.0).astype(BF16)

    def backward(n, carry):
        adjoint, gb, rates_sum = carry
        adjoint, rates_sum = list(adjoint), list(rates_sum)
        b = blocks - 1 - n
        base = pl.multiple_of(b * BLOCK, BLOCK)
        kept = {}
        for i in reversed(range(BLOCK)):
            t = base + i
            rows = pl.ds(pl.multiple_of(t * states, states), states)
            column = cb2_ref[rows, :]
            for j in range(len(slices)):
                delta = row_of(dls, t, j)
                g = column * row_of(dyf, t, j) + adjoint[j]
                adjoint[j] = jnp.exp2(delta * rates[j]) * g
                low = g.astype(BF16)
                q = low * ahs[j, rows, :]
                kept[i, j] = low, q * naturals[j], q * delta.astype(BF16)

        def operand(pair, which):
            return jnp.concatenate(
                [jnp.concatenate([kept[i, j][which] for i in range(BLOCK)], axis=0) for j in pair], axis=1)

        ddu, dwn, product = [], [], None
        for m in range(len(pairs)):
            pair = (2 * m, 2 * m + 1)
            g_block = operand(pair, 0)
            ddu.append(jnp.dot(bd_ref[pl.ds(base, BLOCK), :], g_block, preferred_element_type=F32))
            dwn.append(jnp.dot(over_states, operand(pair, 1), preferred_element_type=F32))
            rates_sum[m] = rates_sum[m] + jnp.dot(over_steps, operand(pair, 2), preferred_element_type=F32)
            part = lax.dot_general(g_block, dub_ref[:, 2 * m * LANES : 2 * (m + 1) * LANES],
                                   (((1,), (1,)), ((), ())), preferred_element_type=F32)
            product = part if product is None else product + part
        for i in range(BLOCK):
            gb = jnp.where(lane == base + i, product[i * states : (i + 1) * states], gb)
        rows = pl.ds(base, BLOCK)
        ddu, dwn = jnp.concatenate(ddu, axis=1), jnp.concatenate(dwn, axis=1)
        dy, u = take(dyf, rows), u_ref[rows, :]
        grad_v = (ddu * u + dwn) * sig_ref[rows, :]
        grad_p = (ddu * take(dls, rows) + sk_ref[...] * dy) * slope_ref[rows, :]
        dpe[pl.ds(pl.multiple_of(base + 8, 8), BLOCK), :] = grad_p
        acc[taps] += row_sum(grad_p)
        acc[taps + 1] += row_sum(grad_v)
        acc[taps + 2] += row_sum(dy * u)
        return tuple(adjoint), gb, tuple(rates_sum)

    start = (tuple(ai_ref[:, s] for s in slices), nothing,
             tuple(jnp.zeros((states, 2 * LANES), F32) for _ in pairs))
    _, gb, rates_sum = lax.fori_loop(0, blocks, backward, start)
    gb_ref[...] += gb
    rates_sum = jnp.concatenate(rates_sum, axis=1)
    for j, s in enumerate(slices):
        pg_ref[0:states, s] = rates_sum[:, s] * (-jnp.exp(dl_ref[:, s]))

    weights = [cw_ref[k : k + 1, :] for k in range(taps)]
    xe[0:8, :] = jnp.zeros((8, width), F32)
    xe[8 - (taps - 1) : 8, :] = rim_ref[...].astype(F32)
    sums = [jnp.zeros((8, width), F32) for _ in range(taps)]
    for b in range(blocks):
        rows = slice(b * BLOCK, (b + 1) * BLOCK)
        xe[8 + b * BLOCK : 8 + (b + 1) * BLOCK, :] = x_ref[rows, :].astype(F32)
        grad_p = dpe[8 + b * BLOCK : 8 + (b + 1) * BLOCK, :]
        grad_x = weights[taps - 1] * grad_p
        for k in range(taps):
            first = b * BLOCK + 9 - taps + k
            sums[k] = sums[k] + row_sum(grad_p * xe[first : first + BLOCK, :])
            if k < taps - 1:
                first = b * BLOCK + 7 + taps - k
                grad_x = grad_x + weights[k] * dpe[first : first + BLOCK, :]
        gin_ref[rows, :] = grad_x.astype(BF16)
        if b == blocks - 1:
            tail_ref[...] = grad_x
    grad_rim = weights[0] * dpe[taps - 1 : taps + 7, :]
    for k in range(1, taps):
        grad_rim = grad_rim + weights[k] * dpe[taps - 1 - k : taps + 7 - k, :]
    borrow_ref[...] = grad_rim[8 - borrow_ref.shape[0] : 8].astype(BF16)
    small = [jnp.sum(a, axis=0, keepdims=True) for a in sums]
    small += [jnp.sum(acc[taps + k], axis=0, keepdims=True) for k in range(3)]
    row = lax.broadcasted_iota(jnp.int32, (8, width), 0)
    packed = jnp.zeros((8, width), F32)
    for k in range(taps + 3):
        packed = jnp.where(row == k, small[k], packed)
    pg_ref[states : states + 8, :] = packed


def flipped(value, axis, bit):
    return lax.ppermute(value, axis, [(k, k ^ bit) for k in range(lax.axis_size(axis))])


def add_up(value):
    inner, outer = lax.axis_size("ctx"), lax.axis_size("dp")
    if inner & (inner - 1) or outer & (outer - 1):
        return lax.psum(value, ("dp", "ctx"))
    me = lax.axis_index("ctx")
    bits = [1 << k for k in range(inner.bit_length() - 1)]
    for bit in bits:
        half = value.shape[1] // 2
        upper = (me // bit) % 2
        give = lax.dynamic_slice_in_dim(value, (1 - upper) * half, half, 1)
        got = flipped(give, "ctx", bit)
        value = lax.dynamic_slice_in_dim(value, upper * half, half, 1) + got
    for k in range(outer.bit_length() - 1):
        value = value + flipped(value, "dp", 1 << k)
    for bit in reversed(bits):
        got = flipped(value, "ctx", bit)
        upper = (me // bit) % 2 == 1
        value = jnp.concatenate([jnp.where(upper, got, value), jnp.where(upper, value, got)], axis=1)
    return value


def entering(ends, decay_log):
    states = decay_log.shape[0]
    count, place = lax.axis_size("ctx"), lax.axis_index("ctx")
    rate = -jnp.exp(decay_log)

    def opened(piece):
        total = jnp.sum(piece[2 * states : 2 * states + 3].astype(F32), axis=0, keepdims=True)
        return piece[:states].astype(F32), piece[states : 2 * states].astype(F32), jnp.exp(rate * total)

    if count == 4:
        upper, late = place % 2 == 1, place // 2 == 1
        mine, other = opened(ends), opened(flipped(ends, "ctx", 1))
        pick = lambda a, b: jnp.where(upper, a, b)
        first, second = [pick(b, a) for a, b in zip(mine, other)], [pick(a, b) for a, b in zip(mine, other)]
        both = jnp.where(late, second[1] * first[2] + first[1], first[0] * second[2] + second[0])
        got = flipped(both.astype(BF16), "ctx", 2).astype(F32)
        before, after = jnp.where(late, got, 0.0), jnp.where(late, 0.0, got)
        state = jnp.where(upper, before * first[2] + first[0], before)
        adjoint = jnp.where(upper, after, after * second[2] + second[1])
        return state, adjoint
    gathered = lax.all_gather(ends, "ctx")
    state = adjoint = jnp.zeros(decay_log.shape, F32)
    for k in range(count - 1):
        end, _, decay = opened(gathered[k])
        state = jnp.where(k < place, decay * state + end, state)
    for k in range(count - 1, 0, -1):
        _, end, decay = opened(gathered[k])
        adjoint = jnp.where(k > place, decay * adjoint + end, adjoint)
    return state, adjoint


def per_device(scan_input, step_raw, input_proj, output_proj, out_cotangent, conv_weight, conv_bias, step_bias,
               decay_log, skip_weight):
    documents, length, channels = scan_input.shape
    states, taps = decay_log.shape[0], conv_weight.shape[0]
    rim = taps - 1
    blocks = length // BLOCK
    count = lax.axis_size("ctx")
    forth = [(k, k + 1) for k in range(count - 1)]
    back = [(k + 1, k) for k in range(count - 1)]
    flat = lambda a: a.reshape(1, channels)
    tiles = WIDTH // LANES
    work = length * states * channels

    def whole(a):
        return pl.BlockSpec(a.shape, lambda i: (0,) * a.ndim)

    def chunk(rows):
        return pl.BlockSpec((rows, WIDTH), lambda i: (0, i))

    tiled = pl.BlockSpec((tiles, length, LANES), lambda i: (i, 0, 0))
    summed = pl.BlockSpec((states, length), lambda i: (0, 0))
    params = pltpu.CompilerParams(vmem_limit_bytes=VMEM, dimension_semantics=("arbitrary",))
    shape = jax.ShapeDtypeStruct

    def one(x, step, b_proj, c_proj, dy):
        rims = lax.ppermute(x[length - rim :, :], "ctx", forth)
        b_rows, c_rows = b_proj.T, c_proj.T
        b_wide = jnp.broadcast_to(b_rows.reshape(length * states, 1), (length * states, LANES))
        c_wide = jnp.broadcast_to(c_rows.reshape(length * states, 1), (length * states, LANES))
        steps_eye, states_eye = jnp.eye(BLOCK, dtype=F32), jnp.eye(states, dtype=F32)
        b_diag = (b_rows.reshape(blocks, 1, BLOCK, states) * steps_eye[None, :, :, None]).reshape(
            length, BLOCK * states).astype(BF16)
        c_diag = (c_rows.reshape(blocks, 1, BLOCK, states) * states_eye[None, :, None, :]).reshape(
            blocks * states, BLOCK * states).astype(BF16)
        long = shape((channels // LANES, length, LANES), F32)
        plain = shape((length, channels), F32)
        ends, *saved = pl.pallas_call(
            ends_kernel,
            grid=(channels // WIDTH,),
            in_specs=[chunk(length), chunk(rim), chunk(length), chunk(length), whole(b_wide), whole(c_diag),
                      chunk(taps), chunk(1), chunk(1), chunk(states)],
            out_specs=[chunk(2 * states + 16)] + [tiled] * 3 + [chunk(length)] * 4,
            out_shape=[shape((2 * states + 16, channels), BF16), long, long, long, plain, plain, plain,
                       shape((length, channels), BF16)],
            scratch_shapes=[pltpu.VMEM((length + 16, WIDTH), F32),
                            pltpu.VMEM((tiles, BLOCK * states, LANES), BF16),
                            pltpu.VMEM((tiles, states, LANES), F32)],
            compiler_params=params,
            cost_estimate=pl.CostEstimate(flops=8 * work, bytes_accessed=20 * length * channels, transcendentals=work),
        )(x, rims, step, dy, b_wide, c_diag, conv_weight, flat(conv_bias), flat(step_bias), decay_log)
        state_in, adjoint_in = entering(ends, decay_log)
        return pl.pallas_call(
            main_kernel,
            grid=(channels // WIDTH,),
            in_specs=[chunk(states), chunk(states), chunk(length), chunk(rim), chunk(length)] + [tiled] * 3
            + [chunk(length)] * 4 + [whole(b_wide), whole(c_wide), whole(b_diag), chunk(taps), chunk(states), chunk(1)],
            out_specs=[chunk(length), chunk(rim), chunk(BLOCK), summed, summed, chunk(states + 8)],
            out_shape=[shape((length, channels), BF16), shape((rim, channels), BF16), shape((BLOCK, channels), F32),
                       shape((states, length), F32), shape((states, length), F32),
                       shape((states + 8, channels), F32)],
            scratch_shapes=[pltpu.VMEM((length + 16, WIDTH), F32),
                            pltpu.VMEM((tiles, length * states, LANES), BF16),
                            pltpu.VMEM((tiles, BLOCK * states, LANES), BF16),
                            pltpu.VMEM((length + 16, WIDTH), F32),
                            pltpu.VMEM((taps + 3, 8, WIDTH), F32),
                            pltpu.VMEM((tiles, states, LANES), F32),
                            pltpu.VMEM((tiles, states, LANES), BF16)],
            compiler_params=params,
            cost_estimate=pl.CostEstimate(flops=20 * work, bytes_accessed=24 * length * channels, transcendentals=2 * work),
        )(state_in, adjoint_in, x, rims, dy, *saved, b_wide, c_wide, b_diag, conv_weight, decay_log,
          flat(skip_weight))

    outs = []
    for d in range(documents):
        gin, borrow, tail, gb, gc, sums = one(
            scan_input[d], step_raw[d], input_proj[d], output_proj[d], out_cotangent[d])
        given = lax.ppermute(borrow, "ctx", back).astype(F32)
        tail = (tail + jnp.pad(given, ((BLOCK - rim, 0), (0, 0)))).astype(BF16)
        gin = lax.dynamic_update_slice(gin, tail, (length - BLOCK, 0))
        outs.append((gin, gb, gc, sums))
    sums = add_up(sum(o[3] for o in outs))
    return (
        jnp.stack([o[0] for o in outs]),
        jnp.stack([o[1] for o in outs]),
        jnp.stack([o[2] for o in outs]),
        sums[states : states + taps],
        sums[states + taps],
        sums[states + taps + 1],
        sums[:states],
        sums[states + taps + 2],
    )


def solution(mesh):
    split, columns = P("dp", "ctx", None), P("dp", None, "ctx")
    return jax.shard_map(
        per_device,
        mesh=mesh,
        in_specs=(split, split, columns, columns, split, P(), P(), P(), P(), P()),
        out_specs=(split, columns, columns, P(), P(), P(), P(), P()),
        check_vma=False,
    )
```

time: 551 us -> 136 us (0.25); the launches traced: 544 us -> 136 us
  other arithmetic: 195 us -> 8.09 us
  local copies, waits for them, and re-layouts: 180 us -> 8.52 us
  Pallas kernels: 0 us -> 80.1 us
  blocking collectives: 61.2 us -> 0 us
  waiting for transfers between devices: 84 us -> 24.2 us
  between operations: 14.2 us -> 0.83 us
  starting transfers between devices: 3.95 us -> 14.2 us
    reduce_sum x83 -> x2, other arithmetic: 91.9 us -> 0.92 us  [opened(): jnp.sum(piece[2 * states:2 * states + 3].astype(F32), axis=0, keepdims=True)]
    psum x1 -> x0, waiting for transfers between devices: 83.9 us -> none  [per_device(): lax.psum((gradients[3], gradients[4], gradients[5], gradients[6], gradien...]
    pallas_call x0 -> x2, Pallas kernels: none -> 80.1 us  [the longest x1 52.8 us: one(): pl.pallas_call(main_kernel, grid=(channels // WIDTH,), in_specs=[chunk(st...]
    squeeze x40 -> x0, local copies, waits for them, and re-layouts: 47.4 us -> none  [blocked_decay_sum(): total, _ = lax.scan(add_block, start_total, parts)]
    psum x1 -> x0, blocking collectives: 43.7 us -> none  [per_device(): lax.psum((gradients[3], gradients[4], gradients[5], gradients[6], gradien...]
    mul x56 -> x1, local copies, waits for them, and re-layouts: 44.4 us -> 0.8 us  [one(): c_rows.reshape(blocks, 1, BLOCK, states) * states_eye[None, :, None, :]]
    dynamic_update_slice x32 -> x1, other arithmetic: 26.9 us -> 0.69 us  [per_device(): gin = lax.dynamic_update_slice(gin, tail, (length - BLOCK, 0))]
    slice x21 -> x1, local copies, waits for them, and re-layouts: 26 us -> 0.86 us  [one(): rims = lax.ppermute(x[length - rim:, :], 'ctx', forth)]
  transfers between devices with their start and end apart: 5 -> 11, of which waited for: 1 -> 9; matrix products, arithmetic and copies ran while one was open for 25% -> 4% of each run, Pallas kernels for 0% -> 0%
where the time goes in v1:
time: 136 us
  Pallas kernels  80.1 us (59%)
  waiting for transfers between devices  24.2 us (18%)
  starting transfers between devices  14.2 us (10%)
  local copies, waits for them, and re-layouts  8.52 us (6%)
  other arithmetic  8.09 us (6%)
    pallas_call x1, Pallas kernels, one(): pl.pallas_call(main_kernel, grid=(channels // WIDTH,), in_specs=[chunk(st...  52.8 us
    pallas_call x1, Pallas kernels, one(): pl.pallas_call(ends_kernel, grid=(channels // WIDTH,), in_specs=[chunk(le...  27.3 us
    ppermute x9, waiting for transfers between devices, flipped(): lax.ppermute(value, axis, [(k, k ^ bit) for k in range(lax.axis_size(axis...  24.2 us
    ppermute x9, starting transfers between devices, flipped(): lax.ppermute(value, axis, [(k, k ^ bit) for k in range(lax.axis_size(axis...  10.5 us
  transfers between devices with their start and end apart: 11, of which 9 were waited for; matrix products, arithmetic and copies ran while one was open for 4% of the time, Pallas kernels for 0%

profile of v1, /device:TPU:0, one launch (start us, length us, event | category | flops | bytes accessed | tf_op | source)
XLA Modules:
  0.0 136.0 jit_solution(1620884316589289715)
XLA Ops:
  0.6 0.9 slice_bitcast_fusion
  1.5 2.4 %collective-permute-start = (bf16[3,4096]{1,0:T(4,128)(2,1)S(1)}, bf16[3,4096]{1,0:T(4,128)(2,1)S(1)}, u32[]{:S(2)}, u32[]{:S(2)}) collective-permute-start(bf16[3,4096]{1,0:T(4,128)(2,1)S(1)} %slice_bitcast_fusion), channel_id=1, source_target_pairs={{0,1},{1,2},{2,3},{4,5},{5,6},{6,7},{8,9},{9,10},{10,11},{12,13},{... | collective-permute-start | bytes 73736 | tf_op jit(solution)/shard_map/ppermute | solution.py:341
  3.9 0.8 copy.20
  4.7 0.8 copy.24
  5.8 1.1 convert_element_type.56.cm_ref
  6.9 1.4 %broadcast_in_dim.25.bb_ref = f32[2048,128]{1,0:T(8,128)} broadcast(f32[2048]{0:T(1024)S(1)} %broadcast_in_dim.24), dimensions={0} | broadcast | bytes 1056768 | tf_op jit(solution)/shard_map/broadcast_in_dim | solution.py:343
  8.3 27.3 %shard_map.161 = (bf16[48,4096]{1,0:T(8,128)(2,1)}, f32[32,128,128]{2,1,0:T(8,128)}, f32[32,128,128]{2,1,0:T(8,128)}, f32[32,128,128]{2,1,0:T(8,128)}, f32[128,4...) custom-call(bf16[128,4096]{1,0:T(8,128)(2,1)} %bitcast.37, ...), custom_call_target="tpu_custom_call" | custom-call | flops 67108864 | bytes 10485760 | tf_op jit(solution)/shard_map/pallas_call | solution.py:352
  35.6 2.7 %collective-permute-start.1 = (bf16[48,4096]{1,0:T(8,128)(2,1)}, bf16[48,4096]{1,0:T(8,128)(2,1)S(1)}, u32[]{:S(2)}, u32[]{:S(2)}) collective-permute-start(bf16[48,4096]{1,0:T(8,128)(2,1)} %get-tuple-element.22), channel_id=1, source_target_pairs={{0,1},{1,0},{2,3},{3,2},{4,5},{5,4},{6,7},{7,6},{8,9},{9,8},{10,11... | collective-permute-start | bytes 1179656 | tf_op jit(solution)/shard_map/ppermute | solution.py:261
  38.3 0.9 convert_reduce_fusion
  39.2 0.7 collective-permute-done.1
  39.9 1.2 fusion.8
  41.8 1.1 convert_element_type.66.bd_ref
  42.9 4.1 %collective-permute-done.2 = bf16[16,4096]{1,0:T(8,128)(2,1)S(1)} collective-permute-done((bf16[16,4096]{1,0:T(8,128)(2,1)S(1)}, bf16[16,4096]{1,0:T(8,128)(2,1)S(1)}, u32[]{:S(2)}, u32[]{:S(2)}) %collective-permute-start.2) | collective-permute-done | bytes 131104 | tf_op jit(solution)/shard_map/ppermute | solution.py:261
  46.9 2.0 %fusion.2 = (f32[16,4096]{1,0:T(8,128)}, f32[16,4096]{1,0:T(8,128)}) fusion(bf16[16,4096]{1,0:T(8,128)(2,1)S(1)} %collective-permute-done.2, pred[]{:T(512)S(6)} %eq.31, pred[]{:T(512)S(6)} %eq.30, bf16[48,4096]{1,0:T(8,128)(2,1)S(1)} %collective-permute-done.1, bf16[48,4096]{1,0:T(8,128)(2,1)} %get-tuple-element.22, f32[4096]{0:T(1024)S(1)} %convert_reduce_fusion.1, ...), kind=kLoop, calls=%fused_computation.12 | loop fusion | flops 1310720 | bytes 1474562 | tf_op jit(solution)/shard_map/jit(_where)/select_n | solution.py:303
  48.9 1.3 broadcast_in_dim.28.cb2_ref
  50.2 52.8 %shard_map.162 = (bf16[128,4096]{1,0:T(8,128)(2,1)}, bf16[3,4096]{1,0:T(4,128)(2,1)}, f32[16,4096]{1,0:T(8,128)}, f32[16,128]{1,0:T(8,128)}, f32[16,128]{1,0:T(8,128)}, /*index=5*/f32[24,4096]{1,0:T(8,128)}) custom-call(f32[16,4096]{1,0:T(8,128)} %get-tuple-element.37.si_ref, f32[16,4096]{1,0:T(8,128)} %get-tuple-element.36.ai_ref, ...), custom_call_target="tpu_custom_call" | custom-call | flops 167772160 | bytes 12582912 | tf_op jit(solution)/shard_map/pallas_call | solution.py:367
  103.1 1.0 constant_dynamic-slice_fusion.1
  104.2 1.4 %collective-permute-done.4 = f32[24,2048]{1,0:T(8,128)S(1)} collective-permute-done((f32[24,2048]{1,0:T(8,128)S(1)}, f32[24,2048]{1,0:T(8,128)S(1)}, u32[]{:S(2)}, u32[]{:S(2)}) %collective-permute-start.4) | collective-permute-done | bytes 196640 | tf_op jit(solution)/shard_map/ppermute | solution.py:261
  105.6 0.9 dynamic-slice_add_fusion
  106.9 4.5 %collective-permute-done.5 = f32[24,1024]{1,0:T(8,128)S(1)} collective-permute-done((f32[24,1024]{1,0:T(8,128)S(1)}, f32[24,1024]{1,0:T(8,128)S(1)}, u32[]{:S(2)}, u32[]{:S(2)}) %collective-permute-start.5) | collective-permute-done | bytes 98336 | tf_op jit(solution)/shard_map/ppermute | solution.py:261
  111.5 1.6 %collective-permute-start.6 = (f32[24,1024]{1,0:T(8,128)S(1)}, f32[24,1024]{1,0:T(8,128)S(1)}, u32[]{:S(2)}, u32[]{:S(2)}) collective-permute-start(f32[24,1024]{1,0:T(8,128)S(1)} %dynamic-slice_add_fusion.1), channel_id=1, source_target_pairs={{0,4},{4,0},{8,12},{12,8},{16,20},{20,16},{24,28},{28,24},{1,5},{5... | collective-permute-start | bytes 294920 | tf_op jit(solution)/shard_map/ppermute | solution.py:261
  113.0 3.1 %collective-permute-done.6 = f32[24,1024]{1,0:T(8,128)S(1)} collective-permute-done((f32[24,1024]{1,0:T(8,128)S(1)}, f32[24,1024]{1,0:T(8,128)S(1)}, u32[]{:S(2)}, u32[]{:S(2)}) %collective-permute-start.6) | collective-permute-done | bytes 98336 | tf_op jit(solution)/shard_map/ppermute | solution.py:261
  116.2 1.6 %collective-permute-start.7 = (f32[24,1024]{1,0:T(8,128)S(1)}, f32[24,1024]{1,0:T(8,128)S(1)}, u32[]{:S(2)}, u32[]{:S(2)}) collective-permute-start(f32[24,1024]{1,0:T(8,128)S(1)} %add.69), channel_id=1, source_target_pairs={{0,8},{4,12},{8,0},{12,4},{16,24},{20,28},{24,16},{28,20},{1,9},{5... | collective-permute-start | bytes 294920 | tf_op jit(solution)/shard_map/ppermute | solution.py:261
  117.8 3.0 %collective-permute-done.7 = f32[24,1024]{1,0:T(8,128)S(1)} collective-permute-done((f32[24,1024]{1,0:T(8,128)S(1)}, f32[24,1024]{1,0:T(8,128)S(1)}, u32[]{:S(2)}, u32[]{:S(2)}) %collective-permute-start.7) | collective-permute-done | bytes 98336 | tf_op jit(solution)/shard_map/ppermute | solution.py:261
  120.9 3.1 %collective-permute-start.8 = (f32[24,1024]{1,0:T(8,128)S(1)}, f32[24,1024]{1,0:T(8,128)S(1)}, u32[]{:S(2)}, u32[]{:S(2)}) collective-permute-start(f32[24,1024]{1,0:T(8,128)S(1)} %add.70), channel_id=1, source_target_pairs={{0,16},{4,20},{8,24},{12,28},{16,0},{20,4},{24,8},{28,12},{1,17},{... | collective-permute-start | bytes 294920 | tf_op jit(solution)/shard_map/ppermute | solution.py:261
  124.0 3.6 %collective-permute-done.8 = f32[24,1024]{1,0:T(8,128)S(1)} collective-permute-done((f32[24,1024]{1,0:T(8,128)S(1)}, f32[24,1024]{1,0:T(8,128)S(1)}, u32[]{:S(2)}, u32[]{:S(2)}) %collective-permute-start.8) | collective-permute-done | bytes 98336 | tf_op jit(solution)/shard_map/ppermute | solution.py:261
  128.1 1.3 collective-permute-start.3
  129.3 3.0 %collective-permute-done.9 = f32[24,1024]{1,0:T(8,128)S(1)} collective-permute-done((f32[24,1024]{1,0:T(8,128)S(1)}, f32[24,1024]{1,0:T(8,128)S(1)}, u32[]{:S(2)}, u32[]{:S(2)}) %collective-permute-start.9) | collective-permute-done | bytes 98336 | tf_op jit(solution)/shard_map/ppermute | solution.py:261
  132.5 0.7 fusion.14
  133.2 0.7 collective-permute-done.10
  133.9 0.7 fusion.10
  134.7 0.7 pad_maximum_fusion.2
  (29 shorter events, 2.7 us)
Async XLA Ops:
  1.5 5.4 %collective-permute-start = (bf16[3,4096]{1,0:T(4,128)(2,1)S(1)}, bf16[3,4096]{1,0:T(4,128)(2,1)S(1)}, u32[]{:S(2)}, u32[]{:S(2)}) collective-permute-start(bf16[3,4096]{1,0:T(4,128)(2,1)S(1)} %slice_bitcast_fusion), channel_id=1, source_target_pairs={{0,1},{1,2},{2,3},{4,5},{5,6},{6,7},{8,9},{9,10},{10,11},{12,13},{... | collective-permute-start | bytes 73736 | tf_op jit(solution)/shard_map/ppermute | solution.py:341
  6.9 1.4 %copy-start.3 = (bf16[3,4096]{1,0:T(4,128)(2,1)}, bf16[3,4096]{1,0:T(4,128)(2,1)S(1)}, u32[]{:S(2)}) copy-start(bf16[3,4096]{1,0:T(4,128)(2,1)S(1)} %collective-permute-done.rim_ref) | copy-start | bytes 73732
  8.3 31.6 %copy-start = (f32[16,4096]{1,0:T(8,128)S(1)}, f32[16,4096]{1,0:T(8,128)}, u32[]{:S(2)}) copy-start(f32[16,4096]{1,0:T(8,128)} %dl_ref.3) | copy-start | bytes 786436
  35.6 4.3 %collective-permute-start.1 = (bf16[48,4096]{1,0:T(8,128)(2,1)}, bf16[48,4096]{1,0:T(8,128)(2,1)S(1)}, u32[]{:S(2)}, u32[]{:S(2)}) collective-permute-start(bf16[48,4096]{1,0:T(8,128)(2,1)} %get-tuple-element.22), channel_id=1, source_target_pairs={{0,1},{1,0},{2,3},{3,2},{4,5},{5,4},{6,7},{7,6},{8,9},{9,8},{10,11... | collective-permute-start | bytes 1179656 | tf_op jit(solution)/shard_map/ppermute | solution.py:261
  41.1 5.8 %collective-permute-start.2 = (bf16[16,4096]{1,0:T(8,128)(2,1)S(1)}, bf16[16,4096]{1,0:T(8,128)(2,1)S(1)}, u32[]{:S(2)}, u32[]{:S(2)}) collective-permute-start(bf16[16,4096]{1,0:T(8,128)(2,1)S(1)} %fusion.8), channel_id=1, source_target_pairs={{0,2},{1,3},{2,0},{3,1},{4,6},{5,7},{6,4},{7,5},{8,10},{9,11},{10,... | collective-permute-start | bytes 393224 | tf_op jit(solution)/shard_map/ppermute | solution.py:261
  103.1 25.0 %copy-start.2 = (bf16[3,4096]{1,0:T(4,128)(2,1)S(1)}, bf16[3,4096]{1,0:T(4,128)(2,1)}, u32[]{:S(2)}) copy-start(bf16[3,4096]{1,0:T(4,128)(2,1)} %get-tuple-element.32) | copy-start | bytes 73732
  103.1 29.4 %copy-start.1 = (f32[16,4096]{1,0:T(8,128)S(1)}, f32[16,4096]{1,0:T(8,128)}, u32[]{:S(2)}) copy-start(f32[16,4096]{1,0:T(8,128)} %get-tuple-element.31) | copy-start | bytes 786436
  104.1 1.5 %collective-permute-start.4 = (f32[24,2048]{1,0:T(8,128)S(1)}, f32[24,2048]{1,0:T(8,128)S(1)}, u32[]{:S(2)}, u32[]{:S(2)}) collective-permute-start(f32[24,2048]{1,0:T(8,128)S(1)} %constant_dynamic-slice_fusion.1), channel_id=1, source_target_pairs={{0,1},{1,0},{2,3},{3,2},{4,5},{5,4},{6,7},{7,6},{8,9},{9,8},{10,11... | collective-permute-start | bytes 589832 | tf_op jit(solution)/shard_map/ppermute | solution.py:261
  106.6 4.9 %collective-permute-start.5 = (f32[24,1024]{1,0:T(8,128)S(1)}, f32[24,1024]{1,0:T(8,128)S(1)}, u32[]{:S(2)}, u32[]{:S(2)}) collective-permute-start(f32[24,1024]{1,0:T(8,128)S(1)} %constant_dynamic-slice_fusion), channel_id=1, source_target_pairs={{0,2},{1,3},{2,0},{3,1},{4,6},{5,7},{6,4},{7,5},{8,10},{9,11},{10,... | collective-permute-start | bytes 294920 | tf_op jit(solution)/shard_map/ppermute | solution.py:261
  111.5 4.7 %collective-permute-start.6 = (f32[24,1024]{1,0:T(8,128)S(1)}, f32[24,1024]{1,0:T(8,128)S(1)}, u32[]{:S(2)}, u32[]{:S(2)}) collective-permute-start(f32[24,1024]{1,0:T(8,128)S(1)} %dynamic-slice_add_fusion.1), channel_id=1, source_target_pairs={{0,4},{4,0},{8,12},{12,8},{16,20},{20,16},{24,28},{28,24},{1,5},{5... | collective-permute-start | bytes 294920 | tf_op jit(solution)/shard_map/ppermute | solution.py:261
  116.2 4.7 %collective-permute-start.7 = (f32[24,1024]{1,0:T(8,128)S(1)}, f32[24,1024]{1,0:T(8,128)S(1)}, u32[]{:S(2)}, u32[]{:S(2)}) collective-permute-start(f32[24,1024]{1,0:T(8,128)S(1)} %add.69), channel_id=1, source_target_pairs={{0,8},{4,12},{8,0},{12,4},{16,24},{20,28},{24,16},{28,20},{1,9},{5... | collective-permute-start | bytes 294920 | tf_op jit(solution)/shard_map/ppermute | solution.py:261
  120.9 6.8 %collective-permute-start.8 = (f32[24,1024]{1,0:T(8,128)S(1)}, f32[24,1024]{1,0:T(8,128)S(1)}, u32[]{:S(2)}, u32[]{:S(2)}) collective-permute-start(f32[24,1024]{1,0:T(8,128)S(1)} %add.70), channel_id=1, source_target_pairs={{0,16},{4,20},{8,24},{12,28},{16,0},{20,4},{24,8},{28,12},{1,17},{... | collective-permute-start | bytes 294920 | tf_op jit(solution)/shard_map/ppermute | solution.py:261
  127.7 4.7 %collective-permute-start.9 = (f32[24,1024]{1,0:T(8,128)S(1)}, f32[24,1024]{1,0:T(8,128)S(1)}, u32[]{:S(2)}, u32[]{:S(2)}) collective-permute-start(f32[24,1024]{1,0:T(8,128)S(1)} %add.71), channel_id=1, source_target_pairs={{0,2},{1,3},{2,0},{3,1},{4,6},{5,7},{6,4},{7,5},{8,10},{9,11},{10,... | collective-permute-start | bytes 294920 | tf_op jit(solution)/shard_map/ppermute | solution.py:261
  128.1 4.4 %collective-permute-start.3 = (bf16[3,4096]{1,0:T(4,128)(2,1)S(1)}, bf16[3,4096]{1,0:T(4,128)(2,1)S(1)}, u32[]{:S(2)}, u32[]{:S(2)}) collective-permute-start(bf16[3,4096]{1,0:T(4,128)(2,1)S(1)} %copy-done.2), channel_id=1, source_target_pairs={{1,0},{2,1},{3,2},{5,4},{6,5},{7,6},{9,8},{10,9},{11,10},{13,12},{... | collective-permute-start | bytes 73736 | tf_op jit(solution)/shard_map/ppermute | solution.py:392
  132.4 1.5 %collective-permute-start.10 = (f32[24,2048]{1,0:T(8,128)S(1)}, f32[24,2048]{1,0:T(8,128)S(1)}, u32[]{:S(2)}, u32[]{:S(2)}) collective-permute-start(f32[24,2048]{1,0:T(8,128)S(1)} %pad_maximum_fusion), channel_id=1, source_target_pairs={{0,1},{1,0},{2,3},{3,2},{4,5},{5,4},{6,7},{7,6},{8,9},{9,8},{10,11... | collective-permute-start | bytes 589832 | tf_op jit(solution)/shard_map/ppermute | solution.py:261

commit v2 on v1

v2 whole, which is shorter than its diff:
```python
import math

import jax
import jax.numpy as jnp
from jax import lax
from jax.experimental import pallas as pl
from jax.experimental.pallas import tpu as pltpu
from jax.sharding import PartitionSpec as P

F32 = jnp.float32
BF16 = jnp.bfloat16
LOG2E = 1.0 / math.log(2.0)
BLOCK = 16
LANES = 128
WIDTH = 512
VMEM = 60 * 1024 * 1024


def lane_slices(width):
    return [slice(j, j + LANES) for j in range(0, width, LANES)]


def row_of(ref, t, j):
    row = ref[j, pl.ds(t, 8, stride=0), :]
    return jnp.concatenate([row, row], axis=0)


def put(ref, rows, value):
    for j in range(ref.shape[0]):
        ref[j, rows, :] = value[:, j * LANES : (j + 1) * LANES]


def take(ref, rows):
    return jnp.concatenate([ref[j, rows, :] for j in range(ref.shape[0])], axis=1)


def joined_tiles(ref):
    return jnp.concatenate([ref[j] for j in range(ref.shape[0])], axis=1)


def row_sum(value):
    total = value[0:8]
    for r in range(8, value.shape[0], 8):
        total = total + value[r : r + 8]
    return total


def set_rates(dl_ref, rates):
    for j, s in enumerate(lane_slices(dl_ref.shape[1])):
        rates[j] = -jnp.exp(dl_ref[:, s]) * LOG2E


def widen(b_ref, c_ref, bw_ref, cw_ref, bd_ref):
    states, length = b_ref.shape
    for t in range(length):
        rows = slice(t * states, (t + 1) * states)
        bw_ref[rows, :] = jnp.broadcast_to(b_ref[:, t : t + 1], (states, LANES))
        cw_ref[rows, :] = jnp.broadcast_to(c_ref[:, t : t + 1], (states, LANES))
    n = lax.broadcasted_iota(jnp.int32, (states, BLOCK * states), 0)
    m = lax.broadcasted_iota(jnp.int32, (states, BLOCK * states), 1)
    repeat = jnp.where(n == m % states, 1.0, 0.0).astype(BF16)
    spread = lax.dot_general(b_ref[...].astype(BF16), repeat, (((0,), (0,)), ((), ())), preferred_element_type=F32)
    t = lax.broadcasted_iota(jnp.int32, (length, BLOCK * states), 0)
    m = lax.broadcasted_iota(jnp.int32, (length, BLOCK * states), 1)
    bd_ref[...] = jnp.where(t % BLOCK == m // states, spread, 0.0).astype(BF16)


def ends_kernel(x_ref, rim_ref, step_ref, dy_ref, b_ref, c_ref, cw_ref, cb_ref, sb_ref, dl_ref,
                out_ref, dls, dus, u_ref, sig_ref, slope_ref, dub_ref, bw_ref, cw2_ref, bd_ref,
                xe, dyf, rates):
    length, width = x_ref.shape
    states = dl_ref.shape[0]
    taps = cw_ref.shape[0]
    blocks = length // BLOCK
    weights = [cw_ref[k : k + 1, :] for k in range(taps)]
    bias, shift = cb_ref[...], sb_ref[...]
    slices = lane_slices(width)

    @pl.when(pl.program_id(0) == 0)
    def _():
        widen(b_ref, c_ref, bw_ref, cw2_ref, bd_ref)

    set_rates(dl_ref, rates)
    xe[0:8, :] = jnp.zeros((8, width), F32)
    xe[8 - (taps - 1) : 8, :] = rim_ref[...].astype(F32)
    total = jnp.zeros((8, width), F32)
    for b in range(blocks):
        rows = slice(b * BLOCK, (b + 1) * BLOCK)
        xe[8 + b * BLOCK : 8 + (b + 1) * BLOCK, :] = x_ref[rows, :].astype(F32)
        put(dyf, rows, dy_ref[rows, :].astype(F32))
        z = jnp.exp(step_ref[rows, :].astype(F32) + shift)
        series = z * (1.0 - z * (0.5 - z * (1.0 / 3.0 - 0.25 * z)))
        delta = jnp.where(z < 0.015625, series, jnp.log(1.0 + z))
        p = bias
        for k in range(taps):
            first = b * BLOCK + 9 - taps + k
            p = p + weights[k] * xe[first : first + BLOCK, :]
        gate = 1.0 / (1.0 + jnp.exp(-p))
        u = p * gate
        du = delta * u
        put(dls, rows, delta)
        put(dus, rows, du)
        u_ref[rows, :] = u
        sig_ref[rows, :] = z / (1.0 + z)
        slope_ref[rows, :] = gate + u * (1.0 - gate)
        dub_ref[rows, :] = du.astype(BF16)
        total = total + row_sum(delta)
    total = jnp.sum(total, axis=0, keepdims=True)

    def block(b, carry):
        state, decay, adjoint = (list(part) for part in carry)
        base = pl.multiple_of(b * BLOCK, BLOCK)
        for i in range(BLOCK):
            t = base + i
            rows = pl.ds(pl.multiple_of(t * states, states), states)
            b_column, c_column = bw_ref[rows, :], cw2_ref[rows, :]
            for j in range(len(slices)):
                a = jnp.exp2(row_of(dls, t, j) * rates[j])
                state[j] = a * state[j] + b_column * row_of(dus, t, j)
                decay[j] = decay[j] * a
                adjoint[j] = adjoint[j] + decay[j] * (c_column * row_of(dyf, t, j))
        return tuple(state), tuple(decay), tuple(adjoint)

    zero = tuple(jnp.zeros((states, LANES), F32) for _ in slices)
    one = tuple(jnp.ones((states, LANES), F32) for _ in slices)
    state, _, adjoint = lax.fori_loop(0, blocks, block, (zero, one, zero), unroll=blocks)
    for j, s in enumerate(slices):
        out_ref[0:states, s] = state[j].astype(BF16)
        out_ref[states : 2 * states, s] = adjoint[j].astype(BF16)
    high = total.astype(BF16)
    rest = total - high.astype(F32)
    middle = rest.astype(BF16)
    low = (rest - middle.astype(F32)).astype(BF16)
    row = lax.broadcasted_iota(jnp.int32, (16, width), 0)
    packed = jnp.where(row == 0, high.astype(F32), jnp.where(row == 1, middle.astype(F32), low.astype(F32)))
    out_ref[2 * states : 2 * states + 16, :] = packed.astype(BF16)


def main_kernel(si_ref, ai_ref, x_ref, rim_ref, dy_ref, dls, dus, u_ref, sig_ref, slope_ref, dub_ref,
                bb_ref, cb2_ref, bd_ref, cw_ref, dl_ref, sk_ref,
                gin_ref, borrow_ref, tail_ref, gb_ref, gc_ref, pg_ref,
                xe, dyf, ahs, hb, dpe, rates, naturals):
    length, width = x_ref.shape
    states = dl_ref.shape[0]
    taps = cw_ref.shape[0]
    blocks = length // BLOCK
    slices = lane_slices(width)
    tiles = range(len(slices))
    skip = sk_ref[...]

    @pl.when(pl.program_id(0) == 0)
    def _():
        gb_ref[...] = jnp.zeros_like(gb_ref)
        gc_ref[...] = jnp.zeros_like(gc_ref)

    set_rates(dl_ref, rates)
    for j, s in enumerate(slices):
        naturals[j] = (-jnp.exp(dl_ref[:, s])).astype(BF16)
    xe[0:8, :] = jnp.zeros((8, width), F32)
    xe[8 - (taps - 1) : 8, :] = rim_ref[...].astype(F32)
    for b in range(blocks):
        rows = slice(b * BLOCK, (b + 1) * BLOCK)
        xe[8 + b * BLOCK : 8 + (b + 1) * BLOCK, :] = x_ref[rows, :].astype(F32)
        put(dyf, rows, dy_ref[rows, :].astype(F32))
    dpe[0:8, :] = jnp.zeros((8, width), F32)
    dpe[length + 8 : length + 16, :] = jnp.zeros((8, width), F32)
    lane = lax.broadcasted_iota(jnp.int32, (states, length), 1)
    by_rows = (((1,), (1,)), ((), ()))

    def picked(table, product, b):
        for i in range(BLOCK):
            table = jnp.where(lane == b * BLOCK + i, product[i * states : (i + 1) * states], table)
        return table

    state = [si_ref[:, s] for s in slices]
    gc = jnp.zeros((states, length), F32)
    for b in range(blocks):
        for i in range(BLOCK):
            t = b * BLOCK + i
            rows = slice(t * states, (t + 1) * states)
            column = bb_ref[rows, :]
            for j in tiles:
                kept = jnp.exp2(row_of(dls, t, j) * rates[j]) * state[j]
                ahs[j, rows, :] = kept.astype(BF16)
                state[j] = kept + column * row_of(dus, t, j)
                hb[b % 2, j, i * states : (i + 1) * states, :] = state[j].astype(BF16)
        product = lax.dot_general(joined_tiles(hb.at[b % 2]), dy_ref[...], by_rows, preferred_element_type=F32)
        gc = picked(gc, product, b)
    gc_ref[...] += gc

    rows_of = lax.broadcasted_iota(jnp.int32, (BLOCK, BLOCK * states), 0)
    cols_of = lax.broadcasted_iota(jnp.int32, (BLOCK, BLOCK * states), 1)
    over_states = jnp.where(rows_of == cols_of // states, 1.0, 0.0).astype(BF16)
    rows_of = lax.broadcasted_iota(jnp.int32, (states, BLOCK * states), 0)
    cols_of = lax.broadcasted_iota(jnp.int32, (states, BLOCK * states), 1)
    over_steps = jnp.where(rows_of == cols_of % states, 1.0, 0.0).astype(BF16)

    adjoint = [ai_ref[:, s] for s in slices]
    gb = jnp.zeros((states, length), F32)
    rates_sum = [jnp.zeros((states, 2 * LANES), F32) for _ in range(0, len(slices), 2)]
    sums = [jnp.zeros((8, width), F32) for _ in range(taps + 3)]
    weights = [cw_ref[k : k + 1, :] for k in range(taps)]
    for b in reversed(range(blocks)):
        kept = {}
        for i in reversed(range(BLOCK)):
            t = b * BLOCK + i
            rows = slice(t * states, (t + 1) * states)
            column = cb2_ref[rows, :]
            for j in tiles:
                delta = row_of(dls, t, j)
                g = column * row_of(dyf, t, j) + adjoint[j]
                adjoint[j] = jnp.exp2(delta * rates[j]) * g
                low = g.astype(BF16)
                q = low * ahs[j, rows, :]
                kept[i, j] = low, q * naturals[j], q * delta.astype(BF16)

        def operand(m, which):
            return jnp.concatenate(
                [jnp.concatenate([kept[i, j][which] for i in range(BLOCK)], axis=0) for j in (2 * m, 2 * m + 1)],
                axis=1)

        rows = slice(b * BLOCK, (b + 1) * BLOCK)
        ddu, dwn, product = [], [], None
        for m in range(len(rates_sum)):
            g_block = operand(m, 0)
            ddu.append(jnp.dot(bd_ref[rows, :], g_block, preferred_element_type=F32))
            dwn.append(jnp.dot(over_states, operand(m, 1), preferred_element_type=F32))
            rates_sum[m] = rates_sum[m] + jnp.dot(over_steps, operand(m, 2), preferred_element_type=F32)
            part = lax.dot_general(g_block, dub_ref[:, 2 * m * LANES : 2 * (m + 1) * LANES], by_rows,
                                   preferred_element_type=F32)
            product = part if product is None else product + part
        gb = picked(gb, product, b)
        ddu, dwn = jnp.concatenate(ddu, axis=1), jnp.concatenate(dwn, axis=1)
        dy, u = take(dyf, rows), u_ref[rows, :]
        grad_v = (ddu * u + dwn) * sig_ref[rows, :]
        grad_p = (ddu * take(dls, rows) + skip * dy) * slope_ref[rows, :]
        dpe[8 + b * BLOCK : 8 + (b + 1) * BLOCK, :] = grad_p
        sums[taps] += row_sum(grad_p)
        sums[taps + 1] += row_sum(grad_v)
        sums[taps + 2] += row_sum(dy * u)
        grad_x = weights[taps - 1] * grad_p
        for k in range(taps):
            first = b * BLOCK + 9 - taps + k
            sums[k] += row_sum(grad_p * xe[first : first + BLOCK, :])
            if k < taps - 1:
                first = b * BLOCK + 7 + taps - k
                grad_x = grad_x + weights[k] * dpe[first : first + BLOCK, :]
        gin_ref[rows, :] = grad_x.astype(BF16)
        if b == blocks - 1:
            tail_ref[...] = grad_x
    gb_ref[...] += gb
    rates_sum = jnp.concatenate(rates_sum, axis=1)
    for j, s in enumerate(slices):
        pg_ref[0:states, s] = rates_sum[:, s] * (-jnp.exp(dl_ref[:, s]))
    grad_rim = weights[0] * dpe[taps - 1 : taps + 7, :]
    for k in range(1, taps):
        grad_rim = grad_rim + weights[k] * dpe[taps - 1 - k : taps + 7 - k, :]
    borrow_ref[...] = grad_rim[8 - borrow_ref.shape[0] : 8].astype(BF16)
    row = lax.broadcasted_iota(jnp.int32, (8, width), 0)
    packed = jnp.zeros((8, width), F32)
    for k in range(taps + 3):
        packed = jnp.where(row == k, jnp.sum(sums[k], axis=0, keepdims=True), packed)
    pg_ref[states : states + 8, :] = packed


def flipped(value, axis, bit):
    return lax.ppermute(value, axis, [(k, k ^ bit) for k in range(lax.axis_size(axis))])


def add_up(value):
    inner, outer = lax.axis_size("ctx"), lax.axis_size("dp")
    if inner & (inner - 1) or outer & (outer - 1):
        return lax.psum(value, ("dp", "ctx"))
    me = lax.axis_index("ctx")
    bits = [1 << k for k in range(inner.bit_length() - 1)]
    for bit in bits:
        half = value.shape[1] // 2
        upper = (me // bit) % 2
        give = lax.dynamic_slice_in_dim(value, (1 - upper) * half, half, 1)
        got = flipped(give, "ctx", bit)
        value = lax.dynamic_slice_in_dim(value, upper * half, half, 1) + got
    for k in range(outer.bit_length() - 1):
        value = value + flipped(value, "dp", 1 << k)
    for bit in reversed(bits):
        got = flipped(value, "ctx", bit)
        upper = (me // bit) % 2 == 1
        value = jnp.concatenate([jnp.where(upper, got, value), jnp.where(upper, value, got)], axis=1)
    return value


def entering(ends, decay_log):
    states = decay_log.shape[0]
    count, place = lax.axis_size("ctx"), lax.axis_index("ctx")
    rate = -jnp.exp(decay_log)

    def opened(piece):
        total = jnp.sum(piece[2 * states : 2 * states + 3].astype(F32), axis=0, keepdims=True)
        return piece[:states].astype(F32), piece[states : 2 * states].astype(F32), jnp.exp(rate * total)

    if count == 4:
        upper, late = place % 2 == 1, place // 2 == 1
        mine, other = opened(ends), opened(flipped(ends, "ctx", 1))
        pick = lambda a, b: jnp.where(upper, a, b)
        first, second = [pick(b, a) for a, b in zip(mine, other)], [pick(a, b) for a, b in zip(mine, other)]
        both = jnp.where(late, second[1] * first[2] + first[1], first[0] * second[2] + second[0])
        got = flipped(both.astype(BF16), "ctx", 2).astype(F32)
        before, after = jnp.where(late, got, 0.0), jnp.where(late, 0.0, got)
        state = jnp.where(upper, before * first[2] + first[0], before)
        adjoint = jnp.where(upper, after, after * second[2] + second[1])
        return state, adjoint
    gathered = lax.all_gather(ends, "ctx")
    state = adjoint = jnp.zeros(decay_log.shape, F32)
    for k in range(count - 1):
        end, _, decay = opened(gathered[k])
        state = jnp.where(k < place, decay * state + end, state)
    for k in range(count - 1, 0, -1):
        _, end, decay = opened(gathered[k])
        adjoint = jnp.where(k > place, decay * adjoint + end, adjoint)
    return state, adjoint


def whole(a):
    return pl.BlockSpec(a.shape, lambda i: (0,) * a.ndim)


def chunk(rows):
    return pl.BlockSpec((rows, WIDTH), lambda i: (0, i))


def tiled(length):
    return pl.BlockSpec((WIDTH // LANES, length, LANES), lambda i: (i, 0, 0))


def flat(a):
    return a.reshape(1, a.shape[0])


SHAPE = jax.ShapeDtypeStruct
PARAMS = pltpu.CompilerParams(vmem_limit_bytes=VMEM, dimension_semantics=("arbitrary",))


def call_ends(x, rims, step, dy, b_proj, c_proj, conv_weight, conv_bias, step_bias, decay_log):
    (length, channels), states = x.shape, decay_log.shape[0]
    taps, rim = conv_weight.shape[0], rims.shape[0]
    work = length * states * channels
    tiles = WIDTH // LANES
    long = SHAPE((channels // LANES, length, LANES), F32)
    plain = SHAPE((length, channels), F32)
    spread = [SHAPE((length * states, LANES), F32)] * 2 + [SHAPE((length, BLOCK * states), BF16)]
    return pl.pallas_call(
        ends_kernel,
        grid=(channels // WIDTH,),
        in_specs=[chunk(length), chunk(rim), chunk(length), chunk(length), whole(b_proj), whole(c_proj),
                  chunk(taps), chunk(1), chunk(1), chunk(states)],
        out_specs=[chunk(2 * states + 16)] + [tiled(length)] * 2 + [chunk(length)] * 4 + [whole(a) for a in spread],
        out_shape=[SHAPE((2 * states + 16, channels), BF16), long, long, plain, plain, plain,
                   SHAPE((length, channels), BF16)] + spread,
        scratch_shapes=[pltpu.VMEM((length + 16, WIDTH), F32),
                        pltpu.VMEM((tiles, length, LANES), F32),
                        pltpu.VMEM((tiles, states, LANES), F32)],
        compiler_params=PARAMS,
        cost_estimate=pl.CostEstimate(flops=8 * work, bytes_accessed=20 * length * channels, transcendentals=work),
    )(x, rims, step, dy, b_proj, c_proj, conv_weight, flat(conv_bias), flat(step_bias), decay_log)


def call_main(state_in, adjoint_in, x, rims, dy, saved, conv_weight, decay_log, skip_weight):
    (length, channels), states = x.shape, decay_log.shape[0]
    taps, rim = conv_weight.shape[0], rims.shape[0]
    work = length * states * channels
    tiles = WIDTH // LANES
    summed = pl.BlockSpec((states, length), lambda i: (0, 0))
    return pl.pallas_call(
        main_kernel,
        grid=(channels // WIDTH,),
        in_specs=[chunk(states), chunk(states), chunk(length), chunk(rim), chunk(length)] + [tiled(length)] * 2
        + [chunk(length)] * 4 + [whole(a) for a in saved[6:]] + [chunk(taps), chunk(states), chunk(1)],
        out_specs=[chunk(length), chunk(rim), chunk(BLOCK), summed, summed, chunk(states + 8)],
        out_shape=[SHAPE((length, channels), BF16), SHAPE((rim, channels), BF16), SHAPE((BLOCK, channels), F32),
                   SHAPE((states, length), F32), SHAPE((states, length), F32), SHAPE((states + 8, channels), F32)],
        scratch_shapes=[pltpu.VMEM((length + 16, WIDTH), F32),
                        pltpu.VMEM((tiles, length, LANES), F32),
                        pltpu.VMEM((tiles, length * states, LANES), BF16),
                        pltpu.VMEM((2, tiles, BLOCK * states, LANES), BF16),
                        pltpu.VMEM((length + 16, WIDTH), F32),
                        pltpu.VMEM((tiles, states, LANES), F32),
                        pltpu.VMEM((tiles, states, LANES), BF16)],
        compiler_params=PARAMS,
        cost_estimate=pl.CostEstimate(flops=20 * work, bytes_accessed=24 * length * channels, transcendentals=2 * work),
    )(state_in, adjoint_in, x, rims, dy, *saved, conv_weight, decay_log, flat(skip_weight))


def per_device(scan_input, step_raw, input_proj, output_proj, out_cotangent, conv_weight, conv_bias, step_bias,
               decay_log, skip_weight):
    documents, length, channels = scan_input.shape
    states, taps = decay_log.shape[0], conv_weight.shape[0]
    rim = taps - 1
    count = lax.axis_size("ctx")
    forth = [(k, k + 1) for k in range(count - 1)]
    back = [(k + 1, k) for k in range(count - 1)]

    def one(x, step, b_proj, c_proj, dy):
        rims = lax.ppermute(x[length - rim :, :], "ctx", forth)
        ends, *saved = call_ends(x, rims, step, dy, b_proj, c_proj, conv_weight, conv_bias, step_bias, decay_log)
        state_in, adjoint_in = entering(ends, decay_log)
        return call_main(state_in, adjoint_in, x, rims, dy, saved, conv_weight, decay_log, skip_weight)

    outs = []
    for d in range(documents):
        gin, borrow, tail, gb, gc, sums = one(
            scan_input[d], step_raw[d], input_proj[d], output_proj[d], out_cotangent[d])
        given = lax.ppermute(borrow, "ctx", back).astype(F32)
        tail = (tail + jnp.pad(given, ((BLOCK - rim, 0), (0, 0)))).astype(BF16)
        gin = lax.dynamic_update_slice(gin, tail, (length - BLOCK, 0))
        outs.append((gin, gb, gc, sums))
    sums = add_up(sum(o[3] for o in outs))
    return (
        jnp.stack([o[0] for o in outs]),
        jnp.stack([o[1] for o in outs]),
        jnp.stack([o[2] for o in outs]),
        sums[states : states + taps],
        sums[states + taps],
        sums[states + taps + 1],
        sums[:states],
        sums[states + taps + 2],
    )


def solution(mesh):
    split, columns = P("dp", "ctx", None), P("dp", None, "ctx")
    return jax.shard_map(
        per_device,
        mesh=mesh,
        in_specs=(split, split, columns, columns, split, P(), P(), P(), P(), P()),
        out_specs=(split, columns, columns, P(), P(), P(), P(), P()),
        check_vma=False,
    )
```

time: 136 us -> 98.5 us (0.72)
  Pallas kernels: 80.1 us -> 45.9 us
  local copies, waits for them, and re-layouts: 8.52 us -> 2.48 us
  starting transfers between devices: 14.2 us -> 19.2 us
  waiting for transfers between devices: 24.2 us -> 21.9 us
    pallas_call x2, Pallas kernels: 80.1 us -> 45.9 us  [the longest x1 28 us: call_main(): pl.pallas_call(main_kernel, grid=(channels // WIDTH,), in_specs=[chunk(st...]
    ppermute x9, starting transfers between devices: 10.5 us -> 15.6 us  [flipped(): lax.ppermute(value, axis, [(k, k ^ bit) for k in range(lax.axis_size(axis...]
    ppermute x9, waiting for transfers between devices: 24.2 us -> 21 us  [flipped(): lax.ppermute(value, axis, [(k, k ^ bit) for k in range(lax.axis_size(axis...]
    broadcast_in_dim x4 -> x0, local copies, waits for them, and re-layouts: 2.85 us -> none  [the longest x2 1.46 us: one(): jnp.broadcast_to(b_rows.reshape(length * states, 1), (length * states, LA...]
    convert_element_type x2 -> x0, local copies, waits for them, and re-layouts: 2.19 us -> none  [the longest x1 1.1 us: one(): c_diag = (c_rows.reshape(blocks, 1, BLOCK, states) * states_eye[None, :,...]
  transfers between devices with their start and end apart: 11 -> 11, of which waited for: 9 -> 11; matrix products, arithmetic and copies ran while one was open for 4% -> 2% of each run, Pallas kernels for 0% -> 0%
where the time goes in v2:
time: 98.5 us; the launch traced here: 98.1 us
  Pallas kernels  45.9 us (47%)
  waiting for transfers between devices  21.9 us (22%)
  starting transfers between devices  19.2 us (19%)
  other arithmetic  7.84 us (8%)
  local copies, waits for them, and re-layouts  2.48 us (3%)
    pallas_call x1, Pallas kernels, call_main(): pl.pallas_call(main_kernel, grid=(channels // WIDTH,), in_specs=[chunk(st...  28 us
    ppermute x9, waiting for transfers between devices, flipped(): lax.ppermute(value, axis, [(k, k ^ bit) for k in range(lax.axis_size(axis...  21 us
    pallas_call x1, Pallas kernels, call_ends(): pl.pallas_call(ends_kernel, grid=(channels // WIDTH,), in_specs=[chunk(le...  17.8 us
    ppermute x9, starting transfers between devices, flipped(): lax.ppermute(value, axis, [(k, k ^ bit) for k in range(lax.axis_size(axis...  15.6 us
    ppermute x1, starting transfers between devices, one(): rims = lax.ppermute(x[length - rim:, :], 'ctx', forth)  2.36 us
  transfers between devices with their start and end apart: 11, of which 11 were waited for; matrix products, arithmetic and copies ran while one was open for 2% of the time, Pallas kernels for 0%

profile of v2, /device:TPU:0, one launch (start us, length us, event | category | flops | bytes accessed | tf_op | source)
XLA Modules:
  0.0 98.1 jit_solution(9254024061891346905)
XLA Ops:
  0.6 0.9 slice_bitcast_fusion
  1.5 2.4 %collective-permute-start = (bf16[3,4096]{1,0:T(4,128)(2,1)S(1)}, bf16[3,4096]{1,0:T(4,128)(2,1)S(1)}, u32[]{:S(2)}, u32[]{:S(2)}) collective-permute-start(bf16[3,4096]{1,0:T(4,128)(2,1)S(1)} %slice_bitcast_fusion), channel_id=1, source_target_pairs={{0,1},{1,2},{2,3},{4,5},{5,6},{6,7},{8,9},{9,10},{10,11},{12,13},{... | collective-permute-start | bytes 73736 | tf_op jit(solution)/shard_map/ppermute | solution.py:402
  3.9 0.8 collective-permute-done.rim_ref
  4.7 0.6 copy-done.3
  5.3 17.8 %shard_map.161 = (bf16[48,4096]{1,0:T(8,128)(2,1)}, f32[32,128,128]{2,1,0:T(8,128)}, f32[32,128,128]{2,1,0:T(8,128)}, f32[128,4096]{1,0:T(8,128)}, f32[128,4096]...) custom-call(bf16[128,4096]{1,0:T(8,128)(2,1)} %bitcast.23, ...), custom_call_target="tpu_custom_call" | custom-call | flops 67108864 | bytes 10485760 | tf_op jit(solution)/shard_map/pallas_call | solution.py:350
  23.1 2.9 %collective-permute-start.1 = (bf16[48,4096]{1,0:T(8,128)(2,1)}, bf16[48,4096]{1,0:T(8,128)(2,1)S(1)}, u32[]{:S(2)}, u32[]{:S(2)}) collective-permute-start(bf16[48,4096]{1,0:T(8,128)(2,1)} %get-tuple-element.24), channel_id=1, source_target_pairs={{0,1},{1,0},{2,3},{3,2},{4,5},{5,4},{6,7},{7,6},{8,9},{9,8},{10,11... | collective-permute-start | bytes 1179656 | tf_op jit(solution)/shard_map/ppermute | solution.py:267
  26.0 0.9 convert_reduce_fusion
  26.9 0.7 collective-permute-done.1
  27.6 1.2 %fusion.8 = bf16[16,4096]{1,0:T(8,128)(2,1)S(1)} fusion(pred[]{:T(512)S(6)} %eq.17, pred[]{:T(512)S(6)} %eq.16, bf16[48,4096]{1,0:T(8,128)(2,1)S(1)} %collective-permute-done.1, bf16[48,4096]{1,0:T(8,128)(2,1)} %get-tuple-element.24, f32[4096]{0:T(1024)S(1)} %convert_reduce_fusion, f32[4096]{0:T(1024)S(1)} %convert_reduce_fusion.1, f32[16,4096]{1,0:T(8,128)S(1)} %copy-done), kind=kLoop, calls=%fused_computation.16 | loop fusion | flops 1245184 | bytes 950274 | tf_op jit(solution)/shard_map/convert_element_type | solution.py:306
  28.8 2.6 %collective-permute-start.2 = (bf16[16,4096]{1,0:T(8,128)(2,1)S(1)}, bf16[16,4096]{1,0:T(8,128)(2,1)S(1)}, u32[]{:S(2)}, u32[]{:S(2)}) collective-permute-start(bf16[16,4096]{1,0:T(8,128)(2,1)S(1)} %fusion.8), channel_id=1, source_target_pairs={{0,2},{1,3},{2,0},{3,1},{4,6},{5,7},{6,4},{7,5},{8,10},{9,11},{10,... | collective-permute-start | bytes 393224 | tf_op jit(solution)/shard_map/ppermute | solution.py:267
  31.5 3.8 %collective-permute-done.2 = bf16[16,4096]{1,0:T(8,128)(2,1)S(1)} collective-permute-done((bf16[16,4096]{1,0:T(8,128)(2,1)S(1)}, bf16[16,4096]{1,0:T(8,128)(2,1)S(1)}, u32[]{:S(2)}, u32[]{:S(2)}) %collective-permute-start.2) | collective-permute-done | bytes 131104 | tf_op jit(solution)/shard_map/ppermute | solution.py:267
  35.2 2.0 %fusion.2 = (f32[16,4096]{1,0:T(8,128)}, f32[16,4096]{1,0:T(8,128)}) fusion(bf16[16,4096]{1,0:T(8,128)(2,1)S(1)} %collective-permute-done.2, pred[]{:T(512)S(6)} %eq.17, pred[]{:T(512)S(6)} %eq.16, bf16[48,4096]{1,0:T(8,128)(2,1)S(1)} %collective-permute-done.1, bf16[48,4096]{1,0:T(8,128)(2,1)} %get-tuple-element.24, f32[4096]{0:T(1024)S(1)} %convert_reduce_fusion.1, ...), kind=kLoop, calls=%fused_computation.10 | loop fusion | flops 1310720 | bytes 1474562 | tf_op jit(solution)/shard_map/jit(_where)/select_n | solution.py:309
  37.2 28.0 %shard_map.162 = (bf16[128,4096]{1,0:T(8,128)(2,1)}, bf16[3,4096]{1,0:T(4,128)(2,1)}, f32[16,4096]{1,0:T(8,128)}, f32[16,128]{1,0:T(8,128)}, f32[16,128]{1,0:T(8,128)}, /*index=5*/f32[24,4096]{1,0:T(8,128)}) custom-call(f32[16,4096]{1,0:T(8,128)} %get-tuple-element.41.si_ref, f32[16,4096]{1,0:T(8,128)} %get-tuple-element.40.ai_ref, ...), custom_call_target="tpu_custom_call" | custom-call | flops 167772160 | bytes 12582912 | tf_op jit(solution)/shard_map/pallas_call | solution.py:372
  65.3 1.0 %constant_dynamic-slice_fusion.1 = f32[24,2048]{1,0:T(8,128)S(1)} fusion(f32[24,4096]{1,0:T(8,128)} %get-tuple-element.39, s32[]{:T(128)S(6)} %select_n.134), kind=kLoop, calls=%fused_computation.42 | loop fusion | bytes 393220 | tf_op jit(solution)/shard_map/dynamic_slice | solution.py:279
  66.4 1.4 %collective-permute-done.4 = f32[24,2048]{1,0:T(8,128)S(1)} collective-permute-done((f32[24,2048]{1,0:T(8,128)S(1)}, f32[24,2048]{1,0:T(8,128)S(1)}, u32[]{:S(2)}, u32[]{:S(2)}) %collective-permute-start.4) | collective-permute-done | bytes 196640 | tf_op jit(solution)/shard_map/ppermute | solution.py:267
  67.8 0.9 dynamic-slice_add_fusion
  68.7 1.8 %collective-permute-start.5 = (f32[24,1024]{1,0:T(8,128)S(1)}, f32[24,1024]{1,0:T(8,128)S(1)}, u32[]{:S(2)}, u32[]{:S(2)}) collective-permute-start(f32[24,1024]{1,0:T(8,128)S(1)} %constant_dynamic-slice_fusion), channel_id=1, source_target_pairs={{0,2},{1,3},{2,0},{3,1},{4,6},{5,7},{6,4},{7,5},{8,10},{9,11},{10,... | collective-permute-start | bytes 294920 | tf_op jit(solution)/shard_map/ppermute | solution.py:267
  70.5 3.1 %collective-permute-done.5 = f32[24,1024]{1,0:T(8,128)S(1)} collective-permute-done((f32[24,1024]{1,0:T(8,128)S(1)}, f32[24,1024]{1,0:T(8,128)S(1)}, u32[]{:S(2)}, u32[]{:S(2)}) %collective-permute-start.5) | collective-permute-done | bytes 98336 | tf_op jit(solution)/shard_map/ppermute | solution.py:267
  73.7 1.6 %collective-permute-start.6 = (f32[24,1024]{1,0:T(8,128)S(1)}, f32[24,1024]{1,0:T(8,128)S(1)}, u32[]{:S(2)}, u32[]{:S(2)}) collective-permute-start(f32[24,1024]{1,0:T(8,128)S(1)} %dynamic-slice_add_fusion.1), channel_id=1, source_target_pairs={{0,4},{4,0},{8,12},{12,8},{16,20},{20,16},{24,28},{28,24},{1,5},{5... | collective-permute-start | bytes 294920 | tf_op jit(solution)/shard_map/ppermute | solution.py:267
  75.2 3.1 %collective-permute-done.6 = f32[24,1024]{1,0:T(8,128)S(1)} collective-permute-done((f32[24,1024]{1,0:T(8,128)S(1)}, f32[24,1024]{1,0:T(8,128)S(1)}, u32[]{:S(2)}, u32[]{:S(2)}) %collective-permute-start.6) | collective-permute-done | bytes 98336 | tf_op jit(solution)/shard_map/ppermute | solution.py:267
  78.4 1.6 %collective-permute-start.7 = (f32[24,1024]{1,0:T(8,128)S(1)}, f32[24,1024]{1,0:T(8,128)S(1)}, u32[]{:S(2)}, u32[]{:S(2)}) collective-permute-start(f32[24,1024]{1,0:T(8,128)S(1)} %add.69), channel_id=1, source_target_pairs={{0,8},{4,12},{8,0},{12,4},{16,24},{20,28},{24,16},{28,20},{1,9},{5... | collective-permute-start | bytes 294920 | tf_op jit(solution)/shard_map/ppermute | solution.py:267
  80.0 3.0 %collective-permute-done.7 = f32[24,1024]{1,0:T(8,128)S(1)} collective-permute-done((f32[24,1024]{1,0:T(8,128)S(1)}, f32[24,1024]{1,0:T(8,128)S(1)}, u32[]{:S(2)}, u32[]{:S(2)}) %collective-permute-start.7) | collective-permute-done | bytes 98336 | tf_op jit(solution)/shard_map/ppermute | solution.py:267
  83.1 3.1 %collective-permute-start.8 = (f32[24,1024]{1,0:T(8,128)S(1)}, f32[24,1024]{1,0:T(8,128)S(1)}, u32[]{:S(2)}, u32[]{:S(2)}) collective-permute-start(f32[24,1024]{1,0:T(8,128)S(1)} %add.70), channel_id=1, source_target_pairs={{0,16},{4,20},{8,24},{12,28},{16,0},{20,4},{24,8},{28,12},{1,17},{... | collective-permute-start | bytes 294920 | tf_op jit(solution)/shard_map/ppermute | solution.py:267
  86.2 3.6 %collective-permute-done.8 = f32[24,1024]{1,0:T(8,128)S(1)} collective-permute-done((f32[24,1024]{1,0:T(8,128)S(1)}, f32[24,1024]{1,0:T(8,128)S(1)}, u32[]{:S(2)}, u32[]{:S(2)}) %collective-permute-start.8) | collective-permute-done | bytes 98336 | tf_op jit(solution)/shard_map/ppermute | solution.py:267
  89.8 1.8 %collective-permute-start.9 = (f32[24,1024]{1,0:T(8,128)S(1)}, f32[24,1024]{1,0:T(8,128)S(1)}, u32[]{:S(2)}, u32[]{:S(2)}) collective-permute-start(f32[24,1024]{1,0:T(8,128)S(1)} %add.71), channel_id=1, source_target_pairs={{0,2},{1,3},{2,0},{3,1},{4,6},{5,7},{6,4},{7,5},{8,10},{9,11},{10,... | collective-permute-start | bytes 294920 | tf_op jit(solution)/shard_map/ppermute | solution.py:267
  91.7 1.3 %collective-permute-start.3 = (bf16[3,4096]{1,0:T(4,128)(2,1)S(1)}, bf16[3,4096]{1,0:T(4,128)(2,1)S(1)}, u32[]{:S(2)}, u32[]{:S(2)}) collective-permute-start(bf16[3,4096]{1,0:T(4,128)(2,1)S(1)} %copy-done.2), channel_id=1, source_target_pairs={{1,0},{2,1},{3,2},{5,4},{6,5},{7,6},{9,8},{10,9},{11,10},{13,12},{... | collective-permute-start | bytes 73736 | tf_op jit(solution)/shard_map/ppermute | solution.py:411
  92.9 1.6 %collective-permute-done.9 = f32[24,1024]{1,0:T(8,128)S(1)} collective-permute-done((f32[24,1024]{1,0:T(8,128)S(1)}, f32[24,1024]{1,0:T(8,128)S(1)}, u32[]{:S(2)}, u32[]{:S(2)}) %collective-permute-start.9) | collective-permute-done | bytes 98336 | tf_op jit(solution)/shard_map/ppermute | solution.py:267
  94.8 0.7 fusion.14
  95.4 0.6 collective-permute-done.10
  96.1 0.7 fusion.10
  96.8 0.7 pad_maximum_fusion.2
  97.5 0.6 pad_maximum_fusion.1
  (19 shorter events, 0.4 us)
Async XLA Ops:
  1.5 3.2 %collective-permute-start = (bf16[3,4096]{1,0:T(4,128)(2,1)S(1)}, bf16[3,4096]{1,0:T(4,128)(2,1)S(1)}, u32[]{:S(2)}, u32[]{:S(2)}) collective-permute-start(bf16[3,4096]{1,0:T(4,128)(2,1)S(1)} %slice_bitcast_fusion), channel_id=1, source_target_pairs={{0,1},{1,2},{2,3},{4,5},{5,6},{6,7},{8,9},{9,10},{10,11},{12,13},{... | collective-permute-start | bytes 73736 | tf_op jit(solution)/shard_map/ppermute | solution.py:402
  4.7 0.6 copy-start.3
  5.3 22.3 %copy-start = (f32[16,4096]{1,0:T(8,128)S(1)}, f32[16,4096]{1,0:T(8,128)}, u32[]{:S(2)}) copy-start(f32[16,4096]{1,0:T(8,128)} %dl_ref.3) | copy-start | bytes 786436
  23.1 4.4 %collective-permute-start.1 = (bf16[48,4096]{1,0:T(8,128)(2,1)}, bf16[48,4096]{1,0:T(8,128)(2,1)S(1)}, u32[]{:S(2)}, u32[]{:S(2)}) collective-permute-start(bf16[48,4096]{1,0:T(8,128)(2,1)} %get-tuple-element.24), channel_id=1, source_target_pairs={{0,1},{1,0},{2,3},{3,2},{4,5},{5,4},{6,7},{7,6},{8,9},{9,8},{10,11... | collective-permute-start | bytes 1179656 | tf_op jit(solution)/shard_map/ppermute | solution.py:267
  28.8 6.4 %collective-permute-start.2 = (bf16[16,4096]{1,0:T(8,128)(2,1)S(1)}, bf16[16,4096]{1,0:T(8,128)(2,1)S(1)}, u32[]{:S(2)}, u32[]{:S(2)}) collective-permute-start(bf16[16,4096]{1,0:T(8,128)(2,1)S(1)} %fusion.8), channel_id=1, source_target_pairs={{0,2},{1,3},{2,0},{3,1},{4,6},{5,7},{6,4},{7,5},{8,10},{9,11},{10,... | collective-permute-start | bytes 393224 | tf_op jit(solution)/shard_map/ppermute | solution.py:267
  65.2 26.4 %copy-start.2 = (bf16[3,4096]{1,0:T(4,128)(2,1)S(1)}, bf16[3,4096]{1,0:T(4,128)(2,1)}, u32[]{:S(2)}) copy-start(bf16[3,4096]{1,0:T(4,128)(2,1)} %get-tuple-element.36) | copy-start | bytes 73732
  65.3 29.5 %copy-start.1 = (f32[16,4096]{1,0:T(8,128)S(1)}, f32[16,4096]{1,0:T(8,128)}, u32[]{:S(2)}) copy-start(f32[16,4096]{1,0:T(8,128)} %get-tuple-element.35) | copy-start | bytes 786436
  66.3 1.5 %collective-permute-start.4 = (f32[24,2048]{1,0:T(8,128)S(1)}, f32[24,2048]{1,0:T(8,128)S(1)}, u32[]{:S(2)}, u32[]{:S(2)}) collective-permute-start(f32[24,2048]{1,0:T(8,128)S(1)} %constant_dynamic-slice_fusion.1), channel_id=1, source_target_pairs={{0,1},{1,0},{2,3},{3,2},{4,5},{5,4},{6,7},{7,6},{8,9},{9,8},{10,11... | collective-permute-start | bytes 589832 | tf_op jit(solution)/shard_map/ppermute | solution.py:267
  68.7 4.9 %collective-permute-start.5 = (f32[24,1024]{1,0:T(8,128)S(1)}, f32[24,1024]{1,0:T(8,128)S(1)}, u32[]{:S(2)}, u32[]{:S(2)}) collective-permute-start(f32[24,1024]{1,0:T(8,128)S(1)} %constant_dynamic-slice_fusion), channel_id=1, source_target_pairs={{0,2},{1,3},{2,0},{3,1},{4,6},{5,7},{6,4},{7,5},{8,10},{9,11},{10,... | collective-permute-start | bytes 294920 | tf_op jit(solution)/shard_map/ppermute | solution.py:267
  73.7 4.7 %collective-permute-start.6 = (f32[24,1024]{1,0:T(8,128)S(1)}, f32[24,1024]{1,0:T(8,128)S(1)}, u32[]{:S(2)}, u32[]{:S(2)}) collective-permute-start(f32[24,1024]{1,0:T(8,128)S(1)} %dynamic-slice_add_fusion.1), channel_id=1, source_target_pairs={{0,4},{4,0},{8,12},{12,8},{16,20},{20,16},{24,28},{28,24},{1,5},{5... | collective-permute-start | bytes 294920 | tf_op jit(solution)/shard_map/ppermute | solution.py:267
  78.4 4.7 %collective-permute-start.7 = (f32[24,1024]{1,0:T(8,128)S(1)}, f32[24,1024]{1,0:T(8,128)S(1)}, u32[]{:S(2)}, u32[]{:S(2)}) collective-permute-start(f32[24,1024]{1,0:T(8,128)S(1)} %add.69), channel_id=1, source_target_pairs={{0,8},{4,12},{8,0},{12,4},{16,24},{20,28},{24,16},{28,20},{1,9},{5... | collective-permute-start | bytes 294920 | tf_op jit(solution)/shard_map/ppermute | solution.py:267
  83.1 6.8 %collective-permute-start.8 = (f32[24,1024]{1,0:T(8,128)S(1)}, f32[24,1024]{1,0:T(8,128)S(1)}, u32[]{:S(2)}, u32[]{:S(2)}) collective-permute-start(f32[24,1024]{1,0:T(8,128)S(1)} %add.70), channel_id=1, source_target_pairs={{0,16},{4,20},{8,24},{12,28},{16,0},{20,4},{24,8},{28,12},{1,17},{... | collective-permute-start | bytes 294920 | tf_op jit(solution)/shard_map/ppermute | solution.py:267
  89.8 4.7 %collective-permute-start.9 = (f32[24,1024]{1,0:T(8,128)S(1)}, f32[24,1024]{1,0:T(8,128)S(1)}, u32[]{:S(2)}, u32[]{:S(2)}) collective-permute-start(f32[24,1024]{1,0:T(8,128)S(1)} %add.71), channel_id=1, source_target_pairs={{0,2},{1,3},{2,0},{3,1},{4,6},{5,7},{6,4},{7,5},{8,10},{9,11},{10,... | collective-permute-start | bytes 294920 | tf_op jit(solution)/shard_map/ppermute | solution.py:267
  91.7 3.1 %collective-permute-start.3 = (bf16[3,4096]{1,0:T(4,128)(2,1)S(1)}, bf16[3,4096]{1,0:T(4,128)(2,1)S(1)}, u32[]{:S(2)}, u32[]{:S(2)}) collective-permute-start(bf16[3,4096]{1,0:T(4,128)(2,1)S(1)} %copy-done.2), channel_id=1, source_target_pairs={{1,0},{2,1},{3,2},{5,4},{6,5},{7,6},{9,8},{10,9},{11,10},{13,12},{... | collective-permute-start | bytes 73736 | tf_op jit(solution)/shard_map/ppermute | solution.py:411
  94.6 1.5 %collective-permute-start.10 = (f32[24,2048]{1,0:T(8,128)S(1)}, f32[24,2048]{1,0:T(8,128)S(1)}, u32[]{:S(2)}, u32[]{:S(2)}) collective-permute-start(f32[24,2048]{1,0:T(8,128)S(1)} %pad_maximum_fusion), channel_id=1, source_target_pairs={{0,1},{1,0},{2,3},{3,2},{4,5},{5,4},{6,7},{7,6},{8,9},{9,8},{10,11... | collective-permute-start | bytes 589832 | tf_op jit(solution)/shard_map/ppermute | solution.py:267

commit v3 on v2

--- a/solution.py
+++ b/solution.py
@@ -1,4 +1,5 @@
 import math
+from functools import partial
 
 import jax
 import jax.numpy as jnp
@@ -13,6 +14,7 @@
 BLOCK = 16
 LANES = 128
 WIDTH = 512
+ENDS_WIDTH = 1024
 VMEM = 60 * 1024 * 1024
 
 
@@ -65,26 +67,66 @@
     bd_ref[...] = jnp.where(t % BLOCK == m // states, spread, 0.0).astype(BF16)
 
 
-def ends_kernel(x_ref, rim_ref, step_ref, dy_ref, b_ref, c_ref, cw_ref, cb_ref, sb_ref, dl_ref,
-                out_ref, dls, dus, u_ref, sig_ref, slope_ref, dub_ref, bw_ref, cw2_ref, bd_ref,
-                xe, dyf, rates):
+def low_parts(value):
+    high = value.astype(BF16)
+    return high, (value - high.astype(F32)).astype(BF16)
+
+
+def summed_over(mask, value):
+    high, low = low_parts(value)
+    mask = jnp.where(mask, 1.0, 0.0).astype(BF16)
+    return jnp.dot(mask, high, preferred_element_type=F32) + jnp.dot(mask, low, preferred_element_type=F32)
+
+
+def set_diagonals(proj_ref, diag):
+    states, length = proj_ref.shape
+    n = lax.broadcasted_iota(jnp.int32, (BLOCK, BLOCK * states), 0)
+    m = lax.broadcasted_iota(jnp.int32, (BLOCK, BLOCK * states), 1)
+    repeat = jnp.where(n == m // states, 1.0, 0.0).astype(BF16)
+    n = lax.broadcasted_iota(jnp.int32, (states, BLOCK * states), 0)
+    m = lax.broadcasted_iota(jnp.int32, (states, BLOCK * states), 1)
+    for b in range(length // BLOCK):
+        columns = proj_ref[:, b * BLOCK : (b + 1) * BLOCK].astype(BF16)
+        spread = jnp.dot(columns, repeat, preferred_element_type=F32)
+        diag[b] = jnp.where(n == m % states, spread, 0.0).astype(BF16)
+
+
+def decayed_sum(exponents, weights, diag, rates, width):
+    blocks, states = diag.shape[0], diag.shape[1]
+    tiles = width // LANES
+    total = [jnp.zeros((states, 2 * LANES), F32) for _ in range(0, tiles, 2)]
+    for b in range(blocks):
+        for m in range(len(total)):
+            columns = []
+            for j in (2 * m, 2 * m + 1):
+                terms = []
+                for i in range(BLOCK):
+                    t = b * BLOCK + i
+                    decay = jnp.exp2(row_of(exponents, t, j).astype(BF16) * rates[j])
+                    terms.append(decay * row_of(weights, t, j).astype(BF16))
+                columns.append(jnp.concatenate(terms, axis=0))
+            total[m] = total[m] + jnp.dot(diag[b], jnp.concatenate(columns, axis=1), preferred_element_type=F32)
+    return jnp.concatenate(total, axis=1)
+
+
+def ends_kernel(late_ref, x_ref, rim_ref, step_ref, dy_ref, b_ref, c_ref, cw_ref, cb_ref, sb_ref, dl_ref,
+                ends_ref, far_ref, dls, sig_ref, dus, u_ref, slope_ref, dub_ref,
+                xe, dyf, upto, after, b_diag, c_diag, rates):
     length, width = x_ref.shape
-    states = dl_ref.shape[0]
-    taps = cw_ref.shape[0]
-    blocks = length // BLOCK
+    states, taps = dl_ref.shape[0], cw_ref.shape[0]
     weights = [cw_ref[k : k + 1, :] for k in range(taps)]
     bias, shift = cb_ref[...], sb_ref[...]
-    slices = lane_slices(width)
 
     @pl.when(pl.program_id(0) == 0)
     def _():
-        widen(b_ref, c_ref, bw_ref, cw2_ref, bd_ref)
-
-    set_rates(dl_ref, rates)
+        set_diagonals(b_ref, b_diag)
+        set_diagonals(c_ref, c_diag)
+
+    for j, s in enumerate(lane_slices(width)):
+        rates[j] = (-jnp.exp(dl_ref[:, s]) * LOG2E).astype(BF16)
     xe[0:8, :] = jnp.zeros((8, width), F32)
     xe[8 - (taps - 1) : 8, :] = rim_ref[...].astype(F32)
-    total = jnp.zeros((8, width), F32)
-    for b in range(blocks):
+    for b in range(length // BLOCK):
         rows = slice(b * BLOCK, (b + 1) * BLOCK)
         xe[8 + b * BLOCK : 8 + (b + 1) * BLOCK, :] = x_ref[rows, :].astype(F32)
         put(dyf, rows, dy_ref[rows, :].astype(F32))
@@ -100,46 +142,56 @@
         du = delta * u
         put(dls, rows, delta)
         put(dus, rows, du)
+        sig_ref[rows, :] = z / (1.0 + z)
         u_ref[rows, :] = u
-        sig_ref[rows, :] = z / (1.0 + z)
         slope_ref[rows, :] = gate + u * (1.0 - gate)
         dub_ref[rows, :] = du.astype(BF16)
-        total = total + row_sum(delta)
-    total = jnp.sum(total, axis=0, keepdims=True)
-
-    def block(b, carry):
-        state, decay, adjoint = (list(part) for part in carry)
-        base = pl.multiple_of(b * BLOCK, BLOCK)
-        for i in range(BLOCK):
-            t = base + i
-            rows = pl.ds(pl.multiple_of(t * states, states), states)
-            b_column, c_column = bw_ref[rows, :], cw2_ref[rows, :]
-            for j in range(len(slices)):
-                a = jnp.exp2(row_of(dls, t, j) * rates[j])
-                state[j] = a * state[j] + b_column * row_of(dus, t, j)
-                decay[j] = decay[j] * a
-                adjoint[j] = adjoint[j] + decay[j] * (c_column * row_of(dyf, t, j))
-        return tuple(state), tuple(decay), tuple(adjoint)
-
-    zero = tuple(jnp.zeros((states, LANES), F32) for _ in slices)
-    one = tuple(jnp.ones((states, LANES), F32) for _ in slices)
-    state, _, adjoint = lax.fori_loop(0, blocks, block, (zero, one, zero), unroll=blocks)
-    for j, s in enumerate(slices):
-        out_ref[0:states, s] = state[j].astype(BF16)
-        out_ref[states : 2 * states, s] = adjoint[j].astype(BF16)
+    t = lax.broadcasted_iota(jnp.int32, (length, length), 0)
+    r = lax.broadcasted_iota(jnp.int32, (length, length), 1)
+    for j in range(width // LANES):
+        upto[j] = summed_over(r <= t, dls[j])
+        after[j] = summed_over(r > t, dls[j])
+    adjoint = decayed_sum(upto, dyf, c_diag, rates, width)
+    state = decayed_sum(after, dus, b_diag, rates, width)
+    total = take(after, slice(0, 1)) + take(dls, slice(0, 1))
     high = total.astype(BF16)
-    rest = total - high.astype(F32)
-    middle = rest.astype(BF16)
-    low = (rest - middle.astype(F32)).astype(BF16)
+    middle = (total - high.astype(F32)).astype(BF16)
+    low = (total - high.astype(F32) - middle.astype(F32)).astype(BF16)
     row = lax.broadcasted_iota(jnp.int32, (16, width), 0)
     packed = jnp.where(row == 0, high.astype(F32), jnp.where(row == 1, middle.astype(F32), low.astype(F32)))
-    out_ref[2 * states : 2 * states + 16, :] = packed.astype(BF16)
-
-
-def main_kernel(si_ref, ai_ref, x_ref, rim_ref, dy_ref, dls, dus, u_ref, sig_ref, slope_ref, dub_ref,
-                bb_ref, cb2_ref, bd_ref, cw_ref, dl_ref, sk_ref,
-                gin_ref, borrow_ref, tail_ref, gb_ref, gc_ref, pg_ref,
-                xe, dyf, ahs, hb, dpe, rates, naturals):
+    packed = packed.astype(BF16)
+    ends_ref[0:states, :] = state.astype(BF16)
+    ends_ref[states : 2 * states, :] = adjoint.astype(BF16)
+    ends_ref[2 * states : 2 * states + 16, :] = packed
+    far_ref[0:states, :] = jnp.where(late_ref[0] == 1, adjoint, state).astype(BF16)
+    far_ref[states : states + 16, :] = packed
+
+
+def joined(place_ref, sib_ref, far_ref, far_sib_ref, rate, s):
+    late, upper = place_ref[0] >= 2, place_ref[0] % 2 == 1
+    states = rate.shape[0]
+
+    def decay(ref, first):
+        parts = ref[first : first + 16, s].astype(F32)
+        return jnp.exp2(rate * (parts[0:1] + parts[1:2] + parts[2:3]))
+
+    pieces = [(ref[0:states, s].astype(F32), decay(ref, states)) for ref in (far_ref, far_sib_ref)]
+    first = [jnp.where(upper, b, a) for a, b in zip(*pieces)]
+    second = [jnp.where(upper, a, b) for a, b in zip(*pieces)]
+    far = jnp.where(late, second[1] * first[0] + second[0], first[0] + first[1] * second[0])
+    step = decay(sib_ref, 2 * states) * far
+    sib_state, sib_adjoint = sib_ref[0:states, s].astype(F32), sib_ref[states : 2 * states, s].astype(F32)
+    state = jnp.where(late, far, 0.0)
+    state = jnp.where(upper, sib_state + jnp.where(late, step, 0.0), state)
+    adjoint = jnp.where(late, 0.0, far)
+    adjoint = jnp.where(upper, adjoint, sib_adjoint + jnp.where(late, 0.0, step))
+    return state, adjoint
+
+
+def main_kernel(entering, place_ref, *refs):
+    (x_ref, rim_ref, dy_ref, dls, sig_ref, dus, u_ref, slope_ref, dub_ref, b_ref, c_ref, cw_ref, dl_ref, sk_ref,
+     gin_ref, borrow_ref, tail_ref, gb_ref, gc_ref, pg_ref,
+     xe, dyf, ahs, hb, dpe, rates, naturals, bb_ref, cb2_ref, bd_ref, back) = refs[entering:]
     length, width = x_ref.shape
     states = dl_ref.shape[0]
     taps = cw_ref.shape[0]
@@ -152,6 +204,7 @@
     def _():
         gb_ref[...] = jnp.zeros_like(gb_ref)
         gc_ref[...] = jnp.zeros_like(gc_ref)
+        widen(b_ref, c_ref, bb_ref, cb2_ref, bd_ref)
 
     set_rates(dl_ref, rates)
     for j, s in enumerate(slices):
@@ -172,7 +225,13 @@
             table = jnp.where(lane == b * BLOCK + i, product[i * states : (i + 1) * states], table)
         return table
 
-    state = [si_ref[:, s] for s in slices]
+    if entering == 2:
+        state, adjoint = ([ref[:, s] for s in slices] for ref in refs[:2])
+    else:
+        state, adjoint = zip(*(joined(place_ref, *refs[:3], rates[j], s) for j, s in enumerate(slices)))
+        state, adjoint = list(state), list(adjoint)
+    for j in tiles:
+        back[j] = adjoint[j]
     gc = jnp.zeros((states, length), F32)
     for b in range(blocks):
         for i in range(BLOCK):
@@ -195,7 +254,7 @@
     cols_of = lax.broadcasted_iota(jnp.int32, (states, BLOCK * states), 1)
     over_steps = jnp.where(rows_of == cols_of % states, 1.0, 0.0).astype(BF16)
 
-    adjoint = [ai_ref[:, s] for s in slices]
+    adjoint = [back[j] for j in tiles]
     gb = jnp.zeros((states, length), F32)
     rates_sum = [jnp.zeros((states, 2 * LANES), F32) for _ in range(0, len(slices), 2)]
     sums = [jnp.zeros((8, width), F32) for _ in range(taps + 3)]
@@ -288,47 +347,34 @@
     return value
 
 
-def entering(ends, decay_log):
+def entering(ends, far, decay_log):
     states = decay_log.shape[0]
     count, place = lax.axis_size("ctx"), lax.axis_index("ctx")
+    if count == 4:
+        far = flipped(far, "ctx", 2)
+        return flipped(ends, "ctx", 1), far, flipped(far, "ctx", 1)
     rate = -jnp.exp(decay_log)
-
-    def opened(piece):
-        total = jnp.sum(piece[2 * states : 2 * states + 3].astype(F32), axis=0, keepdims=True)
-        return piece[:states].astype(F32), piece[states : 2 * states].astype(F32), jnp.exp(rate * total)
-
-    if count == 4:
-        upper, late = place % 2 == 1, place // 2 == 1
-        mine, other = opened(ends), opened(flipped(ends, "ctx", 1))
-        pick = lambda a, b: jnp.where(upper, a, b)
-        first, second = [pick(b, a) for a, b in zip(mine, other)], [pick(a, b) for a, b in zip(mine, other)]
-        both = jnp.where(late, second[1] * first[2] + first[1], first[0] * second[2] + second[0])
-        got = flipped(both.astype(BF16), "ctx", 2).astype(F32)
-        before, after = jnp.where(late, got, 0.0), jnp.where(late, 0.0, got)
-        state = jnp.where(upper, before * first[2] + first[0], before)
-        adjoint = jnp.where(upper, after, after * second[2] + second[1])
-        return state, adjoint
-    gathered = lax.all_gather(ends, "ctx")
+    gathered = lax.all_gather(ends, "ctx").astype(F32)
+    total = gathered[:, 2 * states] + gathered[:, 2 * states + 1] + gathered[:, 2 * states + 2]
+    decay = jnp.exp(rate[None] * total[:, None, :])
     state = adjoint = jnp.zeros(decay_log.shape, F32)
     for k in range(count - 1):
-        end, _, decay = opened(gathered[k])
-        state = jnp.where(k < place, decay * state + end, state)
+        state = jnp.where(k < place, decay[k] * state + gathered[k, :states], state)
     for k in range(count - 1, 0, -1):
-        _, end, decay = opened(gathered[k])
-        adjoint = jnp.where(k > place, decay * adjoint + end, adjoint)
+        adjoint = jnp.where(k > place, decay[k] * adjoint + gathered[k, states : 2 * states], adjoint)
     return state, adjoint
 
 
 def whole(a):
-    return pl.BlockSpec(a.shape, lambda i: (0,) * a.ndim)
+    return pl.BlockSpec(a.shape, lambda i, *_: (0,) * a.ndim)
 
 
 def chunk(rows):
-    return pl.BlockSpec((rows, WIDTH), lambda i: (0, i))
+    return pl.BlockSpec((rows, WIDTH), lambda i, *_: (0, i))
 
 
 def tiled(length):
-    return pl.BlockSpec((WIDTH // LANES, length, LANES), lambda i: (i, 0, 0))
+    return pl.BlockSpec((WIDTH // LANES, length, LANES), lambda i, *_: (i, 0, 0))
 
 
 def flat(a):
@@ -339,54 +385,66 @@
 PARAMS = pltpu.CompilerParams(vmem_limit_bytes=VMEM, dimension_semantics=("arbitrary",))
 
 
-def call_ends(x, rims, step, dy, b_proj, c_proj, conv_weight, conv_bias, step_bias, decay_log):
+def call_ends(late, x, rims, step, dy, b_proj, c_proj, conv_weight, conv_bias, step_bias, decay_log):
+    (length, channels), states = x.shape, decay_log.shape[0]
+    taps, rim = conv_weight.shape[0], rims.shape[0]
+    work = length * states * channels
+    tiles = ENDS_WIDTH // LANES
+    plain = SHAPE((length, channels), F32)
+    long = SHAPE((channels // LANES, length, LANES), F32)
+    chunk = lambda rows: pl.BlockSpec((rows, ENDS_WIDTH), lambda i, *_: (0, i))
+    tiled = pl.BlockSpec((tiles, length, LANES), lambda i, *_: (i, 0, 0))
+    diag = pltpu.VMEM((length // BLOCK, states, BLOCK * states), BF16)
+    return pl.pallas_call(
+        ends_kernel,
+        grid_spec=pltpu.PrefetchScalarGridSpec(
+            num_scalar_prefetch=1,
+            grid=(channels // ENDS_WIDTH,),
+            in_specs=[chunk(length), chunk(rim), chunk(length), chunk(length), whole(b_proj), whole(c_proj),
+                      chunk(taps), chunk(1), chunk(1), chunk(states)],
+            out_specs=[chunk(2 * states + 16), chunk(states + 16), tiled, chunk(length), tiled] + [chunk(length)] * 3,
+            scratch_shapes=[pltpu.VMEM((length + 16, ENDS_WIDTH), F32)] + [pltpu.VMEM((tiles, length, LANES), F32)] * 3
+            + [diag, diag, pltpu.VMEM((tiles, states, LANES), BF16)],
+        ),
+        out_shape=[SHAPE((2 * states + 16, channels), BF16), SHAPE((states + 16, channels), BF16), long, plain, long,
+                   plain, plain, SHAPE((length, channels), BF16)],
+        compiler_params=PARAMS,
+        cost_estimate=pl.CostEstimate(flops=8 * work, bytes_accessed=30 * length * channels, transcendentals=work),
+    )(late, x, rims, step, dy, b_proj, c_proj, conv_weight, flat(conv_bias), flat(step_bias), decay_log)
+
+
+def call_main(place, entering, x, rims, dy, saved, b_proj, c_proj, conv_weight, decay_log, skip_weight):
     (length, channels), states = x.shape, decay_log.shape[0]
     taps, rim = conv_weight.shape[0], rims.shape[0]
     work = length * states * channels
     tiles = WIDTH // LANES
-    long = SHAPE((channels // LANES, length, LANES), F32)
-    plain = SHAPE((length, channels), F32)
-    spread = [SHAPE((length * states, LANES), F32)] * 2 + [SHAPE((length, BLOCK * states), BF16)]
+    summed = pl.BlockSpec((states, length), lambda i, *_: (0, 0))
     return pl.pallas_call(
-        ends_kernel,
-        grid=(channels // WIDTH,),
-        in_specs=[chunk(length), chunk(rim), chunk(length), chunk(length), whole(b_proj), whole(c_proj),
-                  chunk(taps), chunk(1), chunk(1), chunk(states)],
-        out_specs=[chunk(2 * states + 16)] + [tiled(length)] * 2 + [chunk(length)] * 4 + [whole(a) for a in spread],
-        out_shape=[SHAPE((2 * states + 16, channels), BF16), long, long, plain, plain, plain,
-                   SHAPE((length, channels), BF16)] + spread,
-        scratch_shapes=[pltpu.VMEM((length + 16, WIDTH), F32),
-                        pltpu.VMEM((tiles, length, LANES), F32),
-                        pltpu.VMEM((tiles, states, LANES), F32)],
-        compiler_params=PARAMS,
-        cost_estimate=pl.CostEstimate(flops=8 * work, bytes_accessed=20 * length * channels, transcendentals=work),
-    )(x, rims, step, dy, b_proj, c_proj, conv_weight, flat(conv_bias), flat(step_bias), decay_log)
-
-
-def call_main(state_in, adjoint_in, x, rims, dy, saved, conv_weight, decay_log, skip_weight):
-    (length, channels), states = x.shape, decay_log.shape[0]
-    taps, rim = conv_weight.shape[0], rims.shape[0]
-    work = length * states * channels
-    tiles = WIDTH // LANES
-    summed = pl.BlockSpec((states, length), lambda i: (0, 0))
-    return pl.pallas_call(
-        main_kernel,
-        grid=(channels // WIDTH,),
-        in_specs=[chunk(states), chunk(states), chunk(length), chunk(rim), chunk(length)] + [tiled(length)] * 2
-        + [chunk(length)] * 4 + [whole(a) for a in saved[6:]] + [chunk(taps), chunk(states), chunk(1)],
-        out_specs=[chunk(length), chunk(rim), chunk(BLOCK), summed, summed, chunk(states + 8)],
+        partial(main_kernel, len(entering)),
+        grid_spec=pltpu.PrefetchScalarGridSpec(
+            num_scalar_prefetch=1,
+            grid=(channels // WIDTH,),
+            in_specs=[chunk(a.shape[0]) for a in entering] + [chunk(length), chunk(rim), chunk(length), tiled(length),
+                      chunk(length), tiled(length)] + [chunk(length)] * 3 + [whole(b_proj), whole(c_proj), chunk(taps),
+                      chunk(states), chunk(1)],
+            out_specs=[chunk(length), chunk(rim), chunk(BLOCK), summed, summed, chunk(states + 8)],
+            scratch_shapes=[pltpu.VMEM((length + 16, WIDTH), F32),
+                            pltpu.VMEM((tiles, length, LANES), F32),
+                            pltpu.VMEM((tiles, length * states, LANES), BF16),
+                            pltpu.VMEM((2, tiles, BLOCK * states, LANES), BF16),
+                            pltpu.VMEM((length + 16, WIDTH), F32),
+                            pltpu.VMEM((tiles, states, LANES), F32),
+                            pltpu.VMEM((tiles, states, LANES), BF16),
+                            pltpu.VMEM((length * states, LANES), F32),
+                            pltpu.VMEM((length * states, LANES), F32),
+                            pltpu.VMEM((length, BLOCK * states), BF16),
+                            pltpu.VMEM((tiles, states, LANES), F32)],
+        ),
         out_shape=[SHAPE((length, channels), BF16), SHAPE((rim, channels), BF16), SHAPE((BLOCK, channels), F32),
                    SHAPE((states, length), F32), SHAPE((states, length), F32), SHAPE((states + 8, channels), F32)],
-        scratch_shapes=[pltpu.VMEM((length + 16, WIDTH), F32),
-                        pltpu.VMEM((tiles, length, LANES), F32),
-                        pltpu.VMEM((tiles, length * states, LANES), BF16),
-                        pltpu.VMEM((2, tiles, BLOCK * states, LANES), BF16),
-                        pltpu.VMEM((length + 16, WIDTH), F32),
-                        pltpu.VMEM((tiles, states, LANES), F32),
-                        pltpu.VMEM((tiles, states, LANES), BF16)],
         compiler_params=PARAMS,
         cost_estimate=pl.CostEstimate(flops=20 * work, bytes_accessed=24 * length * channels, transcendentals=2 * work),
-    )(state_in, adjoint_in, x, rims, dy, *saved, conv_weight, decay_log, flat(skip_weight))
+    )(place, *entering, x, rims, dy, *saved, b_proj, c_proj, conv_weight, decay_log, flat(skip_weight))
 
 
 def per_device(scan_input, step_raw, input_proj, output_proj, out_cotangent, conv_weight, conv_bias, step_bias,
@@ -395,14 +453,17 @@
     states, taps = decay_log.shape[0], conv_weight.shape[0]
     rim = taps - 1
     count = lax.axis_size("ctx")
+    place = lax.axis_index("ctx").astype(jnp.int32).reshape(1)
+    late = (place >= count // 2).astype(jnp.int32)
     forth = [(k, k + 1) for k in range(count - 1)]
     back = [(k + 1, k) for k in range(count - 1)]
 
     def one(x, step, b_proj, c_proj, dy):
         rims = lax.ppermute(x[length - rim :, :], "ctx", forth)
-        ends, *saved = call_ends(x, rims, step, dy, b_proj, c_proj, conv_weight, conv_bias, step_bias, decay_log)
-        state_in, adjoint_in = entering(ends, decay_log)
-        return call_main(state_in, adjoint_in, x, rims, dy, saved, conv_weight, decay_log, skip_weight)
+        ends, far, *saved = call_ends(late, x, rims, step, dy, b_proj, c_proj, conv_weight, conv_bias, step_bias,
+                                      decay_log)
+        return call_main(place, entering(ends, far, decay_log), x, rims, dy, saved, b_proj, c_proj,
+                         conv_weight, decay_log, skip_weight)
 
     outs = []
     for d in range(documents):

time: 98.5 us -> 97.7 us (level)
  waiting for transfers between devices: 21.9 us -> 27.9 us
  other arithmetic: 7.84 us -> 3.76 us
  starting transfers between devices: 19.2 us -> 16.2 us
    ppermute x9 -> x10, waiting for transfers between devices: 21 us -> 27 us  [flipped(): lax.ppermute(value, axis, [(k, k ^ bit) for k in range(lax.axis_size(axis...]
    ppermute x9 -> x10, starting transfers between devices: 15.6 us -> 12.5 us  [flipped(): lax.ppermute(value, axis, [(k, k ^ bit) for k in range(lax.axis_size(axis...]
    select_n x1 -> x0, other arithmetic: 1.97 us -> none  [entering(): adjoint = jnp.where(upper, after, after * second[2] + second[1])]
    convert_element_type x1 -> x0, other arithmetic: 1.19 us -> none  [entering(): got = flipped(both.astype(BF16), 'ctx', 2).astype(F32)]
  transfers between devices with their start and end apart: 11 -> 12, of which waited for: 11 -> 10; matrix products, arithmetic and copies ran while one was open for 2% -> 1% of each run, Pallas kernels for 0% -> 0%
where the time goes in v3:
time: 97.7 us; the launch traced here: 97.4 us
  Pallas kernels  45.7 us (47%)
  waiting for transfers between devices  27.9 us (29%)
  starting transfers between devices  16.2 us (17%)
  other arithmetic  3.76 us (4%)
  local copies, waits for them, and re-layouts  3.2 us (3%)
    pallas_call x1, Pallas kernels, call_main(): pl.pallas_call(partial(main_kernel, len(entering)), grid_spec=pltpu.Prefe...  28.2 us
    ppermute x10, waiting for transfers between devices, flipped(): lax.ppermute(value, axis, [(k, k ^ bit) for k in range(lax.axis_size(axis...  27 us
    pallas_call x1, Pallas kernels, call_ends(): pl.pallas_call(ends_kernel, grid_spec=pltpu.PrefetchScalarGridSpec(num_sc...  17.5 us
    ppermute x10, starting transfers between devices, flipped(): lax.ppermute(value, axis, [(k, k ^ bit) for k in range(lax.axis_size(axis...  12.5 us
    ppermute x1, starting transfers between devices, one(): rims = lax.ppermute(x[length - rim:, :], 'ctx', forth)  2.36 us
  transfers between devices with their start and end apart: 12, of which 10 were waited for; matrix products, arithmetic and copies ran while one was open for 1% of the time, Pallas kernels for 0%

profile of v3, /device:TPU:0, one launch (start us, length us, event | category | flops | bytes accessed | tf_op | source)
XLA Modules:
  0.0 97.4 jit_solution(12279358769947977310)
XLA Ops:
  0.6 0.9 slice_bitcast_fusion
  1.5 2.4 %collective-permute-start = (bf16[3,4096]{1,0:T(4,128)(2,1)S(1)}, bf16[3,4096]{1,0:T(4,128)(2,1)S(1)}, u32[]{:S(2)}, u32[]{:S(2)}) collective-permute-start(bf16[3,4096]{1,0:T(4,128)(2,1)S(1)} %slice_bitcast_fusion), channel_id=1, source_target_pairs={{0,1},{1,2},{2,3},{4,5},{5,6},{6,7},{8,9},{9,10},{10,11},{12,13},{... | collective-permute-start | bytes 73736 | tf_op jit(solution)/shard_map/ppermute | solution.py:462
  3.9 0.8 collective-permute-done.rim_ref.refs_4_
  4.7 0.6 copy-done.5
  5.3 17.5 %shard_map.161 = (bf16[48,4096]{1,0:T(8,128)(2,1)}, bf16[32,4096]{1,0:T(8,128)(2,1)}, f32[32,128,128]{2,1,0:T(8,128)}, f32[128,4096]{1,0:T(8,128)}, f32[32,128,1...) custom-call(s32[1]{0:T(128)S(6)} %convert_element_type.9.late_ref, ...), custom_call_target="tpu_custom_call" | custom-call | flops 67108864 | bytes 15728640 | tf_op jit(solution)/shard_map/pallas_call | solution.py:398
  22.8 5.1 %collective-permute-start.2 = (bf16[32,4096]{1,0:T(8,128)(2,1)}, bf16[32,4096]{1,0:T(8,128)(2,1)S(1)}, u32[]{:S(2)}, u32[]{:S(2)}) collective-permute-start(bf16[32,4096]{1,0:T(8,128)(2,1)} %get-tuple-element.23), channel_id=1, source_target_pairs={{0,2},{1,3},{2,0},{3,1},{4,6},{5,7},{6,4},{7,5},{8,10},{9,11},{10,... | collective-permute-start | bytes 786440 | tf_op jit(solution)/shard_map/ppermute | solution.py:326
  27.9 6.2 %collective-permute-done.2.refs_1_ = bf16[32,4096]{1,0:T(8,128)(2,1)S(1)} collective-permute-done((bf16[32,4096]{1,0:T(8,128)(2,1)}, bf16[32,4096]{1,0:T(8,128)(2,1)S(1)}, u32[]{:S(2)}, u32[]{:S(2)}) %collective-permute-start.2) | collective-permute-done | bytes 262176 | tf_op jit(solution)/shard_map/ppermute | solution.py:326
  34.1 1.5 %collective-permute-done.3.refs_2_ = bf16[32,4096]{1,0:T(8,128)(2,1)S(1)} collective-permute-done((bf16[32,4096]{1,0:T(8,128)(2,1)S(1)}, bf16[32,4096]{1,0:T(8,128)(2,1)S(1)}, u32[]{:S(2)}, u32[]{:S(2)}) %collective-permute-start.3) | collective-permute-done | bytes 262176 | tf_op jit(solution)/shard_map/ppermute | solution.py:326
  35.6 0.7 copy-done.3
  36.3 28.2 %shard_map.162 = (bf16[128,4096]{1,0:T(8,128)(2,1)}, bf16[3,4096]{1,0:T(4,128)(2,1)}, f32[16,4096]{1,0:T(8,128)}, f32[16,128]{1,0:T(8,128)}, f32[16,128]{1,0:T(8,128)}, /*index=5*/f32[24,4096]{1,0:T(8,128)}) custom-call(s32[1]{0:T(128)} %bitcast.place_ref, bf16[48,4096]{1,0:T(8,128)(2,1)} %copy-done.1, bf16[32,4096]{1,0:T(8,128)(2,1)} %copy-done.2, ...), custom_call_target="tpu_custom_call" | custom-call | flops 167772160 | bytes 12582912 | tf_op jit(solution)/shard_map/pallas_call | solution.py:422
  64.6 1.0 %constant_dynamic-slice_fusion.1 = f32[24,2048]{1,0:T(8,128)S(1)} fusion(f32[24,4096]{1,0:T(8,128)} %get-tuple-element.35, s32[]{:T(128)S(6)} %select_n.64), kind=kLoop, calls=%fused_computation.19 | loop fusion | bytes 393220 | tf_op jit(solution)/shard_map/dynamic_slice | solution.py:338
  65.6 0.2 collective-permute-start.5
  65.8 1.3 %collective-permute-done.5 = f32[24,2048]{1,0:T(8,128)S(1)} collective-permute-done((f32[24,2048]{1,0:T(8,128)S(1)}, f32[24,2048]{1,0:T(8,128)S(1)}, u32[]{:S(2)}, u32[]{:S(2)}) %collective-permute-start.5) | collective-permute-done | bytes 196640 | tf_op jit(solution)/shard_map/ppermute | solution.py:326
  67.1 0.9 dynamic-slice_add_fusion
  68.0 0.4 collective-permute-start.6
  68.5 4.5 %collective-permute-done.6 = f32[24,1024]{1,0:T(8,128)S(1)} collective-permute-done((f32[24,1024]{1,0:T(8,128)S(1)}, f32[24,1024]{1,0:T(8,128)S(1)}, u32[]{:S(2)}, u32[]{:S(2)}) %collective-permute-start.6) | collective-permute-done | bytes 98336 | tf_op jit(solution)/shard_map/ppermute | solution.py:326
  73.0 1.6 %collective-permute-start.7 = (f32[24,1024]{1,0:T(8,128)S(1)}, f32[24,1024]{1,0:T(8,128)S(1)}, u32[]{:S(2)}, u32[]{:S(2)}) collective-permute-start(f32[24,1024]{1,0:T(8,128)S(1)} %dynamic-slice_add_fusion.1), channel_id=1, source_target_pairs={{0,4},{4,0},{8,12},{12,8},{16,20},{20,16},{24,28},{28,24},{1,5},{5... | collective-permute-start | bytes 294920 | tf_op jit(solution)/shard_map/ppermute | solution.py:326
  74.5 3.1 %collective-permute-done.7 = f32[24,1024]{1,0:T(8,128)S(1)} collective-permute-done((f32[24,1024]{1,0:T(8,128)S(1)}, f32[24,1024]{1,0:T(8,128)S(1)}, u32[]{:S(2)}, u32[]{:S(2)}) %collective-permute-start.7) | collective-permute-done | bytes 98336 | tf_op jit(solution)/shard_map/ppermute | solution.py:326
  77.7 1.6 %collective-permute-start.8 = (f32[24,1024]{1,0:T(8,128)S(1)}, f32[24,1024]{1,0:T(8,128)S(1)}, u32[]{:S(2)}, u32[]{:S(2)}) collective-permute-start(f32[24,1024]{1,0:T(8,128)S(1)} %add.52), channel_id=1, source_target_pairs={{0,8},{4,12},{8,0},{12,4},{16,24},{20,28},{24,16},{28,20},{1,9},{5... | collective-permute-start | bytes 294920 | tf_op jit(solution)/shard_map/ppermute | solution.py:326
  79.3 3.0 %collective-permute-done.8 = f32[24,1024]{1,0:T(8,128)S(1)} collective-permute-done((f32[24,1024]{1,0:T(8,128)S(1)}, f32[24,1024]{1,0:T(8,128)S(1)}, u32[]{:S(2)}, u32[]{:S(2)}) %collective-permute-start.8) | collective-permute-done | bytes 98336 | tf_op jit(solution)/shard_map/ppermute | solution.py:326
  82.4 3.1 %collective-permute-start.9 = (f32[24,1024]{1,0:T(8,128)S(1)}, f32[24,1024]{1,0:T(8,128)S(1)}, u32[]{:S(2)}, u32[]{:S(2)}) collective-permute-start(f32[24,1024]{1,0:T(8,128)S(1)} %add.53), channel_id=1, source_target_pairs={{0,16},{4,20},{8,24},{12,28},{16,0},{20,4},{24,8},{28,12},{1,17},{... | collective-permute-start | bytes 294920 | tf_op jit(solution)/shard_map/ppermute | solution.py:326
  85.5 3.6 %collective-permute-done.9 = f32[24,1024]{1,0:T(8,128)S(1)} collective-permute-done((f32[24,1024]{1,0:T(8,128)S(1)}, f32[24,1024]{1,0:T(8,128)S(1)}, u32[]{:S(2)}, u32[]{:S(2)}) %collective-permute-start.9) | collective-permute-done | bytes 98336 | tf_op jit(solution)/shard_map/ppermute | solution.py:326
  89.2 0.4 collective-permute-start.10
  89.6 1.3 %collective-permute-start.4 = (bf16[3,4096]{1,0:T(4,128)(2,1)S(1)}, bf16[3,4096]{1,0:T(4,128)(2,1)S(1)}, u32[]{:S(2)}, u32[]{:S(2)}) collective-permute-start(bf16[3,4096]{1,0:T(4,128)(2,1)S(1)} %copy-done.4), channel_id=1, source_target_pairs={{1,0},{2,1},{3,2},{5,4},{6,5},{7,6},{9,8},{10,9},{11,10},{13,12},{... | collective-permute-start | bytes 73736 | tf_op jit(solution)/shard_map/ppermute | solution.py:472
  90.9 3.0 %collective-permute-done.10 = f32[24,1024]{1,0:T(8,128)S(1)} collective-permute-done((f32[24,1024]{1,0:T(8,128)S(1)}, f32[24,1024]{1,0:T(8,128)S(1)}, u32[]{:S(2)}, u32[]{:S(2)}) %collective-permute-start.10) | collective-permute-done | bytes 98336 | tf_op jit(solution)/shard_map/ppermute | solution.py:326
  93.9 0.1 collective-permute-start.11
  94.0 0.0 collective-permute-done.4
  94.0 0.7 fusion.2
  94.7 0.7 collective-permute-done.11
  95.4 0.7 fusion
  96.2 0.7 pad_maximum_fusion.2
  96.8 0.6 pad_maximum_fusion.1
  (21 shorter events, 0.2 us)
Async XLA Ops:
  1.5 3.2 %collective-permute-start = (bf16[3,4096]{1,0:T(4,128)(2,1)S(1)}, bf16[3,4096]{1,0:T(4,128)(2,1)S(1)}, u32[]{:S(2)}, u32[]{:S(2)}) collective-permute-start(bf16[3,4096]{1,0:T(4,128)(2,1)S(1)} %slice_bitcast_fusion), channel_id=1, source_target_pairs={{0,1},{1,2},{2,3},{4,5},{5,6},{6,7},{8,9},{9,10},{10,11},{12,13},{... | collective-permute-start | bytes 73736 | tf_op jit(solution)/shard_map/ppermute | solution.py:462
  4.7 0.6 copy-start.5
  22.8 11.3 %collective-permute-start.2 = (bf16[32,4096]{1,0:T(8,128)(2,1)}, bf16[32,4096]{1,0:T(8,128)(2,1)S(1)}, u32[]{:S(2)}, u32[]{:S(2)}) collective-permute-start(bf16[32,4096]{1,0:T(8,128)(2,1)} %get-tuple-element.23), channel_id=1, source_target_pairs={{0,2},{1,3},{2,0},{3,1},{4,6},{5,7},{6,4},{7,5},{8,10},{9,11},{10,... | collective-permute-start | bytes 786440 | tf_op jit(solution)/shard_map/ppermute | solution.py:326
  27.9 6.2 %collective-permute-start.1 = (bf16[48,4096]{1,0:T(8,128)(2,1)}, bf16[48,4096]{1,0:T(8,128)(2,1)S(1)}, u32[]{:S(2)}, u32[]{:S(2)}) collective-permute-start(bf16[48,4096]{1,0:T(8,128)(2,1)} %get-tuple-element.22), channel_id=1, source_target_pairs={{0,1},{1,0},{2,3},{3,2},{4,5},{5,4},{6,7},{7,6},{8,9},{9,8},{10,11... | collective-permute-start | bytes 1179656 | tf_op jit(solution)/shard_map/ppermute | solution.py:326
  34.1 1.5 %copy-start.2 = (bf16[32,4096]{1,0:T(8,128)(2,1)}, bf16[32,4096]{1,0:T(8,128)(2,1)S(1)}, u32[]{:S(2)}) copy-start(bf16[32,4096]{1,0:T(8,128)(2,1)S(1)} %collective-permute-done.2.refs_1_) | copy-start | bytes 786436
  34.1 1.5 %collective-permute-start.3 = (bf16[32,4096]{1,0:T(8,128)(2,1)S(1)}, bf16[32,4096]{1,0:T(8,128)(2,1)S(1)}, u32[]{:S(2)}, u32[]{:S(2)}) collective-permute-start(bf16[32,4096]{1,0:T(8,128)(2,1)S(1)} %collective-permute-done.2.refs_1_), channel_id=1, source_target_pairs={{0,1},{1,0},{2,3},{3,2},{4,5},{5,4},{6,7},{7,6},{8,9},{9,8},{10,11... | collective-permute-start | bytes 786440 | tf_op jit(solution)/shard_map/ppermute | solution.py:326
  34.1 1.5 %copy-start.1 = (bf16[48,4096]{1,0:T(8,128)(2,1)}, bf16[48,4096]{1,0:T(8,128)(2,1)S(1)}, u32[]{:S(2)}) copy-start(bf16[48,4096]{1,0:T(8,128)(2,1)S(1)} %collective-permute-done.1.refs_0_) | copy-start | bytes 1179652
  35.6 0.7 copy-start.3
  64.5 25.0 %copy-start.4 = (bf16[3,4096]{1,0:T(4,128)(2,1)S(1)}, bf16[3,4096]{1,0:T(4,128)(2,1)}, u32[]{:S(2)}) copy-start(bf16[3,4096]{1,0:T(4,128)(2,1)} %get-tuple-element.32) | copy-start | bytes 73732
  64.6 29.4 %copy-start = (f32[16,4096]{1,0:T(8,128)S(1)}, f32[16,4096]{1,0:T(8,128)}, u32[]{:S(2)}) copy-start(f32[16,4096]{1,0:T(8,128)} %get-tuple-element.31) | copy-start | bytes 786436
  65.6 1.5 %collective-permute-start.5 = (f32[24,2048]{1,0:T(8,128)S(1)}, f32[24,2048]{1,0:T(8,128)S(1)}, u32[]{:S(2)}, u32[]{:S(2)}) collective-permute-start(f32[24,2048]{1,0:T(8,128)S(1)} %constant_dynamic-slice_fusion.1), channel_id=1, source_target_pairs={{0,1},{1,0},{2,3},{3,2},{4,5},{5,4},{6,7},{7,6},{8,9},{9,8},{10,11... | collective-permute-start | bytes 589832 | tf_op jit(solution)/shard_map/ppermute | solution.py:326
  68.0 4.9 %collective-permute-start.6 = (f32[24,1024]{1,0:T(8,128)S(1)}, f32[24,1024]{1,0:T(8,128)S(1)}, u32[]{:S(2)}, u32[]{:S(2)}) collective-permute-start(f32[24,1024]{1,0:T(8,128)S(1)} %constant_dynamic-slice_fusion), channel_id=1, source_target_pairs={{0,2},{1,3},{2,0},{3,1},{4,6},{5,7},{6,4},{7,5},{8,10},{9,11},{10,... | collective-permute-start | bytes 294920 | tf_op jit(solution)/shard_map/ppermute | solution.py:326
  73.0 4.7 %collective-permute-start.7 = (f32[24,1024]{1,0:T(8,128)S(1)}, f32[24,1024]{1,0:T(8,128)S(1)}, u32[]{:S(2)}, u32[]{:S(2)}) collective-permute-start(f32[24,1024]{1,0:T(8,128)S(1)} %dynamic-slice_add_fusion.1), channel_id=1, source_target_pairs={{0,4},{4,0},{8,12},{12,8},{16,20},{20,16},{24,28},{28,24},{1,5},{5... | collective-permute-start | bytes 294920 | tf_op jit(solution)/shard_map/ppermute | solution.py:326
  77.7 4.7 %collective-permute-start.8 = (f32[24,1024]{1,0:T(8,128)S(1)}, f32[24,1024]{1,0:T(8,128)S(1)}, u32[]{:S(2)}, u32[]{:S(2)}) collective-permute-start(f32[24,1024]{1,0:T(8,128)S(1)} %add.52), channel_id=1, source_target_pairs={{0,8},{4,12},{8,0},{12,4},{16,24},{20,28},{24,16},{28,20},{1,9},{5... | collective-permute-start | bytes 294920 | tf_op jit(solution)/shard_map/ppermute | solution.py:326
  82.4 6.8 %collective-permute-start.9 = (f32[24,1024]{1,0:T(8,128)S(1)}, f32[24,1024]{1,0:T(8,128)S(1)}, u32[]{:S(2)}, u32[]{:S(2)}) collective-permute-start(f32[24,1024]{1,0:T(8,128)S(1)} %add.53), channel_id=1, source_target_pairs={{0,16},{4,20},{8,24},{12,28},{16,0},{20,4},{24,8},{28,12},{1,17},{... | collective-permute-start | bytes 294920 | tf_op jit(solution)/shard_map/ppermute | solution.py:326
  89.2 4.7 %collective-permute-start.10 = (f32[24,1024]{1,0:T(8,128)S(1)}, f32[24,1024]{1,0:T(8,128)S(1)}, u32[]{:S(2)}, u32[]{:S(2)}) collective-permute-start(f32[24,1024]{1,0:T(8,128)S(1)} %add.54), channel_id=1, source_target_pairs={{0,2},{1,3},{2,0},{3,1},{4,6},{5,7},{6,4},{7,5},{8,10},{9,11},{10,... | collective-permute-start | bytes 294920 | tf_op jit(solution)/shard_map/ppermute | solution.py:326
  89.6 4.4 %collective-permute-start.4 = (bf16[3,4096]{1,0:T(4,128)(2,1)S(1)}, bf16[3,4096]{1,0:T(4,128)(2,1)S(1)}, u32[]{:S(2)}, u32[]{:S(2)}) collective-permute-start(bf16[3,4096]{1,0:T(4,128)(2,1)S(1)} %copy-done.4), channel_id=1, source_target_pairs={{1,0},{2,1},{3,2},{5,4},{6,5},{7,6},{9,8},{10,9},{11,10},{13,12},{... | collective-permute-start | bytes 73736 | tf_op jit(solution)/shard_map/ppermute | solution.py:472
  93.9 1.5 %collective-permute-start.11 = (f32[24,2048]{1,0:T(8,128)S(1)}, f32[24,2048]{1,0:T(8,128)S(1)}, u32[]{:S(2)}, u32[]{:S(2)}) collective-permute-start(f32[24,2048]{1,0:T(8,128)S(1)} %pad_maximum_fusion), channel_id=1, source_target_pairs={{0,1},{1,0},{2,3},{3,2},{4,5},{5,4},{6,7},{7,6},{8,9},{9,8},{10,11... | collective-permute-start | bytes 589832 | tf_op jit(solution)/shard_map/ppermute | solution.py:326

commit v4 on v3

--- a/solution.py
+++ b/solution.py
@@ -67,17 +67,6 @@
     bd_ref[...] = jnp.where(t % BLOCK == m // states, spread, 0.0).astype(BF16)
 
 
-def low_parts(value):
-    high = value.astype(BF16)
-    return high, (value - high.astype(F32)).astype(BF16)
-
-
-def summed_over(mask, value):
-    high, low = low_parts(value)
-    mask = jnp.where(mask, 1.0, 0.0).astype(BF16)
-    return jnp.dot(mask, high, preferred_element_type=F32) + jnp.dot(mask, low, preferred_element_type=F32)
-
-
 def set_diagonals(proj_ref, diag):
     states, length = proj_ref.shape
     n = lax.broadcasted_iota(jnp.int32, (BLOCK, BLOCK * states), 0)
@@ -91,27 +80,31 @@
         diag[b] = jnp.where(n == m % states, spread, 0.0).astype(BF16)
 
 
-def decayed_sum(exponents, weights, diag, rates, width):
-    blocks, states = diag.shape[0], diag.shape[1]
-    tiles = width // LANES
-    total = [jnp.zeros((states, 2 * LANES), F32) for _ in range(0, tiles, 2)]
+def piece_ends(steps, inputs, outputs, b_wide, c_diag, rates, width):
+    blocks, states = c_diag.shape[0], c_diag.shape[1]
+    tiles = range(width // LANES)
+    state = [jnp.zeros((states, LANES), F32) for _ in tiles]
+    decay = [jnp.ones((states, LANES), F32) for _ in tiles]
+    adjoint = [jnp.zeros((states, 2 * LANES), F32) for _ in tiles[::2]]
     for b in range(blocks):
-        for m in range(len(total)):
-            columns = []
-            for j in (2 * m, 2 * m + 1):
-                terms = []
-                for i in range(BLOCK):
-                    t = b * BLOCK + i
-                    decay = jnp.exp2(row_of(exponents, t, j).astype(BF16) * rates[j])
-                    terms.append(decay * row_of(weights, t, j).astype(BF16))
-                columns.append(jnp.concatenate(terms, axis=0))
-            total[m] = total[m] + jnp.dot(diag[b], jnp.concatenate(columns, axis=1), preferred_element_type=F32)
-    return jnp.concatenate(total, axis=1)
-
-
-def ends_kernel(late_ref, x_ref, rim_ref, step_ref, dy_ref, b_ref, c_ref, cw_ref, cb_ref, sb_ref, dl_ref,
-                ends_ref, far_ref, dls, sig_ref, dus, u_ref, slope_ref, dub_ref,
-                xe, dyf, upto, after, b_diag, c_diag, rates):
+        terms = [[] for _ in tiles]
+        for i in range(BLOCK):
+            t = b * BLOCK + i
+            column = b_wide[t * states : (t + 1) * states, :]
+            for j in tiles:
+                a = jnp.exp2(row_of(steps, t, j) * rates[j])
+                state[j] = a * state[j] + column * row_of(inputs, t, j)
+                decay[j] = decay[j] * a
+                terms[j].append((decay[j] * row_of(outputs, t, j)).astype(BF16))
+        for m in range(len(adjoint)):
+            pair = [jnp.concatenate(terms[j], axis=0) for j in (2 * m, 2 * m + 1)]
+            adjoint[m] = adjoint[m] + jnp.dot(c_diag[b], jnp.concatenate(pair, axis=1), preferred_element_type=F32)
+    return jnp.concatenate(state, axis=1), jnp.concatenate(adjoint, axis=1)
+
+
+def ends_kernel(x_ref, rim_ref, step_ref, dy_ref, b_ref, c_ref, cw_ref, cb_ref, sb_ref, dl_ref,
+                ends_ref, dls, sig_ref, dus, u_ref, slope_ref, dub_ref,
+                xe, dyf, b_wide, c_diag, rates):
     length, width = x_ref.shape
     states, taps = dl_ref.shape[0], cw_ref.shape[0]
     weights = [cw_ref[k : k + 1, :] for k in range(taps)]
@@ -119,11 +112,12 @@
 
     @pl.when(pl.program_id(0) == 0)
     def _():
-        set_diagonals(b_ref, b_diag)
+        for t in range(length):
+            b_wide[t * states : (t + 1) * states, :] = jnp.broadcast_to(b_ref[:, t : t + 1], (states, LANES))
         set_diagonals(c_ref, c_diag)
 
-    for j, s in enumerate(lane_slices(width)):
-        rates[j] = (-jnp.exp(dl_ref[:, s]) * LOG2E).astype(BF16)
+    set_rates(dl_ref, rates)
+    total = jnp.zeros((8, width), F32)
     xe[0:8, :] = jnp.zeros((8, width), F32)
     xe[8 - (taps - 1) : 8, :] = rim_ref[...].astype(F32)
     for b in range(length // BLOCK):
@@ -146,40 +140,25 @@
         u_ref[rows, :] = u
         slope_ref[rows, :] = gate + u * (1.0 - gate)
         dub_ref[rows, :] = du.astype(BF16)
-    t = lax.broadcasted_iota(jnp.int32, (length, length), 0)
-    r = lax.broadcasted_iota(jnp.int32, (length, length), 1)
-    for j in range(width // LANES):
-        upto[j] = summed_over(r <= t, dls[j])
-        after[j] = summed_over(r > t, dls[j])
-    adjoint = decayed_sum(upto, dyf, c_diag, rates, width)
-    state = decayed_sum(after, dus, b_diag, rates, width)
-    total = take(after, slice(0, 1)) + take(dls, slice(0, 1))
+        total = total + row_sum(delta)
+    state, adjoint = piece_ends(dls, dus, dyf, b_wide, c_diag, rates, width)
+    total = jnp.sum(total, axis=0, keepdims=True)
     high = total.astype(BF16)
     middle = (total - high.astype(F32)).astype(BF16)
     low = (total - high.astype(F32) - middle.astype(F32)).astype(BF16)
     row = lax.broadcasted_iota(jnp.int32, (16, width), 0)
     packed = jnp.where(row == 0, high.astype(F32), jnp.where(row == 1, middle.astype(F32), low.astype(F32)))
-    packed = packed.astype(BF16)
     ends_ref[0:states, :] = state.astype(BF16)
     ends_ref[states : 2 * states, :] = adjoint.astype(BF16)
-    ends_ref[2 * states : 2 * states + 16, :] = packed
-    far_ref[0:states, :] = jnp.where(late_ref[0] == 1, adjoint, state).astype(BF16)
-    far_ref[states : states + 16, :] = packed
-
-
-def joined(place_ref, sib_ref, far_ref, far_sib_ref, rate, s):
+    ends_ref[2 * states : 2 * states + 16, :] = packed.astype(BF16)
+
+
+def joined(place_ref, sib_ref, far_ref, rate, s):
     late, upper = place_ref[0] >= 2, place_ref[0] % 2 == 1
     states = rate.shape[0]
-
-    def decay(ref, first):
-        parts = ref[first : first + 16, s].astype(F32)
-        return jnp.exp2(rate * (parts[0:1] + parts[1:2] + parts[2:3]))
-
-    pieces = [(ref[0:states, s].astype(F32), decay(ref, states)) for ref in (far_ref, far_sib_ref)]
-    first = [jnp.where(upper, b, a) for a, b in zip(*pieces)]
-    second = [jnp.where(upper, a, b) for a, b in zip(*pieces)]
-    far = jnp.where(late, second[1] * first[0] + second[0], first[0] + first[1] * second[0])
-    step = decay(sib_ref, 2 * states) * far
+    far = far_ref[:, s].astype(F32)
+    parts = sib_ref[2 * states : 2 * states + 16, s].astype(F32)
+    step = jnp.exp2(rate * (parts[0:1] + parts[1:2] + parts[2:3])) * far
     sib_state, sib_adjoint = sib_ref[0:states, s].astype(F32), sib_ref[states : 2 * states, s].astype(F32)
     state = jnp.where(late, far, 0.0)
     state = jnp.where(upper, sib_state + jnp.where(late, step, 0.0), state)
@@ -188,10 +167,10 @@
     return state, adjoint
 
 
-def main_kernel(entering, place_ref, *refs):
+def main_kernel(direct, place_ref, *refs):
     (x_ref, rim_ref, dy_ref, dls, sig_ref, dus, u_ref, slope_ref, dub_ref, b_ref, c_ref, cw_ref, dl_ref, sk_ref,
-     gin_ref, borrow_ref, tail_ref, gb_ref, gc_ref, pg_ref,
-     xe, dyf, ahs, hb, dpe, rates, naturals, bb_ref, cb2_ref, bd_ref, back) = refs[entering:]
+     gin_ref, borrow_ref, tail_ref, gb_ref, gc_ref, give_ref, keep_ref,
+     xe, dyf, ahs, hb, dpe, rates, naturals, bb_ref, cb2_ref, bd_ref, back) = refs[2:]
     length, width = x_ref.shape
     states = dl_ref.shape[0]
     taps = cw_ref.shape[0]
@@ -225,10 +204,10 @@
             table = jnp.where(lane == b * BLOCK + i, product[i * states : (i + 1) * states], table)
         return table
 
-    if entering == 2:
+    if direct:
         state, adjoint = ([ref[:, s] for s in slices] for ref in refs[:2])
     else:
-        state, adjoint = zip(*(joined(place_ref, *refs[:3], rates[j], s) for j, s in enumerate(slices)))
+        state, adjoint = zip(*(joined(place_ref, *refs[:2], rates[j], s) for j, s in enumerate(slices)))
         state, adjoint = list(state), list(adjoint)
     for j in tiles:
         back[j] = adjoint[j]
@@ -309,8 +288,6 @@
             tail_ref[...] = grad_x
     gb_ref[...] += gb
     rates_sum = jnp.concatenate(rates_sum, axis=1)
-    for j, s in enumerate(slices):
-        pg_ref[0:states, s] = rates_sum[:, s] * (-jnp.exp(dl_ref[:, s]))
     grad_rim = weights[0] * dpe[taps - 1 : taps + 7, :]
     for k in range(1, taps):
         grad_rim = grad_rim + weights[k] * dpe[taps - 1 - k : taps + 7 - k, :]
@@ -319,19 +296,35 @@
     packed = jnp.zeros((8, width), F32)
     for k in range(taps + 3):
         packed = jnp.where(row == k, jnp.sum(sums[k], axis=0, keepdims=True), packed)
-    pg_ref[states : states + 8, :] = packed
+    step, turns = pl.program_id(0), pl.num_programs(0)
+
+    def give_out(out_ref):
+        for j, s in enumerate(slices):
+            out_ref[0:states, s] = rates_sum[:, s] * (-jnp.exp(dl_ref[:, s]))
+        out_ref[states : states + 8, :] = packed
+
+    @pl.when(step < turns // 2)
+    def _():
+        give_out(give_ref)
+
+    @pl.when(step >= turns // 2)
+    def _():
+        give_out(keep_ref)
 
 
 def flipped(value, axis, bit):
     return lax.ppermute(value, axis, [(k, k ^ bit) for k in range(lax.axis_size(axis))])
 
 
-def add_up(value):
+def add_up(give, keep):
     inner, outer = lax.axis_size("ctx"), lax.axis_size("dp")
-    if inner & (inner - 1) or outer & (outer - 1):
-        return lax.psum(value, ("dp", "ctx"))
     me = lax.axis_index("ctx")
-    bits = [1 << k for k in range(inner.bit_length() - 1)]
+    if inner & (inner - 1) or outer & (outer - 1) or inner == 1:
+        upper = me % 2 == 1
+        lower_half, upper_half = jnp.where(upper, give, keep), jnp.where(upper, keep, give)
+        return lax.psum(jnp.concatenate([lower_half, upper_half], axis=1), ("dp", "ctx"))
+    value = keep + flipped(give, "ctx", 1)
+    bits = [1 << k for k in range(1, inner.bit_length() - 1)]
     for bit in bits:
         half = value.shape[1] // 2
         upper = (me // bit) % 2
@@ -340,19 +333,27 @@
         value = lax.dynamic_slice_in_dim(value, upper * half, half, 1) + got
     for k in range(outer.bit_length() - 1):
         value = value + flipped(value, "dp", 1 << k)
-    for bit in reversed(bits):
+    for bit in [*reversed(bits), 1]:
         got = flipped(value, "ctx", bit)
         upper = (me // bit) % 2 == 1
         value = jnp.concatenate([jnp.where(upper, got, value), jnp.where(upper, value, got)], axis=1)
     return value
 
 
-def entering(ends, far, decay_log):
+def entering(ends, decay_log):
     states = decay_log.shape[0]
     count, place = lax.axis_size("ctx"), lax.axis_index("ctx")
     if count == 4:
-        far = flipped(far, "ctx", 2)
-        return flipped(ends, "ctx", 1), far, flipped(far, "ctx", 1)
+        late, upper = place >= 2, place % 2 == 1
+        sib = flipped(ends, "ctx", 1)
+        mine, other = ends.astype(F32), sib.astype(F32)
+        passing = jnp.where(late == upper, other, mine)
+        onto = jnp.where(late == upper, mine, other)
+        if_early = lambda piece: jnp.where(late, piece[states : 2 * states], piece[:states])
+        total = passing[2 * states : 2 * states + 1] + passing[2 * states + 1 : 2 * states + 2]
+        total = total + passing[2 * states + 2 : 2 * states + 3]
+        both = jnp.exp(-jnp.exp(decay_log) * total) * if_early(onto) + if_early(passing)
+        return sib, flipped(both.astype(BF16), "ctx", 2)
     rate = -jnp.exp(decay_log)
     gathered = lax.all_gather(ends, "ctx").astype(F32)
     total = gathered[:, 2 * states] + gathered[:, 2 * states + 1] + gathered[:, 2 * states + 2]
@@ -369,14 +370,6 @@
     return pl.BlockSpec(a.shape, lambda i, *_: (0,) * a.ndim)
 
 
-def chunk(rows):
-    return pl.BlockSpec((rows, WIDTH), lambda i, *_: (0, i))
-
-
-def tiled(length):
-    return pl.BlockSpec((WIDTH // LANES, length, LANES), lambda i, *_: (i, 0, 0))
-
-
 def flat(a):
     return a.reshape(1, a.shape[0])
 
@@ -385,7 +378,7 @@
 PARAMS = pltpu.CompilerParams(vmem_limit_bytes=VMEM, dimension_semantics=("arbitrary",))
 
 
-def call_ends(late, x, rims, step, dy, b_proj, c_proj, conv_weight, conv_bias, step_bias, decay_log):
+def call_ends(x, rims, step, dy, b_proj, c_proj, conv_weight, conv_bias, step_bias, decay_log):
     (length, channels), states = x.shape, decay_log.shape[0]
     taps, rim = conv_weight.shape[0], rims.shape[0]
     work = length * states * channels
@@ -394,23 +387,21 @@
     long = SHAPE((channels // LANES, length, LANES), F32)
     chunk = lambda rows: pl.BlockSpec((rows, ENDS_WIDTH), lambda i, *_: (0, i))
     tiled = pl.BlockSpec((tiles, length, LANES), lambda i, *_: (i, 0, 0))
-    diag = pltpu.VMEM((length // BLOCK, states, BLOCK * states), BF16)
     return pl.pallas_call(
         ends_kernel,
-        grid_spec=pltpu.PrefetchScalarGridSpec(
-            num_scalar_prefetch=1,
-            grid=(channels // ENDS_WIDTH,),
-            in_specs=[chunk(length), chunk(rim), chunk(length), chunk(length), whole(b_proj), whole(c_proj),
-                      chunk(taps), chunk(1), chunk(1), chunk(states)],
-            out_specs=[chunk(2 * states + 16), chunk(states + 16), tiled, chunk(length), tiled] + [chunk(length)] * 3,
-            scratch_shapes=[pltpu.VMEM((length + 16, ENDS_WIDTH), F32)] + [pltpu.VMEM((tiles, length, LANES), F32)] * 3
-            + [diag, diag, pltpu.VMEM((tiles, states, LANES), BF16)],
-        ),
-        out_shape=[SHAPE((2 * states + 16, channels), BF16), SHAPE((states + 16, channels), BF16), long, plain, long,
-                   plain, plain, SHAPE((length, channels), BF16)],
+        grid=(channels // ENDS_WIDTH,),
+        in_specs=[chunk(length), chunk(rim), chunk(length), chunk(length), whole(b_proj), whole(c_proj), chunk(taps),
+                  chunk(1), chunk(1), chunk(states)],
+        out_specs=[chunk(2 * states + 16), tiled, chunk(length), tiled] + [chunk(length)] * 3,
+        scratch_shapes=[pltpu.VMEM((length + 16, ENDS_WIDTH), F32), pltpu.VMEM((tiles, length, LANES), F32),
+                        pltpu.VMEM((length * states, LANES), F32),
+                        pltpu.VMEM((length // BLOCK, states, BLOCK * states), BF16),
+                        pltpu.VMEM((tiles, states, LANES), F32)],
+        out_shape=[SHAPE((2 * states + 16, channels), BF16), long, plain, long, plain, plain,
+                   SHAPE((length, channels), BF16)],
         compiler_params=PARAMS,
         cost_estimate=pl.CostEstimate(flops=8 * work, bytes_accessed=30 * length * channels, transcendentals=work),
-    )(late, x, rims, step, dy, b_proj, c_proj, conv_weight, flat(conv_bias), flat(step_bias), decay_log)
+    )(x, rims, step, dy, b_proj, c_proj, conv_weight, flat(conv_bias), flat(step_bias), decay_log)
 
 
 def call_main(place, entering, x, rims, dy, saved, b_proj, c_proj, conv_weight, decay_log, skip_weight):
@@ -418,16 +409,27 @@
     taps, rim = conv_weight.shape[0], rims.shape[0]
     work = length * states * channels
     tiles = WIDTH // LANES
+    turns = channels // WIDTH
+    half = turns // 2
     summed = pl.BlockSpec((states, length), lambda i, *_: (0, 0))
+
+    def at(i, place):
+        return (i // half + 1 + place[0]) % 2 * half + i % half
+
+    def chunk(rows):
+        return pl.BlockSpec((rows, WIDTH), lambda i, place: (0, at(i, place)))
+
+    tiled = pl.BlockSpec((tiles, length, LANES), lambda i, place: (at(i, place), 0, 0))
+    give = pl.BlockSpec((states + 8, WIDTH), lambda i, place: (0, jnp.minimum(i, half - 1)))
+    keep = pl.BlockSpec((states + 8, WIDTH), lambda i, place: (0, jnp.maximum(i - half, 0)))
     return pl.pallas_call(
-        partial(main_kernel, len(entering)),
+        partial(main_kernel, lax.axis_size("ctx") != 4),
         grid_spec=pltpu.PrefetchScalarGridSpec(
             num_scalar_prefetch=1,
-            grid=(channels // WIDTH,),
-            in_specs=[chunk(a.shape[0]) for a in entering] + [chunk(length), chunk(rim), chunk(length), tiled(length),
-                      chunk(length), tiled(length)] + [chunk(length)] * 3 + [whole(b_proj), whole(c_proj), chunk(taps),
+            grid=(turns,),
+            in_specs=[chunk(a.shape[0]) for a in entering] + [chunk(length), chunk(rim), chunk(length), tiled, chunk(length), tiled] + [chunk(length)] * 3 + [whole(b_proj), whole(c_proj), chunk(taps),
                       chunk(states), chunk(1)],
-            out_specs=[chunk(length), chunk(rim), chunk(BLOCK), summed, summed, chunk(states + 8)],
+            out_specs=[chunk(length), chunk(rim), chunk(BLOCK), summed, summed, give, keep],
             scratch_shapes=[pltpu.VMEM((length + 16, WIDTH), F32),
                             pltpu.VMEM((tiles, length, LANES), F32),
                             pltpu.VMEM((tiles, length * states, LANES), BF16),
@@ -441,7 +443,7 @@
                             pltpu.VMEM((tiles, states, LANES), F32)],
         ),
         out_shape=[SHAPE((length, channels), BF16), SHAPE((rim, channels), BF16), SHAPE((BLOCK, channels), F32),
-                   SHAPE((states, length), F32), SHAPE((states, length), F32), SHAPE((states + 8, channels), F32)],
+                   SHAPE((states, length), F32), SHAPE((states, length), F32)] + [SHAPE((states + 8, channels // 2), F32)] * 2,
         compiler_params=PARAMS,
         cost_estimate=pl.CostEstimate(flops=20 * work, bytes_accessed=24 * length * channels, transcendentals=2 * work),
     )(place, *entering, x, rims, dy, *saved, b_proj, c_proj, conv_weight, decay_log, flat(skip_weight))
@@ -454,26 +456,24 @@
     rim = taps - 1
     count = lax.axis_size("ctx")
     place = lax.axis_index("ctx").astype(jnp.int32).reshape(1)
-    late = (place >= count // 2).astype(jnp.int32)
     forth = [(k, k + 1) for k in range(count - 1)]
     back = [(k + 1, k) for k in range(count - 1)]
 
     def one(x, step, b_proj, c_proj, dy):
         rims = lax.ppermute(x[length - rim :, :], "ctx", forth)
-        ends, far, *saved = call_ends(late, x, rims, step, dy, b_proj, c_proj, conv_weight, conv_bias, step_bias,
-                                      decay_log)
-        return call_main(place, entering(ends, far, decay_log), x, rims, dy, saved, b_proj, c_proj,
+        ends, *saved = call_ends(x, rims, step, dy, b_proj, c_proj, conv_weight, conv_bias, step_bias, decay_log)
+        return call_main(place, entering(ends, decay_log), x, rims, dy, saved, b_proj, c_proj,
                          conv_weight, decay_log, skip_weight)
 
     outs = []
     for d in range(documents):
-        gin, borrow, tail, gb, gc, sums = one(
+        gin, borrow, tail, gb, gc, *sums = one(
             scan_input[d], step_raw[d], input_proj[d], output_proj[d], out_cotangent[d])
         given = lax.ppermute(borrow, "ctx", back).astype(F32)
         tail = (tail + jnp.pad(given, ((BLOCK - rim, 0), (0, 0)))).astype(BF16)
         gin = lax.dynamic_update_slice(gin, tail, (length - BLOCK, 0))
         outs.append((gin, gb, gc, sums))
-    sums = add_up(sum(o[3] for o in outs))
+    sums = add_up(*(sum(parts) for parts in zip(*(o[3] for o in outs))))
     return (
         jnp.stack([o[0] for o in outs]),
         jnp.stack([o[1] for o in outs]),

time: 97.7 us -> 98.7 us (1.010)
  waiting for transfers between devices: 27.9 us -> 23 us
  starting transfers between devices: 16.2 us -> 19.2 us
  Pallas kernels: 45.7 us -> 48 us
  other arithmetic: 3.76 us -> 5.17 us
  local copies, waits for them, and re-layouts: 3.2 us -> 2.15 us
    ppermute x10 -> x9, waiting for transfers between devices: 27 us -> 21.9 us  [flipped(): lax.ppermute(value, axis, [(k, k ^ bit) for k in range(lax.axis_size(axis...]
    ppermute x10 -> x9, starting transfers between devices: 12.5 us -> 15.6 us  [flipped(): lax.ppermute(value, axis, [(k, k ^ bit) for k in range(lax.axis_size(axis...]
    pallas_call x2, Pallas kernels: 45.7 us -> 48 us  [the longest x1 30.5 us: call_main(): pl.pallas_call(partial(main_kernel, lax.axis_size('ctx') != 4), grid_spec...]
    select_n x0 -> x1, other arithmetic: none -> 1.27 us  [entering(): onto = jnp.where(late == upper, mine, other)]
    dynamic_slice x2 -> x1, local copies, waits for them, and re-layouts: 1.01 us -> 0.02 us  [add_up(): give = lax.dynamic_slice_in_dim(value, (1 - upper) * half, half, 1)]
  transfers between devices with their start and end apart: 12 -> 11, of which waited for: 10 -> 11; matrix products, arithmetic and copies ran while one was open for 1% -> 1% of each run, Pallas kernels for 0% -> 0%
where the time goes in v4:
time: 98.7 us; the launch traced here: 98.4 us
  Pallas kernels  48 us (49%)
  waiting for transfers between devices  23 us (23%)
  starting transfers between devices  19.2 us (19%)
  other arithmetic  5.17 us (5%)
  local copies, waits for them, and re-layouts  2.15 us (2%)
    pallas_call x1, Pallas kernels, call_main(): pl.pallas_call(partial(main_kernel, lax.axis_size('ctx') != 4), grid_spec...  30.5 us
    ppermute x9, waiting for transfers between devices, flipped(): lax.ppermute(value, axis, [(k, k ^ bit) for k in range(lax.axis_size(axis...  21.9 us
    pallas_call x1, Pallas kernels, call_ends(): pl.pallas_call(ends_kernel, grid=(channels // ENDS_WIDTH,), in_specs=[chu...  17.5 us
    ppermute x9, starting transfers between devices, flipped(): lax.ppermute(value, axis, [(k, k ^ bit) for k in range(lax.axis_size(axis...  15.6 us
    ppermute x1, starting transfers between devices, one(): rims = lax.ppermute(x[length - rim:, :], 'ctx', forth)  2.36 us
  transfers between devices with their start and end apart: 11, of which 11 were waited for; matrix products, arithmetic and copies ran while one was open for 1% of the time, Pallas kernels for 0%

profile of v4, /device:TPU:0, one launch (start us, length us, event | category | flops | bytes accessed | tf_op | source)
XLA Modules:
  0.0 98.4 jit_solution(15768926440200003366)
XLA Ops:
  0.6 0.9 slice_bitcast_fusion
  1.5 2.4 %collective-permute-start = (bf16[3,4096]{1,0:T(4,128)(2,1)S(1)}, bf16[3,4096]{1,0:T(4,128)(2,1)S(1)}, u32[]{:S(2)}, u32[]{:S(2)}) collective-permute-start(bf16[3,4096]{1,0:T(4,128)(2,1)S(1)} %slice_bitcast_fusion), channel_id=1, source_target_pairs={{0,1},{1,2},{2,3},{4,5},{5,6},{6,7},{8,9},{9,10},{10,11},{12,13},{... | collective-permute-start | bytes 73736 | tf_op jit(solution)/shard_map/ppermute | solution.py:463
  3.9 0.8 collective-permute-done.rim_ref.refs_3_
  4.7 0.6 copy-done.4
  5.3 17.5 %shard_map.161 = (bf16[48,4096]{1,0:T(8,128)(2,1)}, f32[32,128,128]{2,1,0:T(8,128)}, f32[128,4096]{1,0:T(8,128)}, f32[32,128,128]{2,1,0:T(8,128)}, f32[128,4096]...) custom-call(bf16[128,4096]{1,0:T(8,128)(2,1)} %bitcast.26, bf16[3,4096]{1,0:T(4,128)(2,1)} %copy-done.4, ...), custom_call_target="tpu_custom_call" | custom-call | flops 67108864 | bytes 15728640 | tf_op jit(solution)/shard_map/pallas_call | solution.py:390
  22.8 2.9 %collective-permute-start.1 = (bf16[48,4096]{1,0:T(8,128)(2,1)}, bf16[48,4096]{1,0:T(8,128)(2,1)S(1)}, u32[]{:S(2)}, u32[]{:S(2)}) collective-permute-start(bf16[48,4096]{1,0:T(8,128)(2,1)} %get-tuple-element.22), channel_id=1, source_target_pairs={{0,1},{1,0},{2,3},{3,2},{4,5},{5,4},{6,7},{7,6},{8,9},{9,8},{10,11... | collective-permute-start | bytes 1179656 | tf_op jit(solution)/shard_map/ppermute | solution.py:316
  25.7 1.6 %collective-permute-done.1.refs_0_ = bf16[48,4096]{1,0:T(8,128)(2,1)S(1)} collective-permute-done((bf16[48,4096]{1,0:T(8,128)(2,1)}, bf16[48,4096]{1,0:T(8,128)(2,1)S(1)}, u32[]{:S(2)}, u32[]{:S(2)}) %collective-permute-start.1) | collective-permute-done | bytes 393248 | tf_op jit(solution)/shard_map/ppermute | solution.py:316
  27.2 1.3 %convert_select_fusion = (f32[48,4096]{1,0:T(8,128)S(1)}, f32[48,4096]{1,0:T(8,128)S(1)}) fusion(bf16[48,4096]{1,0:T(8,128)(2,1)} %get-tuple-element.22, bf16[48,4096]{1,0:T(8,128)(2,1)S(1)} %collective-permute-done.1.refs_0_, pred[]{:T(512)S(6)} %eq.17), kind=kLoop, calls=%fused_computation | loop fusion | flops 786432 | bytes 2359297 | tf_op jit(solution)/shard_map/jit(_where)/select_n | solution.py:351
  28.6 0.1 fusion.2
  28.7 2.6 %collective-permute-start.2 = (bf16[16,4096]{1,0:T(8,128)(2,1)S(1)}, bf16[16,4096]{1,0:T(8,128)(2,1)S(1)}, u32[]{:S(2)}, u32[]{:S(2)}) collective-permute-start(bf16[16,4096]{1,0:T(8,128)(2,1)S(1)} %fusion.2), channel_id=1, source_target_pairs={{0,2},{1,3},{2,0},{3,1},{4,6},{5,7},{6,4},{7,5},{8,10},{9,11},{10,... | collective-permute-start | bytes 393224 | tf_op jit(solution)/shard_map/ppermute | solution.py:316
  31.3 3.8 %collective-permute-done.2.refs_1_ = bf16[16,4096]{1,0:T(8,128)(2,1)S(1)} collective-permute-done((bf16[16,4096]{1,0:T(8,128)(2,1)S(1)}, bf16[16,4096]{1,0:T(8,128)(2,1)S(1)}, u32[]{:S(2)}, u32[]{:S(2)}) %collective-permute-start.2) | collective-permute-done | bytes 131104 | tf_op jit(solution)/shard_map/ppermute | solution.py:316
  35.1 0.6 copy-done.3
  35.8 30.5 %shard_map.162 = (bf16[128,4096]{1,0:T(8,128)(2,1)}, bf16[3,4096]{1,0:T(4,128)(2,1)}, f32[16,4096]{1,0:T(8,128)}, f32[16,128]{1,0:T(8,128)}, f32[16,128]{1,0:T(8...) custom-call(s32[1]{0:T(128)} %bitcast.place_ref, bf16[48,4096]{1,0:T(8,128)(2,1)} %copy-done, bf16[16,4096]{1,0:T(8,128)(2,1)} %copy-done.3, ...), custom_call_target="tpu_custom_call" | custom-call | flops 167772160 | bytes 12582912 | tf_op jit(solution)/shard_map/pallas_call | solution.py:425
  66.4 1.6 %collective-permute-done.4 = f32[24,2048]{1,0:T(8,128)S(1)} collective-permute-done((f32[24,2048]{1,0:T(8,128)}, f32[24,2048]{1,0:T(8,128)S(1)}, u32[]{:S(2)}, u32[]{:S(2)}) %collective-permute-start.4) | collective-permute-done | bytes 196640 | tf_op jit(solution)/shard_map/ppermute | solution.py:316
  68.0 0.9 add.52
  69.0 1.8 %collective-permute-start.5 = (f32[24,1024]{1,0:T(8,128)S(1)}, f32[24,1024]{1,0:T(8,128)S(1)}, u32[]{:S(2)}, u32[]{:S(2)}) collective-permute-start(f32[24,1024]{1,0:T(8,128)S(1)} %constant_dynamic-slice_fusion), channel_id=1, source_target_pairs={{0,2},{1,3},{2,0},{3,1},{4,6},{5,7},{6,4},{7,5},{8,10},{9,11},{10,... | collective-permute-start | bytes 294920 | tf_op jit(solution)/shard_map/ppermute | solution.py:316
  70.8 3.1 %collective-permute-done.5 = f32[24,1024]{1,0:T(8,128)S(1)} collective-permute-done((f32[24,1024]{1,0:T(8,128)S(1)}, f32[24,1024]{1,0:T(8,128)S(1)}, u32[]{:S(2)}, u32[]{:S(2)}) %collective-permute-start.5) | collective-permute-done | bytes 98336 | tf_op jit(solution)/shard_map/ppermute | solution.py:316
  73.9 1.6 %collective-permute-start.6 = (f32[24,1024]{1,0:T(8,128)S(1)}, f32[24,1024]{1,0:T(8,128)S(1)}, u32[]{:S(2)}, u32[]{:S(2)}) collective-permute-start(f32[24,1024]{1,0:T(8,128)S(1)} %dynamic-slice_add_fusion), channel_id=1, source_target_pairs={{0,4},{4,0},{8,12},{12,8},{16,20},{20,16},{24,28},{28,24},{1,5},{5... | collective-permute-start | bytes 294920 | tf_op jit(solution)/shard_map/ppermute | solution.py:316
  75.5 3.1 %collective-permute-done.6 = f32[24,1024]{1,0:T(8,128)S(1)} collective-permute-done((f32[24,1024]{1,0:T(8,128)S(1)}, f32[24,1024]{1,0:T(8,128)S(1)}, u32[]{:S(2)}, u32[]{:S(2)}) %collective-permute-start.6) | collective-permute-done | bytes 98336 | tf_op jit(solution)/shard_map/ppermute | solution.py:316
  78.6 1.6 %collective-permute-start.7 = (f32[24,1024]{1,0:T(8,128)S(1)}, f32[24,1024]{1,0:T(8,128)S(1)}, u32[]{:S(2)}, u32[]{:S(2)}) collective-permute-start(f32[24,1024]{1,0:T(8,128)S(1)} %add.56), channel_id=1, source_target_pairs={{0,8},{4,12},{8,0},{12,4},{16,24},{20,28},{24,16},{28,20},{1,9},{5... | collective-permute-start | bytes 294920 | tf_op jit(solution)/shard_map/ppermute | solution.py:316
  80.3 3.0 %collective-permute-done.7 = f32[24,1024]{1,0:T(8,128)S(1)} collective-permute-done((f32[24,1024]{1,0:T(8,128)S(1)}, f32[24,1024]{1,0:T(8,128)S(1)}, u32[]{:S(2)}, u32[]{:S(2)}) %collective-permute-start.7) | collective-permute-done | bytes 98336 | tf_op jit(solution)/shard_map/ppermute | solution.py:316
  83.3 3.1 %collective-permute-start.8 = (f32[24,1024]{1,0:T(8,128)S(1)}, f32[24,1024]{1,0:T(8,128)S(1)}, u32[]{:S(2)}, u32[]{:S(2)}) collective-permute-start(f32[24,1024]{1,0:T(8,128)S(1)} %add.57), channel_id=1, source_target_pairs={{0,16},{4,20},{8,24},{12,28},{16,0},{20,4},{24,8},{28,12},{1,17},{... | collective-permute-start | bytes 294920 | tf_op jit(solution)/shard_map/ppermute | solution.py:316
  86.5 3.6 %collective-permute-done.8 = f32[24,1024]{1,0:T(8,128)S(1)} collective-permute-done((f32[24,1024]{1,0:T(8,128)S(1)}, f32[24,1024]{1,0:T(8,128)S(1)}, u32[]{:S(2)}, u32[]{:S(2)}) %collective-permute-start.8) | collective-permute-done | bytes 98336 | tf_op jit(solution)/shard_map/ppermute | solution.py:316
  90.1 1.8 %collective-permute-start.9 = (f32[24,1024]{1,0:T(8,128)S(1)}, f32[24,1024]{1,0:T(8,128)S(1)}, u32[]{:S(2)}, u32[]{:S(2)}) collective-permute-start(f32[24,1024]{1,0:T(8,128)S(1)} %add.58), channel_id=1, source_target_pairs={{0,2},{1,3},{2,0},{3,1},{4,6},{5,7},{6,4},{7,5},{8,10},{9,11},{10,... | collective-permute-start | bytes 294920 | tf_op jit(solution)/shard_map/ppermute | solution.py:316
  91.9 1.3 %collective-permute-start.3 = (bf16[3,4096]{1,0:T(4,128)(2,1)}, bf16[3,4096]{1,0:T(4,128)(2,1)S(1)}, u32[]{:S(2)}, u32[]{:S(2)}) collective-permute-start(bf16[3,4096]{1,0:T(4,128)(2,1)} %get-tuple-element.31), channel_id=1, source_target_pairs={{1,0},{2,1},{3,2},{5,4},{6,5},{7,6},{9,8},{10,9},{11,10},{13,12},{... | collective-permute-start | bytes 73736 | tf_op jit(solution)/shard_map/ppermute | solution.py:472
  93.2 1.6 %collective-permute-done.9 = f32[24,1024]{1,0:T(8,128)S(1)} collective-permute-done((f32[24,1024]{1,0:T(8,128)S(1)}, f32[24,1024]{1,0:T(8,128)S(1)}, u32[]{:S(2)}, u32[]{:S(2)}) %collective-permute-start.9) | collective-permute-done | bytes 98336 | tf_op jit(solution)/shard_map/ppermute | solution.py:316
  94.9 0.3 collective-permute-done.3
  95.2 0.7 fusion.5
  95.9 0.4 collective-permute-done.10
  96.4 0.7 pad_maximum_fusion.2
  97.0 0.6 pad_maximum_fusion.1
  97.7 0.7 fusion
  (19 shorter events, 0.3 us)
Async XLA Ops:
  1.5 3.2 %collective-permute-start = (bf16[3,4096]{1,0:T(4,128)(2,1)S(1)}, bf16[3,4096]{1,0:T(4,128)(2,1)S(1)}, u32[]{:S(2)}, u32[]{:S(2)}) collective-permute-start(bf16[3,4096]{1,0:T(4,128)(2,1)S(1)} %slice_bitcast_fusion), channel_id=1, source_target_pairs={{0,1},{1,2},{2,3},{4,5},{5,6},{6,7},{8,9},{9,10},{10,11},{12,13},{... | collective-permute-start | bytes 73736 | tf_op jit(solution)/shard_map/ppermute | solution.py:463
  4.7 0.6 copy-start.4
  22.8 5.8 %copy-start.2 = (f32[16,4096]{1,0:T(8,128)S(1)}, f32[16,4096]{1,0:T(8,128)}, u32[]{:S(2)}) copy-start(f32[16,4096]{1,0:T(8,128)} %refs_14_.1) | copy-start | bytes 786436
  22.8 4.4 %collective-permute-start.1 = (bf16[48,4096]{1,0:T(8,128)(2,1)}, bf16[48,4096]{1,0:T(8,128)(2,1)S(1)}, u32[]{:S(2)}, u32[]{:S(2)}) collective-permute-start(bf16[48,4096]{1,0:T(8,128)(2,1)} %get-tuple-element.22), channel_id=1, source_target_pairs={{0,1},{1,0},{2,3},{3,2},{4,5},{5,4},{6,7},{7,6},{8,9},{9,8},{10,11... | collective-permute-start | bytes 1179656 | tf_op jit(solution)/shard_map/ppermute | solution.py:316
  27.2 7.9 %copy-start = (bf16[48,4096]{1,0:T(8,128)(2,1)}, bf16[48,4096]{1,0:T(8,128)(2,1)S(1)}, u32[]{:S(2)}) copy-start(bf16[48,4096]{1,0:T(8,128)(2,1)S(1)} %collective-permute-done.1.refs_0_) | copy-start | bytes 1179652
  28.7 6.4 %collective-permute-start.2 = (bf16[16,4096]{1,0:T(8,128)(2,1)S(1)}, bf16[16,4096]{1,0:T(8,128)(2,1)S(1)}, u32[]{:S(2)}, u32[]{:S(2)}) collective-permute-start(bf16[16,4096]{1,0:T(8,128)(2,1)S(1)} %fusion.2), channel_id=1, source_target_pairs={{0,2},{1,3},{2,0},{3,1},{4,6},{5,7},{6,4},{7,5},{8,10},{9,11},{10,... | collective-permute-start | bytes 393224 | tf_op jit(solution)/shard_map/ppermute | solution.py:316
  35.1 0.6 copy-start.3
  66.3 28.9 %copy-start.1 = (f32[16,4096]{1,0:T(8,128)S(1)}, f32[16,4096]{1,0:T(8,128)}, u32[]{:S(2)}) copy-start(f32[16,4096]{1,0:T(8,128)} %get-tuple-element.30) | copy-start | bytes 786436
  66.3 1.7 %collective-permute-start.4 = (f32[24,2048]{1,0:T(8,128)}, f32[24,2048]{1,0:T(8,128)S(1)}, u32[]{:S(2)}, u32[]{:S(2)}) collective-permute-start(f32[24,2048]{1,0:T(8,128)} %get-tuple-element.35), channel_id=1, source_target_pairs={{0,1},{1,0},{2,3},{3,2},{4,5},{5,4},{6,7},{7,6},{8,9},{9,8},{10,11... | collective-permute-start | bytes 589832 | tf_op jit(solution)/shard_map/ppermute | solution.py:316
  69.0 4.9 %collective-permute-start.5 = (f32[24,1024]{1,0:T(8,128)S(1)}, f32[24,1024]{1,0:T(8,128)S(1)}, u32[]{:S(2)}, u32[]{:S(2)}) collective-permute-start(f32[24,1024]{1,0:T(8,128)S(1)} %constant_dynamic-slice_fusion), channel_id=1, source_target_pairs={{0,2},{1,3},{2,0},{3,1},{4,6},{5,7},{6,4},{7,5},{8,10},{9,11},{10,... | collective-permute-start | bytes 294920 | tf_op jit(solution)/shard_map/ppermute | solution.py:316
  73.9 4.7 %collective-permute-start.6 = (f32[24,1024]{1,0:T(8,128)S(1)}, f32[24,1024]{1,0:T(8,128)S(1)}, u32[]{:S(2)}, u32[]{:S(2)}) collective-permute-start(f32[24,1024]{1,0:T(8,128)S(1)} %dynamic-slice_add_fusion), channel_id=1, source_target_pairs={{0,4},{4,0},{8,12},{12,8},{16,20},{20,16},{24,28},{28,24},{1,5},{5... | collective-permute-start | bytes 294920 | tf_op jit(solution)/shard_map/ppermute | solution.py:316
  78.6 4.7 %collective-permute-start.7 = (f32[24,1024]{1,0:T(8,128)S(1)}, f32[24,1024]{1,0:T(8,128)S(1)}, u32[]{:S(2)}, u32[]{:S(2)}) collective-permute-start(f32[24,1024]{1,0:T(8,128)S(1)} %add.56), channel_id=1, source_target_pairs={{0,8},{4,12},{8,0},{12,4},{16,24},{20,28},{24,16},{28,20},{1,9},{5... | collective-permute-start | bytes 294920 | tf_op jit(solution)/shard_map/ppermute | solution.py:316
  83.3 6.8 %collective-permute-start.8 = (f32[24,1024]{1,0:T(8,128)S(1)}, f32[24,1024]{1,0:T(8,128)S(1)}, u32[]{:S(2)}, u32[]{:S(2)}) collective-permute-start(f32[24,1024]{1,0:T(8,128)S(1)} %add.57), channel_id=1, source_target_pairs={{0,16},{4,20},{8,24},{12,28},{16,0},{20,4},{24,8},{28,12},{1,17},{... | collective-permute-start | bytes 294920 | tf_op jit(solution)/shard_map/ppermute | solution.py:316
  90.1 4.7 %collective-permute-start.9 = (f32[24,1024]{1,0:T(8,128)S(1)}, f32[24,1024]{1,0:T(8,128)S(1)}, u32[]{:S(2)}, u32[]{:S(2)}) collective-permute-start(f32[24,1024]{1,0:T(8,128)S(1)} %add.58), channel_id=1, source_target_pairs={{0,2},{1,3},{2,0},{3,1},{4,6},{5,7},{6,4},{7,5},{8,10},{9,11},{10,... | collective-permute-start | bytes 294920 | tf_op jit(solution)/shard_map/ppermute | solution.py:316
  91.9 3.3 %collective-permute-start.3 = (bf16[3,4096]{1,0:T(4,128)(2,1)}, bf16[3,4096]{1,0:T(4,128)(2,1)S(1)}, u32[]{:S(2)}, u32[]{:S(2)}) collective-permute-start(bf16[3,4096]{1,0:T(4,128)(2,1)} %get-tuple-element.31), channel_id=1, source_target_pairs={{1,0},{2,1},{3,2},{5,4},{6,5},{7,6},{9,8},{10,9},{11,10},{13,12},{... | collective-permute-start | bytes 73736 | tf_op jit(solution)/shard_map/ppermute | solution.py:472
  94.8 1.5 %collective-permute-start.10 = (f32[24,2048]{1,0:T(8,128)S(1)}, f32[24,2048]{1,0:T(8,128)S(1)}, u32[]{:S(2)}, u32[]{:S(2)}) collective-permute-start(f32[24,2048]{1,0:T(8,128)S(1)} %pad_maximum_fusion), channel_id=1, source_target_pairs={{0,1},{1,0},{2,3},{3,2},{4,5},{5,4},{6,7},{7,6},{8,9},{9,8},{10,11... | collective-permute-start | bytes 589832 | tf_op jit(solution)/shard_map/ppermute | solution.py:316

commit v5 on v4

--- a/solution.py
+++ b/solution.py
@@ -346,13 +346,12 @@
     if count == 4:
         late, upper = place >= 2, place % 2 == 1
         sib = flipped(ends, "ctx", 1)
-        mine, other = ends.astype(F32), sib.astype(F32)
-        passing = jnp.where(late == upper, other, mine)
-        onto = jnp.where(late == upper, mine, other)
-        if_early = lambda piece: jnp.where(late, piece[states : 2 * states], piece[:states])
-        total = passing[2 * states : 2 * states + 1] + passing[2 * states + 1 : 2 * states + 2]
-        total = total + passing[2 * states + 2 : 2 * states + 3]
-        both = jnp.exp(-jnp.exp(decay_log) * total) * if_early(onto) + if_early(passing)
+        swap = late == upper
+        mine = jnp.where(late, ends[states : 2 * states], ends[:states]).astype(F32)
+        other = jnp.where(late, sib[states : 2 * states], sib[:states]).astype(F32)
+        parts = [jnp.where(swap, sib[k : k + 1], ends[k : k + 1]).astype(F32) for k in range(2 * states, 2 * states + 3)]
+        decay = jnp.exp(-jnp.exp(decay_log) * (parts[0] + parts[1] + parts[2]))
+        both = decay * jnp.where(swap, mine, other) + jnp.where(swap, other, mine)
         return sib, flipped(both.astype(BF16), "ctx", 2)
     rate = -jnp.exp(decay_log)
     gathered = lax.all_gather(ends, "ctx").astype(F32)
@@ -414,7 +413,7 @@
     summed = pl.BlockSpec((states, length), lambda i, *_: (0, 0))
 
     def at(i, place):
-        return (i // half + 1 + place[0]) % 2 * half + i % half
+        return place[1 + i]
 
     def chunk(rows):
         return pl.BlockSpec((rows, WIDTH), lambda i, place: (0, at(i, place)))
@@ -422,6 +421,8 @@
     tiled = pl.BlockSpec((tiles, length, LANES), lambda i, place: (at(i, place), 0, 0))
     give = pl.BlockSpec((states + 8, WIDTH), lambda i, place: (0, jnp.minimum(i, half - 1)))
     keep = pl.BlockSpec((states + 8, WIDTH), lambda i, place: (0, jnp.maximum(i - half, 0)))
+    turn = jnp.arange(turns, dtype=jnp.int32)
+    place = jnp.concatenate([place, (turn + half * (1 - place % 2)) % turns])
     return pl.pallas_call(
         partial(main_kernel, lax.axis_size("ctx") != 4),
         grid_spec=pltpu.PrefetchScalarGridSpec(

time: 98.7 us -> 100 us (1.013)
  other arithmetic: 5.17 us -> 6.6 us
    select_n x1, other arithmetic: 1.27 us -> 0.01 us  [call_main(): place = jnp.concatenate([place, (turn + half * (1 - place % 2)) % turns])]
    add x1, other arithmetic: 0.03 us -> 1.12 us  [entering(): decay = jnp.exp(-jnp.exp(decay_log) * (parts[0] + parts[1] + parts[2]))]
    convert_element_type x1, other arithmetic: 0.11 us -> 1.12 us  [entering(): return (sib, flipped(both.astype(BF16), 'ctx', 2))]
where the time goes in v5:
time: 100 us; the launch traced here: 99.9 us
  Pallas kernels  48.7 us (49%)
  waiting for transfers between devices  22.4 us (22%)
  starting transfers between devices  19.2 us (19%)
  other arithmetic  6.6 us (7%)
  local copies, waits for them, and re-layouts  2.15 us (2%)
    pallas_call x1, Pallas kernels, call_main(): pl.pallas_call(partial(main_kernel, lax.axis_size('ctx') != 4), grid_spec...  31.2 us
    ppermute x9, waiting for transfers between devices, flipped(): lax.ppermute(value, axis, [(k, k ^ bit) for k in range(lax.axis_size(axis...  21.3 us
    pallas_call x1, Pallas kernels, call_ends(): pl.pallas_call(ends_kernel, grid=(channels // ENDS_WIDTH,), in_specs=[chu...  17.5 us
    ppermute x9, starting transfers between devices, flipped(): lax.ppermute(value, axis, [(k, k ^ bit) for k in range(lax.axis_size(axis...  15.6 us
    ppermute x1, starting transfers between devices, one(): rims = lax.ppermute(x[length - rim:, :], 'ctx', forth)  2.36 us
  transfers between devices with their start and end apart: 11, of which 11 were waited for; matrix products, arithmetic and copies ran while one was open for 1% of the time, Pallas kernels for 0%

profile of v5, /device:TPU:0, one launch (start us, length us, event | category | flops | bytes accessed | tf_op | source)
XLA Modules:
  0.0 99.9 jit_solution(8043261007090413660)
XLA Ops:
  0.6 0.9 slice_bitcast_fusion
  1.5 2.4 %collective-permute-start = (bf16[3,4096]{1,0:T(4,128)(2,1)S(1)}, bf16[3,4096]{1,0:T(4,128)(2,1)S(1)}, u32[]{:S(2)}, u32[]{:S(2)}) collective-permute-start(bf16[3,4096]{1,0:T(4,128)(2,1)S(1)} %slice_bitcast_fusion), channel_id=1, source_target_pairs={{0,1},{1,2},{2,3},{4,5},{5,6},{6,7},{8,9},{9,10},{10,11},{12,13},{... | collective-permute-start | bytes 73736 | tf_op jit(solution)/shard_map/ppermute | solution.py:464
  3.9 0.8 collective-permute-done.rim_ref.refs_3_
  4.7 0.6 copy-done.4
  5.3 17.5 %shard_map.161 = (bf16[48,4096]{1,0:T(8,128)(2,1)}, f32[32,128,128]{2,1,0:T(8,128)}, f32[128,4096]{1,0:T(8,128)}, f32[32,128,128]{2,1,0:T(8,128)}, f32[128,4096]...) custom-call(bf16[128,4096]{1,0:T(8,128)(2,1)} %bitcast.27, bf16[3,4096]{1,0:T(4,128)(2,1)} %copy-done.4, ...), custom_call_target="tpu_custom_call" | custom-call | flops 67108864 | bytes 15728640 | tf_op jit(solution)/shard_map/pallas_call | solution.py:389
  22.9 2.9 %collective-permute-start.1 = (bf16[48,4096]{1,0:T(8,128)(2,1)}, bf16[48,4096]{1,0:T(8,128)(2,1)S(1)}, u32[]{:S(2)}, u32[]{:S(2)}) collective-permute-start(bf16[48,4096]{1,0:T(8,128)(2,1)} %get-tuple-element.22), channel_id=1, source_target_pairs={{0,1},{1,0},{2,3},{3,2},{4,5},{5,4},{6,7},{7,6},{8,9},{9,8},{10,11... | collective-permute-start | bytes 1179656 | tf_op jit(solution)/shard_map/ppermute | solution.py:316
  25.7 1.6 %collective-permute-done.1.refs_0_ = bf16[48,4096]{1,0:T(8,128)(2,1)S(1)} collective-permute-done((bf16[48,4096]{1,0:T(8,128)(2,1)}, bf16[48,4096]{1,0:T(8,128)(2,1)S(1)}, u32[]{:S(2)}, u32[]{:S(2)}) %collective-permute-start.1) | collective-permute-done | bytes 393248 | tf_op jit(solution)/shard_map/ppermute | solution.py:316
  27.3 1.1 %fusion.8 = f32[1,4096]{1,0:T(1,128)S(1)} fusion(pred[]{:T(512)S(6)} %eq.20, bf16[48,4096]{1,0:T(8,128)(2,1)S(1)} %collective-permute-done.1.refs_0_, bf16[48,4096]{1,0:T(8,128)(2,1)} %get-tuple-element.22), kind=kLoop, calls=%fused_computation.25 | loop fusion | flops 32768 | bytes 65537 | tf_op jit(solution)/shard_map/add | solution.py:353
  28.4 1.1 %fusion.2 = bf16[16,4096]{1,0:T(8,128)(2,1)S(1)} fusion(f32[16,4096]{1,0:T(8,128)S(1)} %copy-done, bf16[48,4096]{1,0:T(8,128)(2,1)S(1)} %collective-permute-done.1.refs_0_, bf16[48,4096]{1,0:T(8,128)(2,1)} %get-tuple-element.22, f32[4096]{0:T(1024)S(1)} %bitcast.23, pred[]{:T(512)S(6)} %ge.3, pred[]{:T(512)S(6)} %eq.20), kind=kLoop, calls=%fused_computation.6 | loop fusion | flops 720896 | bytes 933890 | tf_op jit(solution)/shard_map/convert_element_type | solution.py:355
  29.5 2.6 %collective-permute-start.2 = (bf16[16,4096]{1,0:T(8,128)(2,1)S(1)}, bf16[16,4096]{1,0:T(8,128)(2,1)S(1)}, u32[]{:S(2)}, u32[]{:S(2)}) collective-permute-start(bf16[16,4096]{1,0:T(8,128)(2,1)S(1)} %fusion.2), channel_id=1, source_target_pairs={{0,2},{1,3},{2,0},{3,1},{4,6},{5,7},{6,4},{7,5},{8,10},{9,11},{10,... | collective-permute-start | bytes 393224 | tf_op jit(solution)/shard_map/ppermute | solution.py:316
  32.2 0.6 pad_add_fusion.place_ref
  32.8 3.2 %collective-permute-done.2.refs_1_ = bf16[16,4096]{1,0:T(8,128)(2,1)S(1)} collective-permute-done((bf16[16,4096]{1,0:T(8,128)(2,1)S(1)}, bf16[16,4096]{1,0:T(8,128)(2,1)S(1)}, u32[]{:S(2)}, u32[]{:S(2)}) %collective-permute-start.2) | collective-permute-done | bytes 131104 | tf_op jit(solution)/shard_map/ppermute | solution.py:316
  36.0 0.6 copy-done.3
  36.6 31.2 %shard_map.162 = (bf16[128,4096]{1,0:T(8,128)(2,1)}, bf16[3,4096]{1,0:T(4,128)(2,1)}, f32[16,4096]{1,0:T(8,128)}, f32[16,128]{1,0:T(8,128)}, f32[16,128]{1,0:T(8...) custom-call(s32[9]{0:T(128)} %pad_add_fusion.place_ref, bf16[48,4096]{1,0:T(8,128)(2,1)} %copy-done.2, ...), custom_call_target="tpu_custom_call" | custom-call | flops 167772160 | bytes 12582912 | tf_op jit(solution)/shard_map/pallas_call | solution.py:426
  67.9 1.6 %collective-permute-done.4 = f32[24,2048]{1,0:T(8,128)S(1)} collective-permute-done((f32[24,2048]{1,0:T(8,128)}, f32[24,2048]{1,0:T(8,128)S(1)}, u32[]{:S(2)}, u32[]{:S(2)}) %collective-permute-start.4) | collective-permute-done | bytes 196640 | tf_op jit(solution)/shard_map/ppermute | solution.py:316
  69.5 0.9 add.79
  70.5 1.8 %collective-permute-start.5 = (f32[24,1024]{1,0:T(8,128)S(1)}, f32[24,1024]{1,0:T(8,128)S(1)}, u32[]{:S(2)}, u32[]{:S(2)}) collective-permute-start(f32[24,1024]{1,0:T(8,128)S(1)} %constant_dynamic-slice_fusion), channel_id=1, source_target_pairs={{0,2},{1,3},{2,0},{3,1},{4,6},{5,7},{6,4},{7,5},{8,10},{9,11},{10,... | collective-permute-start | bytes 294920 | tf_op jit(solution)/shard_map/ppermute | solution.py:316
  72.3 3.1 %collective-permute-done.5 = f32[24,1024]{1,0:T(8,128)S(1)} collective-permute-done((f32[24,1024]{1,0:T(8,128)S(1)}, f32[24,1024]{1,0:T(8,128)S(1)}, u32[]{:S(2)}, u32[]{:S(2)}) %collective-permute-start.5) | collective-permute-done | bytes 98336 | tf_op jit(solution)/shard_map/ppermute | solution.py:316
  75.4 1.6 %collective-permute-start.6 = (f32[24,1024]{1,0:T(8,128)S(1)}, f32[24,1024]{1,0:T(8,128)S(1)}, u32[]{:S(2)}, u32[]{:S(2)}) collective-permute-start(f32[24,1024]{1,0:T(8,128)S(1)} %dynamic-slice_add_fusion), channel_id=1, source_target_pairs={{0,4},{4,0},{8,12},{12,8},{16,20},{20,16},{24,28},{28,24},{1,5},{5... | collective-permute-start | bytes 294920 | tf_op jit(solution)/shard_map/ppermute | solution.py:316
  77.0 3.1 %collective-permute-done.6 = f32[24,1024]{1,0:T(8,128)S(1)} collective-permute-done((f32[24,1024]{1,0:T(8,128)S(1)}, f32[24,1024]{1,0:T(8,128)S(1)}, u32[]{:S(2)}, u32[]{:S(2)}) %collective-permute-start.6) | collective-permute-done | bytes 98336 | tf_op jit(solution)/shard_map/ppermute | solution.py:316
  80.1 1.6 %collective-permute-start.7 = (f32[24,1024]{1,0:T(8,128)S(1)}, f32[24,1024]{1,0:T(8,128)S(1)}, u32[]{:S(2)}, u32[]{:S(2)}) collective-permute-start(f32[24,1024]{1,0:T(8,128)S(1)} %add.83), channel_id=1, source_target_pairs={{0,8},{4,12},{8,0},{12,4},{16,24},{20,28},{24,16},{28,20},{1,9},{5... | collective-permute-start | bytes 294920 | tf_op jit(solution)/shard_map/ppermute | solution.py:316
  81.8 3.0 %collective-permute-done.7 = f32[24,1024]{1,0:T(8,128)S(1)} collective-permute-done((f32[24,1024]{1,0:T(8,128)S(1)}, f32[24,1024]{1,0:T(8,128)S(1)}, u32[]{:S(2)}, u32[]{:S(2)}) %collective-permute-start.7) | collective-permute-done | bytes 98336 | tf_op jit(solution)/shard_map/ppermute | solution.py:316
  84.8 3.1 %collective-permute-start.8 = (f32[24,1024]{1,0:T(8,128)S(1)}, f32[24,1024]{1,0:T(8,128)S(1)}, u32[]{:S(2)}, u32[]{:S(2)}) collective-permute-start(f32[24,1024]{1,0:T(8,128)S(1)} %add.84), channel_id=1, source_target_pairs={{0,16},{4,20},{8,24},{12,28},{16,0},{20,4},{24,8},{28,12},{1,17},{... | collective-permute-start | bytes 294920 | tf_op jit(solution)/shard_map/ppermute | solution.py:316
  88.0 3.6 %collective-permute-done.8 = f32[24,1024]{1,0:T(8,128)S(1)} collective-permute-done((f32[24,1024]{1,0:T(8,128)S(1)}, f32[24,1024]{1,0:T(8,128)S(1)}, u32[]{:S(2)}, u32[]{:S(2)}) %collective-permute-start.8) | collective-permute-done | bytes 98336 | tf_op jit(solution)/shard_map/ppermute | solution.py:316
  91.6 1.8 %collective-permute-start.9 = (f32[24,1024]{1,0:T(8,128)S(1)}, f32[24,1024]{1,0:T(8,128)S(1)}, u32[]{:S(2)}, u32[]{:S(2)}) collective-permute-start(f32[24,1024]{1,0:T(8,128)S(1)} %add.85), channel_id=1, source_target_pairs={{0,2},{1,3},{2,0},{3,1},{4,6},{5,7},{6,4},{7,5},{8,10},{9,11},{10,... | collective-permute-start | bytes 294920 | tf_op jit(solution)/shard_map/ppermute | solution.py:316
  93.4 1.3 %collective-permute-start.3 = (bf16[3,4096]{1,0:T(4,128)(2,1)}, bf16[3,4096]{1,0:T(4,128)(2,1)S(1)}, u32[]{:S(2)}, u32[]{:S(2)}) collective-permute-start(bf16[3,4096]{1,0:T(4,128)(2,1)} %get-tuple-element.31), channel_id=1, source_target_pairs={{1,0},{2,1},{3,2},{5,4},{6,5},{7,6},{9,8},{10,9},{11,10},{13,12},{... | collective-permute-start | bytes 73736 | tf_op jit(solution)/shard_map/ppermute | solution.py:473
  94.7 1.6 %collective-permute-done.9 = f32[24,1024]{1,0:T(8,128)S(1)} collective-permute-done((f32[24,1024]{1,0:T(8,128)S(1)}, f32[24,1024]{1,0:T(8,128)S(1)}, u32[]{:S(2)}, u32[]{:S(2)}) %collective-permute-start.9) | collective-permute-done | bytes 98336 | tf_op jit(solution)/shard_map/ppermute | solution.py:316
  96.7 0.7 fusion.5
  97.4 0.4 collective-permute-done.10
  97.9 0.7 pad_maximum_fusion.2
  98.6 0.6 pad_maximum_fusion.1
  99.2 0.7 fusion.3
  (20 shorter events, 0.6 us)
Async XLA Ops:
  1.5 3.2 %collective-permute-start = (bf16[3,4096]{1,0:T(4,128)(2,1)S(1)}, bf16[3,4096]{1,0:T(4,128)(2,1)S(1)}, u32[]{:S(2)}, u32[]{:S(2)}) collective-permute-start(bf16[3,4096]{1,0:T(4,128)(2,1)S(1)} %slice_bitcast_fusion), channel_id=1, source_target_pairs={{0,1},{1,2},{2,3},{4,5},{5,6},{6,7},{8,9},{9,10},{10,11},{12,13},{... | collective-permute-start | bytes 73736 | tf_op jit(solution)/shard_map/ppermute | solution.py:464
  4.7 0.6 copy-start.4
  5.3 23.1 %copy-start = (f32[16,4096]{1,0:T(8,128)S(1)}, f32[16,4096]{1,0:T(8,128)}, u32[]{:S(2)}) copy-start(f32[16,4096]{1,0:T(8,128)} %refs_14_.1) | copy-start | bytes 786436
  22.9 4.4 %collective-permute-start.1 = (bf16[48,4096]{1,0:T(8,128)(2,1)}, bf16[48,4096]{1,0:T(8,128)(2,1)S(1)}, u32[]{:S(2)}, u32[]{:S(2)}) collective-permute-start(bf16[48,4096]{1,0:T(8,128)(2,1)} %get-tuple-element.22), channel_id=1, source_target_pairs={{0,1},{1,0},{2,3},{3,2},{4,5},{5,4},{6,7},{7,6},{8,9},{9,8},{10,11... | collective-permute-start | bytes 1179656 | tf_op jit(solution)/shard_map/ppermute | solution.py:316
  27.3 8.7 %copy-start.2 = (bf16[48,4096]{1,0:T(8,128)(2,1)}, bf16[48,4096]{1,0:T(8,128)(2,1)S(1)}, u32[]{:S(2)}) copy-start(bf16[48,4096]{1,0:T(8,128)(2,1)S(1)} %collective-permute-done.1.refs_0_) | copy-start | bytes 1179652
  29.5 6.4 %collective-permute-start.2 = (bf16[16,4096]{1,0:T(8,128)(2,1)S(1)}, bf16[16,4096]{1,0:T(8,128)(2,1)S(1)}, u32[]{:S(2)}, u32[]{:S(2)}) collective-permute-start(bf16[16,4096]{1,0:T(8,128)(2,1)S(1)} %fusion.2), channel_id=1, source_target_pairs={{0,2},{1,3},{2,0},{3,1},{4,6},{5,7},{6,4},{7,5},{8,10},{9,11},{10,... | collective-permute-start | bytes 393224 | tf_op jit(solution)/shard_map/ppermute | solution.py:316
  36.0 0.6 copy-start.3
  67.8 28.9 %copy-start.1 = (f32[16,4096]{1,0:T(8,128)S(1)}, f32[16,4096]{1,0:T(8,128)}, u32[]{:S(2)}) copy-start(f32[16,4096]{1,0:T(8,128)} %get-tuple-element.30) | copy-start | bytes 786436
  67.8 1.7 %collective-permute-start.4 = (f32[24,2048]{1,0:T(8,128)}, f32[24,2048]{1,0:T(8,128)S(1)}, u32[]{:S(2)}, u32[]{:S(2)}) collective-permute-start(f32[24,2048]{1,0:T(8,128)} %get-tuple-element.35), channel_id=1, source_target_pairs={{0,1},{1,0},{2,3},{3,2},{4,5},{5,4},{6,7},{7,6},{8,9},{9,8},{10,11... | collective-permute-start | bytes 589832 | tf_op jit(solution)/shard_map/ppermute | solution.py:316
  70.5 4.9 %collective-permute-start.5 = (f32[24,1024]{1,0:T(8,128)S(1)}, f32[24,1024]{1,0:T(8,128)S(1)}, u32[]{:S(2)}, u32[]{:S(2)}) collective-permute-start(f32[24,1024]{1,0:T(8,128)S(1)} %constant_dynamic-slice_fusion), channel_id=1, source_target_pairs={{0,2},{1,3},{2,0},{3,1},{4,6},{5,7},{6,4},{7,5},{8,10},{9,11},{10,... | collective-permute-start | bytes 294920 | tf_op jit(solution)/shard_map/ppermute | solution.py:316
  75.4 4.7 %collective-permute-start.6 = (f32[24,1024]{1,0:T(8,128)S(1)}, f32[24,1024]{1,0:T(8,128)S(1)}, u32[]{:S(2)}, u32[]{:S(2)}) collective-permute-start(f32[24,1024]{1,0:T(8,128)S(1)} %dynamic-slice_add_fusion), channel_id=1, source_target_pairs={{0,4},{4,0},{8,12},{12,8},{16,20},{20,16},{24,28},{28,24},{1,5},{5... | collective-permute-start | bytes 294920 | tf_op jit(solution)/shard_map/ppermute | solution.py:316
  80.1 4.7 %collective-permute-start.7 = (f32[24,1024]{1,0:T(8,128)S(1)}, f32[24,1024]{1,0:T(8,128)S(1)}, u32[]{:S(2)}, u32[]{:S(2)}) collective-permute-start(f32[24,1024]{1,0:T(8,128)S(1)} %add.83), channel_id=1, source_target_pairs={{0,8},{4,12},{8,0},{12,4},{16,24},{20,28},{24,16},{28,20},{1,9},{5... | collective-permute-start | bytes 294920 | tf_op jit(solution)/shard_map/ppermute | solution.py:316
  84.8 6.8 %collective-permute-start.8 = (f32[24,1024]{1,0:T(8,128)S(1)}, f32[24,1024]{1,0:T(8,128)S(1)}, u32[]{:S(2)}, u32[]{:S(2)}) collective-permute-start(f32[24,1024]{1,0:T(8,128)S(1)} %add.84), channel_id=1, source_target_pairs={{0,16},{4,20},{8,24},{12,28},{16,0},{20,4},{24,8},{28,12},{1,17},{... | collective-permute-start | bytes 294920 | tf_op jit(solution)/shard_map/ppermute | solution.py:316
  91.6 4.7 %collective-permute-start.9 = (f32[24,1024]{1,0:T(8,128)S(1)}, f32[24,1024]{1,0:T(8,128)S(1)}, u32[]{:S(2)}, u32[]{:S(2)}) collective-permute-start(f32[24,1024]{1,0:T(8,128)S(1)} %add.85), channel_id=1, source_target_pairs={{0,2},{1,3},{2,0},{3,1},{4,6},{5,7},{6,4},{7,5},{8,10},{9,11},{10,... | collective-permute-start | bytes 294920 | tf_op jit(solution)/shard_map/ppermute | solution.py:316
  93.4 3.3 %collective-permute-start.3 = (bf16[3,4096]{1,0:T(4,128)(2,1)}, bf16[3,4096]{1,0:T(4,128)(2,1)S(1)}, u32[]{:S(2)}, u32[]{:S(2)}) collective-permute-start(bf16[3,4096]{1,0:T(4,128)(2,1)} %get-tuple-element.31), channel_id=1, source_target_pairs={{1,0},{2,1},{3,2},{5,4},{6,5},{7,6},{9,8},{10,9},{11,10},{13,12},{... | collective-permute-start | bytes 73736 | tf_op jit(solution)/shard_map/ppermute | solution.py:473
  96.4 1.5 %collective-permute-start.10 = (f32[24,2048]{1,0:T(8,128)S(1)}, f32[24,2048]{1,0:T(8,128)S(1)}, u32[]{:S(2)}, u32[]{:S(2)}) collective-permute-start(f32[24,2048]{1,0:T(8,128)S(1)} %pad_maximum_fusion), channel_id=1, source_target_pairs={{0,1},{1,0},{2,3},{3,2},{4,5},{5,4},{6,7},{7,6},{8,9},{9,8},{10,11... | collective-permute-start | bytes 589832 | tf_op jit(solution)/shard_map/ppermute | solution.py:316
